TPU v7x, 512 devices: a whole 4x4x16 slice. The times are simulated.
512 devices in a mesh: branch: 4 (over x), tile: 128 (over z, y, core).
Axes of the slice: x: 4, y: 4, z: 16, core: 2. Of those that a mesh axis runs over, the one named last changes fastest.
Arguments:
- grad_first: bfloat16 [1024, 12288], P('tile', 'branch'), may hold values from -6 to 6
- grad_second: bfloat16 [512, 12288], P('tile', 'branch'), may hold values from -6 to 6
- grad_third: bfloat16 [256, 12288], P('tile', 'branch'), may hold values from -6 to 6
- grad_fourth: bfloat16 [128, 12288], P('tile', 'branch'), may hold values from -6 to 6
- pre_first: bfloat16 [1024, 12288], P('tile', 'branch'), may hold values from -6 to 6
- pre_second: bfloat16 [512, 12288], P('tile', 'branch'), may hold values from -6 to 6
- pre_third: bfloat16 [256, 12288], P('tile', 'branch'), may hold values from -6 to 6
- pre_fourth: bfloat16 [128, 12288], P('tile', 'branch'), may hold values from -6 to 6
- mid_twozero: bfloat16 [512, 6144], P('tile', 'branch'), may hold values from -6 to 6
- mid_threezero_one: bfloat16 [512, 6144], P('tile', 'branch'), may hold values from -6 to 6
- mid_threezero_two: bfloat16 [256, 3072], P('tile', 'branch'), may hold values from -6 to 6
- mid_threeone: bfloat16 [256, 6144], P('tile', 'branch'), may hold values from -6 to 6
- block_params: bfloat16 [1757952], P('tile'), may hold values from -1 to 1
Outputs:
- back_first: bfloat16 [1024, 12288], P('tile', 'branch')
- back_second: bfloat16 [512, 12288], P('tile', 'branch')
- back_third: bfloat16 [256, 12288], P('tile', 'branch')
- back_fourth: bfloat16 [128, 12288], P('tile', 'branch')
All inputs are finite; a program needn't handle non-finite values.
Results may differ from a plain program's by a relative error of at most 0.013.
Values may be sent and summed in bfloat16 or wider, within the bound.
A program may use at most 128 MiB of HBM per device.

v0:
```python
import math

import jax
import jax.numpy as jnp
from jax import lax
from jax.sharding import PartitionSpec as P

C = 48


def passed_along(value, axis, steps):
    count = lax.axis_size(axis)
    leading, last = (max(0, -steps), min(count, count - steps))
    return lax.ppermute(value, axis, [(source, source + steps) for source in range(leading, last)])


def weight_table(base):
    widths = [base, 2 * base, 4 * base, 8 * base]
    entries = []
    for target in range(4):
        for source in range(4):
            if target < source:
                entries.append(((target, source, 0), (widths[source], widths[target])))
            elif target > source:
                for section_no in range(target - source):
                    out_width = (
                        widths[target] if section_no == target - source - 1 else widths[source]
                    )
                    entries.append(
                        ((target, source, section_no), (3, 3, widths[source], out_width))
                    )
    return entries


def unpack(flat_params, base):
    unpacked = {}
    offset = 0
    for entry_key, entry_shape in weight_table(base):
        entry_size = math.prod(entry_shape)
        unpacked[entry_key] = flat_params[offset : offset + entry_size].reshape(entry_shape)
        offset += entry_size
    return unpacked


def pool_project(masked_map, factor, kernel):
    in_width = kernel.shape[1]
    out_width = kernel.shape[0]
    fine_rows = masked_map.shape[0]
    fine_cols = masked_map.shape[1] // in_width
    blocks = masked_map.reshape(fine_rows // factor, factor, fine_cols // factor, factor, in_width)
    pooled = jnp.sum(blocks, axis=(1, 3), dtype=jnp.float32).astype(jnp.bfloat16)
    product = jnp.dot(pooled.reshape(-1, in_width), kernel.T, preferred_element_type=jnp.float32)
    return product.reshape(fine_rows // factor, fine_cols // factor * out_width)


def spread(coarse_ext, kernel):
    in_width = kernel.shape[2]
    out_width = kernel.shape[3]
    rows_ext = coarse_ext.shape[0]
    cols_ext = coarse_ext.shape[1] // out_width
    tap_table = jnp.transpose(kernel, (3, 0, 1, 2)).reshape(out_width, 9 * in_width)
    tap_sums = jnp.dot(
        coarse_ext.reshape(rows_ext * cols_ext, out_width),
        tap_table,
        preferred_element_type=jnp.float32,
    )
    tap_sums = tap_sums.reshape(rows_ext, cols_ext, 3, 3, in_width)
    even_cols = tap_sums[:, :, :, 1]
    odd_cols = tap_sums[:, :-1, :, 2] + tap_sums[:, 1:, :, 0]
    columns = jnp.stack([even_cols[:, :-1], odd_cols], axis=2).reshape(
        rows_ext, 2 * cols_ext - 2, 3, in_width
    )
    columns = jnp.concatenate([columns, even_cols[:, -1:]], axis=1)
    even_rows = columns[:, :, 1]
    odd_rows = columns[:-1, :, 2] + columns[1:, :, 0]
    paired = jnp.stack([even_rows[:-1], odd_rows], axis=1).reshape(
        2 * rows_ext - 2, 2 * cols_ext - 1, in_width
    )
    joined = jnp.concatenate([paired, even_rows[-1:]], axis=0)
    return joined.reshape(2 * rows_ext - 1, (2 * cols_ext - 1) * in_width)


def trim_edge(extended_map, pixel_width):
    kept_rows = extended_map.shape[0] - 1
    shaped = extended_map[:-1].reshape(kept_rows, -1, pixel_width)
    return shaped[:, :-1].reshape(kept_rows, -1)


def per_device(
    grad_first,
    grad_second,
    grad_third,
    grad_fourth,
    pre_first,
    pre_second,
    pre_third,
    pre_fourth,
    mid_twozero,
    mid_threezero_one,
    mid_threezero_two,
    mid_threeone,
    block_params,
):
    gathered = lax.all_gather(block_params, "tile", axis=0, tiled=True)
    kernels = unpack(gathered, C)
    widths = [C, 2 * C, 4 * C, 8 * C]
    held = list(
        (
            lax.all_gather(grad_first, "branch", axis=1, tiled=True),
            lax.all_gather(grad_second, "branch", axis=1, tiled=True),
            lax.all_gather(grad_third, "branch", axis=1, tiled=True),
            lax.all_gather(grad_fourth, "branch", axis=1, tiled=True),
            lax.all_gather(pre_first, "branch", axis=1, tiled=True),
            lax.all_gather(pre_second, "branch", axis=1, tiled=True),
            lax.all_gather(pre_third, "branch", axis=1, tiled=True),
            lax.all_gather(pre_fourth, "branch", axis=1, tiled=True),
            lax.all_gather(mid_twozero, "branch", axis=1, tiled=True),
            lax.all_gather(mid_threezero_one, "branch", axis=1, tiled=True),
            lax.all_gather(mid_threezero_two, "branch", axis=1, tiled=True),
            lax.all_gather(mid_threeone, "branch", axis=1, tiled=True),
        )
    )
    cotangents = held[0:4]
    preacts = held[4:8]
    inner_maps = held[8:12]
    leading = cotangents[1:] + preacts[1:] + inner_maps
    pixel_widths = [2 * C, 4 * C, 8 * C, 2 * C, 4 * C, 8 * C, C, C, C, 2 * C]
    packed = jnp.concatenate([piece[:1] for piece in leading], axis=1)
    arrived = passed_along(packed, "tile", -1)
    row_ext = []
    offset = 0
    for piece in leading:
        row_width = piece.shape[1]
        row_ext.append(jnp.concatenate([piece, arrived[:, offset : offset + row_width]], axis=0))
        offset += row_width
    edges = [
        jnp.zeros((piece.shape[0], width), jnp.bfloat16)
        for piece, width in zip(row_ext, pixel_widths)
    ]
    extended = [jnp.concatenate([piece, edge], axis=1) for piece, edge in zip(row_ext, edges)]
    masked_ext = [None]
    for branch_no in range(1, 4):
        grad_ext = extended[branch_no - 1]
        masked_ext.append(
            jnp.where(extended[branch_no + 2] > 0, grad_ext, jnp.zeros_like(grad_ext))
        )
    masked_local = [jnp.where(preacts[0] > 0, cotangents[0], jnp.zeros_like(cotangents[0]))]
    masked_local = masked_local + [
        trim_edge(masked_ext[branch_no], widths[branch_no]) for branch_no in range(1, 4)
    ]
    inner = {(2, 0): [extended[6]], (3, 0): [extended[7], extended[8]], (3, 1): [extended[9]]}

    def pair_term(target, source):
        if target < source:
            return pool_project(
                masked_local[target], 2 ** (source - target), kernels[target, source, 0]
            )
        current = masked_ext[target]
        pulled = None
        for section_no in reversed(range(target - source)):
            pulled = spread(current, kernels[target, source, section_no])
            if section_no > 0:
                current = jnp.where(inner[target, source][section_no - 1] > 0, pulled, 0.0).astype(
                    jnp.bfloat16
                )
        return trim_edge(pulled, widths[source])

    def make_work(own_branch):

        def compute():
            totals = [
                jnp.zeros(masked_local[branch_no].shape, jnp.float32) for branch_no in range(4)
            ]
            totals[own_branch] = masked_local[own_branch].astype(jnp.float32)
            for source in range(4):
                if source != own_branch:
                    totals[source] = totals[source] + pair_term(own_branch, source)
            return tuple(totals)

        return compute

    partials = lax.switch(lax.axis_index("branch"), [make_work(group_no) for group_no in range(4)])
    summed = (
        lax.psum_scatter(partials[0], "branch", scatter_dimension=1, tiled=True),
        lax.psum_scatter(partials[1], "branch", scatter_dimension=1, tiled=True),
        lax.psum_scatter(partials[2], "branch", scatter_dimension=1, tiled=True),
        lax.psum_scatter(partials[3], "branch", scatter_dimension=1, tiled=True),
    )
    results = [piece.astype(jnp.bfloat16) for piece in summed]
    return (results[0], results[1], results[2], results[3])


def solution(mesh):
    in_specs = (
        P("tile", "branch"),
        P("tile", "branch"),
        P("tile", "branch"),
        P("tile", "branch"),
        P("tile", "branch"),
        P("tile", "branch"),
        P("tile", "branch"),
        P("tile", "branch"),
        P("tile", "branch"),
        P("tile", "branch"),
        P("tile", "branch"),
        P("tile", "branch"),
        P("tile"),
    )
    out_specs = (P("tile", "branch"), P("tile", "branch"), P("tile", "branch"), P("tile", "branch"))
    return jax.shard_map(
        per_device, mesh=mesh, in_specs=in_specs, out_specs=out_specs, check_vma=False
    )
```

profile of v0, /device:TPU:1, one launch (start us, length us, event | category | flops | bytes accessed | tf_op | source)
XLA Modules:
  0.0 784.0 jit_solution(10450582586779949644)
XLA Ops:
  7.2 10.4 %all_gather.43 = bf16[4,12288]{1,0:T(4,128)(2,1)S(1)} all-gather(bf16[4,3072]{1,0:T(4,128)(2,1)} %param.18), channel_id=1, replica_groups=mesh['branch'=4,'tile'=128] {'branch'}, dimensions={1}, use_global_device_ids=true | all-gather | bytes 122880 | tf_op jit(solution)/shard_map/all_gather | solution.py:110
  17.6 0.6 copy-done.3
  18.3 0.7 slice_dynamic-update-slice_fusion.3
  18.9 9.2 %all_gather.44 = bf16[2,12288]{1,0:T(2,128)(2,1)S(1)} all-gather(bf16[2,3072]{1,0:T(2,128)(2,1)} %param.19), channel_id=1, replica_groups=mesh['branch'=4,'tile'=128] {'branch'}, dimensions={1}, use_global_device_ids=true | all-gather | bytes 61440 | tf_op jit(solution)/shard_map/all_gather | solution.py:111
  28.2 9.4 %all_gather.45 = bf16[1,12288]{1,0:T(2,128)(2,1)S(1)} all-gather(bf16[1,3072]{1,0:T(2,128)(2,1)} %param.20), channel_id=1, replica_groups=mesh['branch'=4,'tile'=128] {'branch'}, dimensions={1}, use_global_device_ids=true | all-gather | bytes 30720 | tf_op jit(solution)/shard_map/all_gather | solution.py:112
  37.5 9.2 %all_gather.42 = bf16[4,12288]{1,0:T(4,128)(2,1)S(1)} all-gather(bf16[4,3072]{1,0:T(4,128)(2,1)} %param.22), channel_id=1, replica_groups=mesh['branch'=4,'tile'=128] {'branch'}, dimensions={1}, use_global_device_ids=true | all-gather | bytes 122880 | tf_op jit(solution)/shard_map/all_gather | solution.py:114
  46.8 9.3 %all_gather.46 = bf16[2,12288]{1,0:T(2,128)(2,1)S(1)} all-gather(bf16[2,3072]{1,0:T(2,128)(2,1)} %param.23), channel_id=1, replica_groups=mesh['branch'=4,'tile'=128] {'branch'}, dimensions={1}, use_global_device_ids=true | all-gather | bytes 61440 | tf_op jit(solution)/shard_map/all_gather | solution.py:115
  56.0 9.2 %all_gather.47 = bf16[1,12288]{1,0:T(2,128)(2,1)S(1)} all-gather(bf16[1,3072]{1,0:T(2,128)(2,1)} %param.24), channel_id=1, replica_groups=mesh['branch'=4,'tile'=128] {'branch'}, dimensions={1}, use_global_device_ids=true | all-gather | bytes 30720 | tf_op jit(solution)/shard_map/all_gather | solution.py:116
  65.3 9.5 %all_gather.48 = bf16[4,6144]{1,0:T(4,128)(2,1)S(1)} all-gather(bf16[4,1536]{1,0:T(4,128)(2,1)} %param.25), channel_id=1, replica_groups=mesh['branch'=4,'tile'=128] {'branch'}, dimensions={1}, use_global_device_ids=true | all-gather | bytes 61440 | tf_op jit(solution)/shard_map/all_gather | solution.py:117
  74.8 9.2 %all_gather.49 = bf16[4,6144]{1,0:T(4,128)(2,1)S(1)} all-gather(bf16[4,1536]{1,0:T(4,128)(2,1)} %param.26), channel_id=1, replica_groups=mesh['branch'=4,'tile'=128] {'branch'}, dimensions={1}, use_global_device_ids=true | all-gather | bytes 61440 | tf_op jit(solution)/shard_map/all_gather | solution.py:118
  84.0 9.1 %all_gather.50 = bf16[2,3072]{1,0:T(2,128)(2,1)S(1)} all-gather(bf16[2,768]{1,0:T(2,128)(2,1)} %param.27), channel_id=1, replica_groups=mesh['branch'=4,'tile'=128] {'branch'}, dimensions={1}, use_global_device_ids=true | all-gather | bytes 15360 | tf_op jit(solution)/shard_map/all_gather | solution.py:119
  93.1 9.2 %all_gather.51 = bf16[2,6144]{1,0:T(2,128)(2,1)S(1)} all-gather(bf16[2,1536]{1,0:T(2,128)(2,1)} %param.28), channel_id=1, replica_groups=mesh['branch'=4,'tile'=128] {'branch'}, dimensions={1}, use_global_device_ids=true | all-gather | bytes 30720 | tf_op jit(solution)/shard_map/all_gather | solution.py:120
  102.3 0.7 slice_dynamic-update-slice_fusion.2
  103.0 0.7 constant_dynamic-update-slice_fusion.2
  103.6 0.6 slice_dynamic-update-slice_fusion.1
  104.3 0.6 slice_dynamic-update-slice_fusion
  104.9 0.7 constant_dynamic-update-slice_fusion.1
  105.6 0.6 slice_dynamic-update-slice_fusion.6
  106.2 0.6 slice_dynamic-update-slice_fusion.5
  106.9 0.6 constant_dynamic-update-slice_fusion
  107.5 0.6 slice_dynamic-update-slice_fusion.4
  108.1 36.1 %collective-permute-start = (bf16[1,95232]{1,0:T(2,128)(2,1)}, bf16[1,95232]{1,0:T(2,128)(2,1)}, u32[]{:S(2)}, u32[]{:S(2)}) collective-permute-start(bf16[1,95232]{1,0:T(2,128)(2,1)} %slice_dynamic-update-slice_fusion.4), channel_id=1, source_target_pairs={{1,0},{2,1},{3,2},{4,3},{5,4},{6,5},{7,6},{8,7},{9,8},{10,9},{11,1... | collective-permute-start | bytes 571400 | tf_op jit(solution)/shard_map/ppermute | solution.py:14
  144.2 1.3 dynamic-slice
  146.1 0.3 broadcast.61
  146.4 1.1 dynamic-update-slice
  147.5 1.8 copy-done
  149.4 10.0 %all_gather.39 = bf16[8,12288]{1,0:T(8,128)(2,1)S(1)} all-gather(bf16[8,3072]{1,0:T(8,128)(2,1)} %param.21), channel_id=1, replica_groups=mesh['branch'=4,'tile'=128] {'branch'}, dimensions={1}, use_global_device_ids=true | all-gather | bytes 245760 | tf_op jit(solution)/shard_map/all_gather | solution.py:113
  159.4 9.4 %all_gather.40 = bf16[8,12288]{1,0:T(8,128)(2,1)S(1)} all-gather(bf16[8,3072]{1,0:T(8,128)(2,1)} %param.17), channel_id=1, replica_groups=mesh['branch'=4,'tile'=128] {'branch'}, dimensions={1}, use_global_device_ids=true | all-gather | bytes 245760 | tf_op jit(solution)/shard_map/all_gather | solution.py:109
  168.8 0.9 fusion.60
  169.7 1.6 pad_maximum_fusion.32
  171.3 1.2 fusion.61
  172.5 1.7 pad_maximum_fusion.33
  174.2 0.9 pad_maximum_fusion.36
  175.1 0.7 pad_maximum_fusion.38
  175.7 0.7 slice.843
  176.5 0.6 pad_maximum_fusion.39
  177.1 0.2 pad_maximum_fusion.30
  177.3 324.4 %all-reduce.13.cloned.1.call-done = bf16[1757952]{0:T(1024)(128)(2,1)} async-done(((bf16[1757952]{0:T(1024)(128)(2,1)}), bf16[1757952]{0:T(1024)(128)(2,1)}) %all-reduce.13.cloned.1.call-update) | async-done | bytes 3515920
  501.7 7.5 conditional.1
  501.7 0.2 fusion.58
  501.9 0.5 reshape.1001
  502.5 1.2 reduce_sum.81
  503.6 0.7 slice.619
  504.4 0.2 fusion.63
  504.6 0.2 reshape.1004
  504.9 0.5 reshape.1005
  505.4 0.5 reduce_sum.82
  505.9 0.7 slice.620
  506.7 0.2 fusion.64
  506.9 0.8 reshape.1008
  507.9 0.8 slice.621
  508.8 0.1 convolution_bitcast_fusion
  509.3 4.0 copy.363
  513.3 4.7 copy.361
  518.1 4.0 copy.359
  522.2 0.5 reduce-scatter.11.cloned.1.call-update
  522.7 75.9 %reduce-scatter.17.cloned.1.call-done = f32[3072,1]{1,0:T(8,128)} async-done(((f32[12288,1]{1,0:T(8,128)}), f32[3072,1]{1,0:T(8,128)}) %reduce-scatter.17.cloned.1.call-update) | async-done | bytes 12304
  598.6 2.5 copy.364
  601.1 71.8 %reduce-scatter.15.cloned.1.call-done = f32[3072,2]{1,0:T(8,128)} async-done(((f32[12288,2]{1,0:T(8,128)}), f32[3072,2]{1,0:T(8,128)}) %reduce-scatter.15.cloned.1.call-update) | async-done | bytes 24592
  672.9 2.5 copy.362
  675.4 71.7 %reduce-scatter.13.cloned.1.call-done = f32[3072,4]{1,0:T(8,128)} async-done(((f32[12288,4]{1,0:T(8,128)}), f32[3072,4]{1,0:T(8,128)}) %reduce-scatter.13.cloned.1.call-update) | async-done | bytes 49168
  747.1 2.5 copy.360
  749.6 26.4 %reduce-scatter.11.cloned.1.call-done = f32[8,3072]{1,0:T(8,128)} async-done(((f32[8,12288]{1,0:T(8,128)}), f32[8,3072]{1,0:T(8,128)}) %reduce-scatter.11.cloned.1.call-update) | async-done | bytes 98320 | tf_op jit(solution)/shard_map/reduce_scatter | solution.py:184
  776.0 1.5 convert_element_type.78
  (43 shorter events, 0.9 us)
Async XLA Ops:
  7.2 494.6 %all-reduce.13.cloned.1.call-start = ((), (), s32[]{:S(2)}) async-start(), calls=%async_computation.5 | async-start | bytes 7032832
  17.6 0.6 copy-start.3
  28.2 77.4 %copy-start.11 = (bf16[2,12288]{1,0:T(2,128)(2,1)}, bf16[2,12288]{1,0:T(2,128)(2,1)S(1)}, u32[]{:S(2)}) copy-start(bf16[2,12288]{1,0:T(2,128)(2,1)S(1)} %all_gather.44) | copy-start | bytes 147460
  37.5 66.8 %copy-start.7 = (bf16[1,12288]{1,0:T(2,128)(2,1)}, bf16[1,12288]{1,0:T(2,128)(2,1)S(1)}, u32[]{:S(2)}) copy-start(bf16[1,12288]{1,0:T(2,128)(2,1)S(1)} %all_gather.45) | copy-start | bytes 73732
  46.8 56.9 %copy-start.5 = (bf16[4,12288]{1,0:T(4,128)(2,1)}, bf16[4,12288]{1,0:T(4,128)(2,1)S(1)}, u32[]{:S(2)}) copy-start(bf16[4,12288]{1,0:T(4,128)(2,1)S(1)} %all_gather.42) | copy-start | bytes 294916
  56.0 50.2 %copy-start.12 = (bf16[2,12288]{1,0:T(2,128)(2,1)}, bf16[2,12288]{1,0:T(2,128)(2,1)S(1)}, u32[]{:S(2)}) copy-start(bf16[2,12288]{1,0:T(2,128)(2,1)S(1)} %all_gather.46) | copy-start | bytes 147460
  65.3 39.7 %copy-start.9 = (bf16[1,12288]{1,0:T(2,128)(2,1)}, bf16[1,12288]{1,0:T(2,128)(2,1)S(1)}, u32[]{:S(2)}) copy-start(bf16[1,12288]{1,0:T(2,128)(2,1)S(1)} %all_gather.47) | copy-start | bytes 73732
  74.8 32.1 %copy-start.15 = (bf16[4,6144]{1,0:T(4,128)(2,1)}, bf16[4,6144]{1,0:T(4,128)(2,1)S(1)}, u32[]{:S(2)}) copy-start(bf16[4,6144]{1,0:T(4,128)(2,1)S(1)} %all_gather.48) | copy-start | bytes 147460
  84.0 23.5 %copy-start.16 = (bf16[4,6144]{1,0:T(4,128)(2,1)}, bf16[4,6144]{1,0:T(4,128)(2,1)S(1)}, u32[]{:S(2)}) copy-start(bf16[4,6144]{1,0:T(4,128)(2,1)S(1)} %all_gather.49) | copy-start | bytes 147460
  108.1 60.7 %collective-permute-start = (bf16[1,95232]{1,0:T(2,128)(2,1)}, bf16[1,95232]{1,0:T(2,128)(2,1)}, u32[]{:S(2)}, u32[]{:S(2)}) collective-permute-start(bf16[1,95232]{1,0:T(2,128)(2,1)} %slice_dynamic-update-slice_fusion.4), channel_id=1, source_target_pairs={{1,0},{2,1},{3,2},{4,3},{5,4},{6,5},{7,6},{8,7},{9,8},{10,9},{11,1... | collective-permute-start | bytes 571400 | tf_op jit(solution)/shard_map/ppermute | solution.py:14
  147.5 1.8 copy-start
  149.3 24.9 %copy-start.8 = (bf16[1,12288]{1,0:T(2,128)(2,1)S(1)}, bf16[1,12288]{1,0:T(2,128)(2,1)}, u32[]{:S(2)}) copy-start(bf16[1,12288]{1,0:T(2,128)(2,1)} %copy-done.7) | copy-start | bytes 73732
  149.3 24.9 %copy-start.10 = (bf16[1,12288]{1,0:T(2,128)(2,1)S(1)}, bf16[1,12288]{1,0:T(2,128)(2,1)}, u32[]{:S(2)}) copy-start(bf16[1,12288]{1,0:T(2,128)(2,1)} %copy-done.9) | copy-start | bytes 73732
  149.3 27.8 %copy-start.4 = (bf16[4,12288]{1,0:T(4,128)(2,1)S(1)}, bf16[4,12288]{1,0:T(4,128)(2,1)}, u32[]{:S(2)}) copy-start(bf16[4,12288]{1,0:T(4,128)(2,1)} %copy-done.3) | copy-start | bytes 294916
  149.3 27.8 %copy-start.6 = (bf16[4,12288]{1,0:T(4,128)(2,1)S(1)}, bf16[4,12288]{1,0:T(4,128)(2,1)}, u32[]{:S(2)}) copy-start(bf16[4,12288]{1,0:T(4,128)(2,1)} %copy-done.5) | copy-start | bytes 294916
  149.3 449.3 %reduce-scatter.17.cloned.1.call-start = ((), (), s32[]{:S(2)}) async-start(), calls=%async_computation.8 | async-start | bytes 7864320
  509.2 4.0 copy-start.1
  513.3 159.7 %reduce-scatter.15.cloned.1.call-start = ((), (), s32[]{:S(2)}) async-start(), calls=%async_computation.7 | async-start | bytes 7864320
  518.1 229.0 %reduce-scatter.13.cloned.1.call-start = ((), (), s32[]{:S(2)}) async-start(), calls=%async_computation.6 | async-start | bytes 7864320
  522.1 253.9 %reduce-scatter.11.cloned.1.call-start = ((), (), s32[]{:S(2)}) async-start(), calls=%async_computation.4 | async-start | bytes 491520 | tf_op jit(solution)/shard_map/reduce_scatter | solution.py:184
Sparse Core Ops, SparseCore 0:
  149.4 352.2 all-reduce.12
  513.4 85.1 reduce-scatter.16
  601.5 71.4 reduce-scatter.14
  675.6 71.3 reduce-scatter.12
  749.8 26.1 reduce-scatter.10
where the time goes:
time: 786 us; the launch traced here: 784 us
  waiting for transfers between devices  571 us (73%)
  blocking collectives  113 us (14%)
  local copies, waits for them, and re-layouts  39.3 us (5%)
  starting transfers between devices  36.3 us (5%)
  between operations  14.6 us (2%)
  other arithmetic  9.08 us (1%)
    unnamed x9, waiting for transfers between devices  544 us
    ppermute x1, starting transfers between devices, passed_along(): lax.ppermute(value, axis, [(source, source + steps) for source in range(l...  36.1 us
    unnamed x46, local copies, waits for them, and re-layouts  31.1 us
    reduce_scatter x1, waiting for transfers between devices, per_device(): lax.psum_scatter(partials[0], 'branch', scatter_dimension=1, tiled=True)  26.4 us
  transfers between devices with their start and end apart: 6, of which 5 were waited for; matrix products, arithmetic and copies ran while one was open for 3% of the time, Pallas kernels for 0%

commit v1 on v0

v1 whole, which is shorter than its diff:
```python
import jax
import jax.numpy as jnp
from jax import lax
from jax.experimental import pallas as pl
from jax.experimental.pallas import tpu as pltpu
from jax.sharding import PartitionSpec as P

BF = jnp.bfloat16
F32 = jnp.float32
MESH = pl.DeviceIdType.MESH
N_TILE = 128
N_BRANCH = 4
NZ = 16
SHARD = 13734
CELL = 384
RAW_ROWS = 112
BASE = 104
WINDOW = 464

ROW0 = {
    (0, 1, 0): 0,
    (0, 2, 0): 12,
    (0, 3, 0): 36,
    (1, 0, 0): 84,
    (1, 2, 0): 192,
    (1, 3, 0): 240,
    (2, 0, 0): 336,
    (2, 0, 1): 390,
    (2, 1, 0): 606,
    (2, 3, 0): 1038,
    (3, 0, 0): 1230,
    (3, 0, 1): 1284,
    (3, 0, 2): 1338,
    (3, 1, 0): 1770,
    (3, 1, 1): 1986,
    (3, 2, 0): 2850,
}


def remote(src, dst, send, recv, branch, tile):
    return pltpu.make_async_remote_copy(
        src_ref=src, dst_ref=dst, send_sem=send, recv_sem=recv, device_id=(branch, tile), device_id_type=MESH
    )


def gather_kernel(
    raw, g2, g3, g4, p2, p3, p4, m20, m30a, m30b, m31,
    tiles, row_in, col_in, corner_in,
    raw1, raw2, win, row_f, col_f, row_out, col_out,
    h_send, h_recv, z_send, z_recv, s_send, s_recv,
):
    b = lax.axis_index("branch")
    k = lax.axis_index("tile")
    z, y, c = k // 8, lax.rem(k // 2, 4), lax.rem(k, 2)

    def tile_of(zz, yy, cc):
        return zz * 8 + yy * 2 + cc

    def wrap(value, count):
        return lax.rem(value + count, count)

    row_f[...] = jnp.zeros_like(row_f)
    col_f[...] = jnp.zeros_like(col_f)
    at_row, at_col = 0, 0
    for g, p in ((g2, p2), (g3, p3), (g4, p4)):
        rows = g.shape[0]
        masked = jnp.where(p[...].astype(F32) > 0, g[...].astype(F32), 0.0)
        for cell in range(8):
            row_f[at_row + cell : at_row + cell + 1, :] = masked[0:1, CELL * cell : CELL * (cell + 1)]
        col_f[at_col : at_col + rows, :] = masked[:, 0:CELL]
        at_row, at_col = at_row + 8, at_col + rows
    for m, at_row, at_col in ((m20, 24, 8), (m30a, 28, 12), (m31, 32, 18), (m30b, 36, 16)):
        rows, units = m.shape[0], m.shape[1] // CELL
        value = m[...].astype(F32)
        for unit in range(units):
            row_f[at_row + unit : at_row + unit + 1, :] = value[0:1, CELL * unit : CELL * (unit + 1)]
        col_f[at_col : at_col + rows, :] = value[:, 0:CELL]
    row_out[...] = row_f[...].astype(BF)
    col_out[...] = col_f[...].astype(BF)

    left, right = wrap(b - 1, N_BRANCH), wrap(b + 1, N_BRANCH)
    up1, up2 = wrap(k - 1, N_TILE), wrap(k - 2, N_TILE)
    down1, down2 = wrap(k + 1, N_TILE), wrap(k + 2, N_TILE)
    y_prev, y_next = wrap(y - 1, 4), wrap(y + 1, 4)

    partners = [
        (b, up1), (b, up2), (b, down1), (b, down2), (left, k), (right, k), (left, up1), (right, down1),
        (b, tile_of(z, y_prev, c)), (b, tile_of(z, y_next, c)), (b, tile_of(z, y, 1 - c)),
    ]
    barrier = pltpu.get_barrier_semaphore()
    for who in partners:
        pl.semaphore_signal(barrier, inc=1, device_id=who, device_id_type=MESH)
    for step in range(1, NZ):
        pl.semaphore_signal(
            barrier, inc=1, device_id=(b, tile_of(wrap(z + step, NZ), y, c)), device_id_type=MESH
        )
    pl.semaphore_wait(barrier, len(partners) + NZ - 1)

    first = [
        remote(raw, raw1, h_send.at[0], h_recv.at[0], b, up1),
        remote(raw, raw2, h_send.at[1], h_recv.at[1], b, up2),
        remote(row_out, row_in, h_send.at[2], h_recv.at[2], b, up1),
        remote(col_out, col_in, h_send.at[3], h_recv.at[3], left, k),
        remote(col_out, corner_in, h_send.at[4], h_recv.at[4], left, up1),
    ]
    for copy in first:
        copy.start()

    group, j = k // 4, lax.rem(k, 4)
    first_tile = (7 * j) // 3
    delta = 13734 * j - 6144 * first_tile - 360 * group + BASE * 128
    win[...] = jnp.zeros_like(win)
    lane = lax.broadcasted_iota(jnp.int32, (RAW_ROWS, 128), 1)
    for d, shard in enumerate((raw, raw1, raw2)):
        if d > 0:
            first[d - 1].wait_recv()
        start = delta + SHARD * d
        q, phase = start // 128, lax.rem(start, 128)
        rolled = pltpu.roll(shard[...].astype(F32), phase, 1)
        win[pl.ds(q, RAW_ROWS), :] += jnp.where(lane >= phase, rolled, 0.0)
        win[pl.ds(q + 1, RAW_ROWS), :] += jnp.where(lane >= phase, 0.0, rolled)
    for s in range(2):
        n = 7 * j + 2 * b + s
        row_tile = 9 * group + n // 3
        offset = jnp.where(row_tile >= 124, 2, 10)
        origin = BASE + 3 * (16 * (n // 3 - first_tile) + offset) + lax.rem(n, 3)
        tiles[s, b, y, c, z] = win[pl.ds(origin, 16, stride=3), :].astype(BF)

    copies = []
    own = tiles.at[:, b, y, c, z]
    for step in range(1, NZ):
        copy = remote(
            own, own, z_send.at[step - 1], z_recv.at[step - 1], b, tile_of(wrap(z + step, NZ), y, c)
        )
        copy.start()
        copies.append(copy)
    for copy in copies:
        copy.wait_recv()

    pending = []

    class Half:
        def __init__(self, s):
            self.s = s
            self.u, self.v = (b, y) if s == 0 else (y, b)
            self.used = 36 * s

        def bundle(self, u, v, part):
            x_at, y_at = (u, v) if self.s == 0 else (v, u)
            ref = tiles.at[self.s, x_at, y_at, c]
            return ref if part is None else ref.at[pl.ds(8 * part, 8)]

        def send(self, u, v, part, to_u, to_v, other_core=False):
            x_to, y_to = (to_u, to_v) if self.s == 0 else (to_v, to_u)
            ref = self.bundle(u, v, part)
            copy = remote(
                ref, ref, s_send.at[self.used], s_recv.at[self.used], x_to,
                tile_of(z, y_to, 1 - c if other_core else c),
            )
            copy.start()
            self.used += 1
            pending.append(copy)
            return copy

        def first(self):
            u, v = self.u, self.v
            self.to_next = self.send(u, v, None, wrap(u + 1, 4), v)
            self.to_prev = self.send(u, v, None, wrap(u - 1, 4), v)
            self.second = [self.spread(u)]

        def spread(self, u_of):
            u, v = self.u, self.v
            to_next = self.send(u_of, v, None, u, wrap(v + 1, 4))
            to_prev = self.send(u_of, v, None, u, wrap(v - 1, 4))
            self.send(u_of, v, None, u, v, True)
            return u_of, to_next, to_prev

        def forward(self):
            u, v = self.u, self.v
            self.to_next.wait_recv()
            prev_u, next_u = wrap(u - 1, 4), wrap(u + 1, 4)
            self.far_next = self.send(prev_u, v, 0, next_u, v)
            self.second.append(self.spread(prev_u))
            self.to_prev.wait_recv()
            self.far_prev = self.send(next_u, v, 1, prev_u, v)
            self.second.append(self.spread(next_u))

        def far(self):
            self.far_next.wait_recv()
            self.far_prev.wait_recv()
            self.second.append(self.spread(wrap(self.u + 2, 4)))

        def finish(self, number):
            u, v = self.u, self.v
            u_of, to_next, to_prev = self.second[number]
            to_next.wait_recv()
            a = self.send(u_of, wrap(v - 1, 4), 0, u, wrap(v + 1, 4))
            self.send(u_of, wrap(v - 1, 4), None, u, v, True)
            to_prev.wait_recv()
            d = self.send(u_of, wrap(v + 1, 4), 1, u, wrap(v - 1, 4))
            self.send(u_of, wrap(v + 1, 4), None, u, v, True)
            return u_of, a, d

        def last(self, state):
            u_of, a, d = state
            a.wait_recv()
            d.wait_recv()
            self.send(u_of, wrap(self.v + 2, 4), None, self.u, self.v, True)

    halves = [Half(0), Half(1)]
    for half in halves:
        half.first()
    for half in halves:
        half.forward()
    for half in halves:
        half.far()
    states = []
    for number in range(4):
        for half in halves:
            states.append((half, half.finish(number)))
    for half, state in states:
        half.last(state)
    waited = set()
    for half in halves:
        waited.update([id(half.to_next), id(half.to_prev), id(half.far_next), id(half.far_prev)])
        for _, to_next, to_prev in half.second:
            waited.update([id(to_next), id(to_prev)])
    for _, (_, a, d) in states:
        waited.update([id(a), id(d)])
    for copy in pending:
        if id(copy) not in waited:
            copy.wait_recv()
    for copy in pending + copies + first:
        copy.wait_send()
    for copy in first[2:]:
        copy.wait_recv()


def tile_at(row_tile, jb):
    group, n = row_tile // 9, 3 * (row_tile % 9) + jb
    j, slot = n // 7, n % 7
    k = 4 * group + j
    return slot % 2, slot // 2, (k // 2) % 4, k % 2, k // 8


def dot(a, b):
    return lax.dot_general(a, b, (((1,), (0,)), ((), ())), preferred_element_type=F32)


def dot_nt(a, b):
    return lax.dot_general(a, b, (((1,), (1,)), ((), ())), preferred_element_type=F32)


def unit_matrix(rows, cols, target):
    column = lax.broadcasted_iota(jnp.int32, (1, cols), 1)
    row = lax.broadcasted_iota(jnp.int32, (rows, cols), 0)
    return jnp.where(row == target(column), 1.0, 0.0).astype(BF)


def compute_kernel(
    tiles, row_in, col_in, corner_in,
    g1, g2, g3, g4, p1, p2, p3, p4, m20, m30a, m30b, m31,
    o1, o2, o3, o4,
    e3, e2, e1, u3, u2, u1,
    wide, c0, c1, c2, c3, sg1, sg2, q20, q30a, q30b, q31, k1, k2a, k2b, nxt, out,
):
    b = lax.axis_index("branch")
    k = lax.axis_index("tile")
    has_row = k < N_TILE - 1
    has_col = b < N_BRANCH - 1

    def load_rows(row_tile, count):
        columns = [
            jnp.concatenate([tiles[tile_at(row_tile + t, jb)] for t in range(count)], axis=0) for jb in range(3)
        ]
        return jnp.concatenate(columns, axis=1)

    def rows_of(key, rows, j, at=0):
        n = CELL // j
        r0 = ROW0[key]
        row_tile, offset = (286, 0) if r0 == 0 else divmod(r0 - 10, 16)
        count = -(-(offset + rows) // 16)
        width = 256 if j == 192 else 128

        def target(col):
            part, lane = col // width, lax.rem(col, width) - at
            return jnp.where((lane >= 0) & (lane < j), part * j + lane, -1)

        split = dot(load_rows(row_tile, count), unit_matrix(CELL, n * width, target))
        parts = []
        for half in range(width // 128):
            for part in range(n):
                wide[half, pl.ds(part, 16 * count, stride=n), :] = split[
                    :, part * width + 128 * half : part * width + 128 * (half + 1)
                ]
            parts.append(wide[half, offset * n : (offset + rows) * n, :])
        return parts[0] if len(parts) == 1 else jnp.concatenate(parts, axis=1)

    def place(weights, j, low, high):
        rows = weights.shape[1]

        def target(col):
            which = col // j
            return jnp.where((which >= low) & (which < high), lax.rem(col, j), -1)

        return dot(weights, unit_matrix(rows, CELL, target))

    def taps(e, row0, pitch, weights, placed, seg, nxt_seg, nxt_width):
        count = len(placed)
        i = weights.shape[0] // 9

        def tap(value, a, bb):
            return value[(3 * a + bb) * i : (3 * a + bb + 1) * i]

        for a in range(3):
            for q in range(count):
                even = row0 + CELL * a + 2 * q * pitch
                e[even : even + i, seg : seg + CELL] = tap(placed[q], a, 1).astype(BF)
                odd = even + pitch
                value = tap(placed[q], a, 2)
                if q + 1 < count:
                    value = value + tap(placed[q + 1], a, 0)
                else:
                    e[odd : odd + i, nxt_seg : nxt_seg + nxt_width] = tap(weights, a, 0).astype(BF)
                e[odd : odd + i, seg : seg + CELL] = value.astype(BF)

    e3[...] = jnp.zeros_like(e3)
    e2[...] = jnp.zeros_like(e2)
    e1[...] = jnp.zeros_like(e1)

    for key, i, row0, pitch in (
        ((3, 2, 0), 192, 0, 192),
        ((3, 1, 1), 96, 1152, 96),
        ((3, 0, 2), 48, 1152 + 192, 48),
    ):
        r0 = ROW0[key]
        start = 124 + (r0 - 1986) // 16 if r0 >= 1986 else (r0 - 10) // 16
        for a in range(3):
            even = row0 + CELL * a
            odd = even + pitch
            for bb, at, seg in ((1, even, 0), (2, odd, 0), (0, odd, CELL)):
                first = start + (3 * a + bb) * (i // 16)
                for t in range(i // 16):
                    for jb in range(3):
                        e3[at + 16 * t : at + 16 * (t + 1), seg + 128 * jb : seg + 128 * (jb + 1)] = tiles[
                            tile_at(first + t, jb)
                        ]

    w = rows_of((2, 1, 0), 432, 192)
    taps(e2, 0, 96, w, [place(w.astype(BF), 192, q, q + 1) for q in range(2)], 0, 768, 256)
    w = rows_of((3, 1, 0), 216, 96)
    taps(e2, 0, 96, w, [place(w.astype(BF), 96, q, q + 1) for q in range(2)], 384, 1024, 128)
    w = rows_of((2, 0, 1), 216, 192)
    placed = [place(w.astype(BF), 192, q, q + 1) for q in range(2)]
    taps(e2, 1152, 96, w, placed, 0, 768, 256)
    w = rows_of((3, 0, 1), 54, 48)
    w_next = rows_of((3, 0, 1), 54, 48, 64)
    placed = [place(w.astype(BF), 48, 4 + q, 5 + q) for q in range(2)]
    taps(e2, 1152 + 48, 96, w_next, placed, 384, 1024 + 128, 128)

    w = rows_of((1, 0, 0), 108, 96)
    taps(e1, 0, 48, w, [place(w.astype(BF), 96, q, q + 1) for q in range(4)], 0, 768, 128)
    w = rows_of((2, 0, 0), 54, 48) + 0.0
    w = w + rows_of((3, 0, 0), 54, 48, 48)
    taps(e1, 0, 48, w, [place(w.astype(BF), 96, q, q + 1) for q in range(4)], 384, 896, 128)

    u3[:, 0:384] = place(rows_of((0, 3, 0), 48, 48).astype(BF), 48, 0, 8).astype(BF)
    u3[:, 384:768] = place(rows_of((1, 3, 0), 96, 96).astype(BF), 96, 0, 4).astype(BF)
    u3[:, 768:1152] = place(rows_of((2, 3, 0), 192, 192).astype(BF), 192, 0, 2).astype(BF)
    w02 = rows_of((0, 2, 0), 24, 48).astype(BF)
    w12 = rows_of((1, 2, 0), 48, 96).astype(BF)
    for q in range(2):
        u2[192 * q : 192 * (q + 1), 0:384] = place(w02, 48, 4 * q, 4 * q + 4).astype(BF)
        u2[192 * q : 192 * (q + 1), 384:768] = place(w12, 96, 2 * q, 2 * q + 2).astype(BF)
    w01 = rows_of((0, 1, 0), 12, 48).astype(BF)
    for q in range(4):
        u1[96 * q : 96 * (q + 1), :] = place(w01, 48, 2 * q, 2 * q + 2).astype(BF)

    def put(buffer, row, value):
        rows = value.shape[0]
        for l in range(3):
            buffer[l, row : row + rows, :] = value[:, 128 * l : 128 * (l + 1)]

    def spread_units(buffer, value, units):
        rows = value.shape[0]
        for unit in range(units):
            for l in range(3):
                piece = value[:, CELL * unit + 128 * l : CELL * unit + 128 * (l + 1)]
                if rows == 1:
                    buffer[l, unit : unit + 1, :] = piece
                else:
                    buffer[l, pl.ds(unit, rows, stride=units), :] = piece

    def masked(g, p):
        return jnp.where(p[...].astype(F32) > 0, g[...].astype(F32), 0.0)

    row_halo = row_in[...].astype(F32)
    col_halo = col_in[...].astype(F32)
    corner = corner_in[...].astype(F32)
    row_zero = jnp.where(has_row, row_halo, 0.0)
    col_zero = jnp.where(has_col, col_halo, 0.0)
    corner_zero = jnp.where(has_row & has_col, corner, 0.0)

    for buffer in (c1, c2, c3, sg1, sg2, q20, q30a, q30b, q31, k1, k2a, k2b, nxt):
        buffer[...] = jnp.zeros_like(buffer)
    spread_units(c0, masked(g1, p1), 8)
    at = 0
    for buffer, g, p, rows, halo in ((c1, g2, p2, 4, 0), (c2, g3, p3, 2, 8), (c3, g4, p4, 1, 16)):
        spread_units(buffer, masked(g, p), 8)
        put(buffer, 8 * rows, row_zero[halo : halo + 8])
        put(buffer, 8 * rows + 8, col_zero[at : at + rows])
        put(buffer, 8 * rows + 8 + rows, corner_zero[at : at + 1])
        at += rows

    for buffer, m, rows, units, halo, at in (
        (q20, m20, 4, 4, 24, 8), (q30a, m30a, 4, 4, 28, 12), (q31, m31, 2, 4, 32, 18), (q30b, m30b, 2, 2, 36, 16),
    ):
        spread_units(buffer, m[...].astype(F32), units)
        put(buffer, rows * units, row_halo[halo : halo + units])
        put(buffer, (rows + 1) * units, col_halo[at : at + rows])
        put(buffer, (rows + 1) * units + rows, corner[at : at + 1])

    def flags(buffer):
        whole = jnp.concatenate([buffer[l] for l in range(3)], axis=1)
        return jnp.where(whole > 0, 1.0, 0.0).astype(BF)

    def target20(shift):
        def target(col):
            part, lane = col // CELL, lax.rem(col, CELL)
            pixel, channel = lane // 96, lax.rem(lane, 96) - shift
            return jnp.where((channel >= 0) & (channel < 48), part * 192 + pixel * 48 + channel, -1)

        return target

    def target31(col):
        part, lane = col // CELL, lax.rem(col, CELL)
        return jnp.where(lane < 192, part * 192 + lane, -1)

    def target30b(col):
        part, lane = col // CELL, lax.rem(col, CELL) - 192
        return jnp.where((lane >= 0) & (lane < 96), part * 96 + lane, -1)

    def keep(buffer, value, parts, count, extra_from, extra_rows, extra_to):
        for l in range(3):
            for part in range(parts):
                lanes = slice(part * CELL + 128 * l, part * CELL + 128 * (l + 1))
                buffer[l, pl.ds(part, count, stride=parts), :] = value[0:count, lanes]
            buffer[l, extra_to : extra_to + extra_rows, :] = value[
                extra_from : extra_from + extra_rows, 128 * l : 128 * (l + 1)
            ]

    mask1 = dot(flags(q20), unit_matrix(CELL, 768, target20(0))) + dot(
        flags(q30a), unit_matrix(CELL, 768, target20(48))
    )
    keep(k1, mask1, 2, 20, 20, 5, 40)
    keep(k2a, dot(flags(q31), unit_matrix(CELL, 768, target31)), 2, 12, 12, 3, 24)
    keep(k2b, dot(flags(q30b), unit_matrix(CELL, 1536, target30b)), 4, 6, 6, 3, 24)

    def lanes_of(buffer, count=3):
        return [buffer[l] for l in range(count)]

    def shifted(buffer, rows, count):
        total = buffer.shape[1]
        pieces = []
        for l in range(count):
            nxt[l, 0 : 8 * rows, :] = buffer[l, 1 : 8 * rows + 1, :]
            for p in range(rows):
                nxt[l, 8 * p + 7 : 8 * p + 8, :] = buffer[l, 8 * rows + p : 8 * rows + p + 1, :]
            nxt[l, 8 * rows : total, :] = jnp.zeros((total - 8 * rows, 128), F32)
            pieces.append(nxt[l, 0:total, :])
        return pieces

    def lhs(pieces):
        return jnp.concatenate([piece.astype(BF) for piece in pieces], axis=1)

    def rows_out(y, a, lo, hi, lane0):
        return y[lo:hi, lane0 + CELL * a : lane0 + CELL * (a + 1)]

    def upsampled(y, p, lane0):
        even = rows_out(y, 1, 8 * p, 8 * p + 8, lane0)
        odd = rows_out(y, 2, 8 * p, 8 * p + 8, lane0) + rows_out(y, 0, 8 * p + 8, 8 * p + 16, lane0)
        return even, odd

    def section(buffer, y, rows, kept):
        base = 8 * (rows + 1)
        for p in range(rows):
            even, odd = upsampled(y, p, 1152)
            put(buffer, 16 * p, even)
            put(buffer, 16 * p + 8, odd)
        put(buffer, 16 * rows, rows_out(y, 1, 8 * rows, 8 * rows + 8, 1152))
        extra = 8 * (2 * rows + 1)
        for p in range(rows + 1):
            put(buffer, extra + 2 * p, rows_out(y, 1, base + p, base + p + 1, 1152))
            if p < rows:
                odd = rows_out(y, 2, base + p, base + p + 1, 1152) + rows_out(y, 0, base + p + 1, base + p + 2, 1152)
                put(buffer, extra + 2 * p + 1, odd)
        for l in range(3):
            buffer[l] = jnp.where(kept(l) > 0.5, buffer[l], 0.0)

    def emit(ref, rows, value):
        put(out, 0, value)
        for cell in range(8):
            for l in range(3):
                lane0 = CELL * cell + 128 * l
                if rows == 1:
                    piece = out[l, cell : cell + 1, :]
                else:
                    piece = out[l, pl.ds(cell, rows, stride=8), :]
                ref[:, lane0 : lane0 + 128] = piece.astype(BF)

    def block_sums(buffer, rows, factor):
        groups = []
        for first in range(0, rows, factor):
            pieces = []
            for l in range(3):
                total = buffer[l, 8 * first : 8 * first + 8, :]
                for p in range(first + 1, first + factor):
                    total = total + buffer[l, 8 * p : 8 * p + 8, :]
                pieces.append(total)
            groups.append(jnp.concatenate(pieces, axis=1))
        return jnp.concatenate(groups, axis=0).astype(BF)

    def own(buffer, rows):
        return jnp.concatenate([buffer[l, 0 : 8 * rows, :] for l in range(3)], axis=1)

    up = jnp.concatenate([block_sums(c0, 8, 8), block_sums(c1, 4, 4), block_sums(c2, 2, 2)], axis=1)
    emit(o4, 1, own(c3, 1) + dot_nt(up, u3[...]))

    y3 = dot_nt(lhs(lanes_of(c3) + shifted(c3, 2, 3)), e3[...])
    up = jnp.concatenate([block_sums(c0, 8, 4), block_sums(c1, 4, 2)], axis=1)
    down = jnp.concatenate(upsampled(y3, 0, 0), axis=0)
    emit(o3, 2, own(c2, 2) + dot_nt(up, u2[...]) + down)

    section(sg2, y3, 1, lambda l: k2a[l] + k2b[l])
    y2 = dot_nt(lhs(lanes_of(c2) + lanes_of(sg2) + shifted(c2, 3, 2) + shifted(sg2, 3, 2)), e2[...])
    down = jnp.concatenate(upsampled(y2, 0, 0) + upsampled(y2, 1, 0), axis=0)
    emit(o2, 4, own(c1, 4) + dot_nt(block_sums(c0, 8, 2), u1[...]) + down)

    section(sg1, y2, 2, lambda l: k1[l])
    y1 = dot_nt(lhs(lanes_of(c1) + lanes_of(sg1) + shifted(c1, 5, 1) + shifted(sg1, 5, 1)), e1[...])
    rows = []
    for p in range(4):
        rows.extend(upsampled(y1, p, 0))
    emit(o1, 8, own(c0, 8) + jnp.concatenate(rows, axis=0))


VMEM = pl.BlockSpec(memory_space=pltpu.VMEM)
TILES = (2, 4, 4, 2, NZ, 16, 128)


def exchange(*operands):
    def cells(rows):
        return pltpu.VMEM((3, rows, 128), F32)

    return pl.pallas_call(
        compute_kernel,
        out_shape=[jax.ShapeDtypeStruct(g.shape, BF) for g in operands[4:8]],
        in_specs=[VMEM] * 16,
        out_specs=[VMEM] * 4,
        scratch_shapes=[
            pltpu.VMEM((2304, 768), BF),
            pltpu.VMEM((2304, 1280), BF),
            pltpu.VMEM((1152, 1024), BF),
            pltpu.VMEM((384, 1152), BF),
            pltpu.VMEM((384, 768), BF),
            pltpu.VMEM((384, 384), BF),
            pltpu.VMEM((2, 1024, 128), F32),
            cells(64), cells(48), cells(32), cells(32), cells(48), cells(32),
            cells(32), cells(32), cells(16), cells(16), cells(48), cells(32), cells(32), cells(48), cells(64),
        ],
        compiler_params=pltpu.CompilerParams(vmem_limit_bytes=56 * 2**20),
        name="exchange",
    )(*operands)


def per_device(g1, g2, g3, g4, p1, p2, p3, p4, m20, m30a, m30b, m31, block_params):
    raw = jnp.pad(block_params, (0, RAW_ROWS * 128 - SHARD)).reshape(RAW_ROWS, 128)
    halo_types = [jax.ShapeDtypeStruct((rows, CELL), BF) for rows in (48, 32, 32)]
    gathered = pl.pallas_call(
        gather_kernel,
        out_shape=[jax.ShapeDtypeStruct(TILES, BF)] + halo_types,
        in_specs=[VMEM] * 11,
        out_specs=[VMEM] * 4,
        scratch_shapes=[
            pltpu.VMEM((RAW_ROWS, 128), BF),
            pltpu.VMEM((RAW_ROWS, 128), BF),
            pltpu.VMEM((WINDOW, 128), F32),
            pltpu.VMEM((48, CELL), F32),
            pltpu.VMEM((32, CELL), F32),
            pltpu.VMEM((48, CELL), BF),
            pltpu.VMEM((32, CELL), BF),
            pltpu.SemaphoreType.DMA((5,)),
            pltpu.SemaphoreType.DMA((5,)),
            pltpu.SemaphoreType.DMA((NZ - 1,)),
            pltpu.SemaphoreType.DMA((NZ - 1,)),
            pltpu.SemaphoreType.DMA((72,)),
            pltpu.SemaphoreType.DMA((72,)),
        ],
        compiler_params=pltpu.CompilerParams(
            collective_id=0, has_side_effects=True, vmem_limit_bytes=32 * 2**20
        ),
        name="gather",
    )(raw, g2, g3, g4, p2, p3, p4, m20, m30a, m30b, m31)

    return exchange(*gathered, g1, g2, g3, g4, p1, p2, p3, p4, m20, m30a, m30b, m31)


def solution(mesh):
    maps = P("tile", "branch")
    return jax.shard_map(
        per_device, mesh=mesh, in_specs=(maps,) * 12 + (P("tile"),), out_specs=(maps,) * 4, check_vma=False
    )
```

time: 786 us -> 75.2 us (0.10)
  waiting for transfers between devices: 571 us -> 0 us
  blocking collectives: 113 us -> 0 us
  Pallas kernels: 0 us -> 62.3 us
  starting transfers between devices: 36.3 us -> 0 us
  local copies, waits for them, and re-layouts: 39.3 us -> 11.6 us
  between operations: 14.6 us -> 0.66 us
  other arithmetic: 9.08 us -> 0 us
    unnamed x9 -> x0, waiting for transfers between devices: 544 us -> none
    all_gather x12 -> x0, blocking collectives: 113 us -> none  [the longest x1 10.4 us: per_device(): lax.all_gather(grad_second, 'branch', axis=1, tiled=True)]
    pallas_call x0 -> x2, Pallas kernels: none -> 62.3 us  [the longest x1 48.8 us: per_device(): pl.pallas_call(gather_kernel, out_shape=[jax.ShapeDtypeStruct(TILES, BF)]...]
    ppermute x1 -> x0, starting transfers between devices: 36.1 us -> none  [passed_along(): lax.ppermute(value, axis, [(source, source + steps) for source in range(l...]
    reduce_scatter x1 -> x0, waiting for transfers between devices: 26.4 us -> none  [per_device(): lax.psum_scatter(partials[0], 'branch', scatter_dimension=1, tiled=True)]
    unnamed x46 -> x28, local copies, waits for them, and re-layouts: 31.1 us -> 10.8 us
  transfers between devices with their start and end apart: 6 -> 0, of which waited for: 5 -> 0; matrix products, arithmetic and copies ran while one was open for 3% -> 0% of each run, Pallas kernels for 0% -> 0%
where the time goes in v1:
time: 75.2 us; the launch traced here: 74.5 us
  Pallas kernels  62.3 us (83%)
  local copies, waits for them, and re-layouts  11.6 us (15%)
    pallas_call x1, Pallas kernels, per_device(): pl.pallas_call(gather_kernel, out_shape=[jax.ShapeDtypeStruct(TILES, BF)]...  48.8 us
    pallas_call x1, Pallas kernels, exchange(): pl.pallas_call(compute_kernel, out_shape=[jax.ShapeDtypeStruct(g.shape, B...  13.5 us
    unnamed x28, local copies, waits for them, and re-layouts  10.8 us

profile of v1, /device:TPU:1, one launch (start us, length us, event | category | flops | bytes accessed | tf_op | source)
XLA Modules:
  0.0 74.5 jit_solution(9985386721783128572)
XLA Ops:
  0.6 0.8 %pad_bitcast_fusion.raw = bf16[112,128]{1,0:T(8,128)(2,1)S(1)} fusion(bf16[13734]{0:T(1024)(128)(2,1)} %param.25), kind=kLoop, calls=%fused_computation | loop fusion | bytes 56140 | tf_op jit(solution)/shard_map/reshape | solution.py:577
  1.4 0.0 copy-start.1
  1.4 0.7 copy-done.1
  2.1 0.0 copy-start.2
  2.1 0.7 copy-done.2
  2.9 0.0 copy-start.3
  2.9 0.7 copy-done.3
  3.6 0.0 copy-start.4
  3.6 0.7 copy-done.4
  4.3 0.0 copy-start.5
  4.3 0.7 copy-done.5
  5.0 0.0 copy-start.6
  5.0 0.7 copy-done.6
  5.7 0.0 copy-start.7
  5.7 0.7 copy-done.7
  6.4 0.0 copy-start.8
  6.4 0.7 copy-done.8
  7.1 0.0 copy-start.12
  7.1 0.7 copy-done.12
  7.8 0.0 copy-start.13
  7.8 0.7 copy-done.13
  8.5 48.8 %gather.1 = (bf16[2,4,4,2,16,16,128]{6,5,4,3,2,1,0:T(8,128)(2,1)S(1)}, bf16[48,384]{1,0:T(8,128)(2,1)S(1)}, bf16[32,384]{1,0:T(8,128)(2,1)S(1)}, bf16[32,384]{1,0:T(8,128)(2,1)S(1)}) custom-call(bf16[112,128]{1,0:T(8,128)(2,1)S(1)} %pad_bitcast_fusion.raw, bf16[4,3072]{1,0:T(4,128)(2,1)S(1)} %copy-done.1, bf16[2,3072]{1,0:T(2,128)(2,1)S(1)} %copy-done.3, ...), custom_call_target="tpu_custom_call" | custom-call | tf_op jit(solution)/shard_map/gather/pallas_call | solution.py:579
  57.2 0.0 copy-start
  57.3 1.9 %copy-done = bf16[2,4,4,2,16,16,128]{6,5,4,3,2,1,0:T(8,128)(2,1)} copy-done((bf16[2,4,4,2,16,16,128]{6,5,4,3,2,1,0:T(8,128)(2,1)}, bf16[2,4,4,2,16,16,128]{6,5,4,3,2,1,0:T(8,128)(2,1)S(1)}, u32[]{:S(2)}) %copy-start) | copy-done | bytes 4194328
  59.2 0.0 copy-start.9
  59.2 0.6 copy-done.9
  59.8 0.0 copy-start.10
  59.8 0.6 copy-done.10
  60.4 0.0 copy-start.11
  60.4 0.6 copy-done.11
  61.0 13.5 %exchange.1 = (bf16[8,3072]{1,0:T(8,128)(2,1)}, bf16[4,3072]{1,0:T(4,128)(2,1)}, bf16[2,3072]{1,0:T(2,128)(2,1)}, bf16[1,3072]{1,0:T(2,128)(2,1)}) custom-call(bf16[2,4,4,2,16,16,128]{6,5,4,3,2,1,0:T(8,128)(2,1)} %copy-done, bf16[48,384]{1,0:T(8,128)(2,1)} %copy-done.9, bf16[32,384]{1,0:T(8,128)(2,1)} %copy-done.10, bf16[32,384]{1,0:T(8,128)(2,1)} %copy-done.11, ...), custom_call_target="tpu_custom_call" | custom-call | tf_op jit(solution)/shard_map/exchange/pallas_call | solution.py:555
Async XLA Ops:
  1.4 0.7 copy-start.1
  2.1 0.7 copy-start.2
  2.9 0.7 copy-start.3
  3.6 0.7 copy-start.4
  4.3 0.7 copy-start.5
  5.0 0.7 copy-start.6
  5.7 0.7 copy-start.7
  6.4 0.7 copy-start.8
  7.1 0.7 copy-start.12
  7.8 0.7 copy-start.13
  57.2 1.9 %copy-start = (bf16[2,4,4,2,16,16,128]{6,5,4,3,2,1,0:T(8,128)(2,1)}, bf16[2,4,4,2,16,16,128]{6,5,4,3,2,1,0:T(8,128)(2,1)S(1)}, u32[]{:S(2)}) copy-start(bf16[2,4,4,2,16,16,128]{6,5,4,3,2,1,0:T(8,128)(2,1)S(1)} %get-tuple-element.8.tiles) | copy-start | bytes 12582916
  59.2 0.6 copy-start.9
  59.8 0.6 copy-start.10
  60.4 0.6 copy-start.11

commit v2 on v1

v2 whole, which is shorter than its diff:
```python
import jax
import jax.numpy as jnp
from jax import lax
from jax.experimental import pallas as pl
from jax.experimental.pallas import tpu as pltpu
from jax.sharding import PartitionSpec as P

BF = jnp.bfloat16
F32 = jnp.float32
MESH = pl.DeviceIdType.MESH
N_TILE = 128
N_BRANCH = 4
NZ = 16
SHARD = 13734
CELL = 384
RAW_ROWS = 112
BASE = 104
WINDOW = 464

ROW0 = {
    (0, 1, 0): 0,
    (0, 2, 0): 12,
    (0, 3, 0): 36,
    (1, 0, 0): 84,
    (1, 2, 0): 192,
    (1, 3, 0): 240,
    (2, 0, 0): 336,
    (2, 0, 1): 390,
    (2, 1, 0): 606,
    (2, 3, 0): 1038,
    (3, 0, 0): 1230,
    (3, 0, 1): 1284,
    (3, 0, 2): 1338,
    (3, 1, 0): 1770,
    (3, 1, 1): 1986,
    (3, 2, 0): 2850,
}


def remote(src, dst, send, recv, branch, tile):
    return pltpu.make_async_remote_copy(
        src_ref=src, dst_ref=dst, send_sem=send, recv_sem=recv, device_id=(branch, tile), device_id_type=MESH
    )


def tile_at(row_tile, jb):
    group, n = row_tile // 9, 3 * (row_tile % 9) + jb
    j, slot = n // 7, n % 7
    k = 4 * group + j
    return slot % 2, slot // 2, (k // 2) % 4, k % 2, k // 8


def dot(a, b):
    return lax.dot_general(a, b, (((1,), (0,)), ((), ())), preferred_element_type=F32)


def dot_nt(a, b):
    return lax.dot_general(a, b, (((1,), (1,)), ((), ())), preferred_element_type=F32)


def unit_matrix(rows, cols, target):
    column = lax.broadcasted_iota(jnp.int32, (1, cols), 1)
    row = lax.broadcasted_iota(jnp.int32, (rows, cols), 0)
    return jnp.where(row == target(column), 1.0, 0.0).astype(BF)


def exchange_kernel(
    *refs,
):
    inputs, outputs, refs = refs[:13], refs[13:17], refs[17:]
    loaded, refs = refs[:13], refs[13:]
    (
        tiles, row_in, col_in, corner_in, raw1, raw2, win, row_f, col_f, row_out, col_out,
        e3, e2, e1, u3, u2, u1, wide,
        c0, c1, c2, c3, sg1, sg2, q20, q30a, q30b, q31, k1, k2a, k2b, nxt, out,
        l_sem, h_send, h_recv, z_send, z_recv, s_send, s_recv,
    ) = refs
    g1, g2, g3, g4, p1, p2, p3, p4, m20, m30a, m30b, m31, raw = loaded
    o1, o2, o3, o4 = outputs
    b = lax.axis_index("branch")
    k = lax.axis_index("tile")
    z, y, c = k // 8, lax.rem(k // 2, 4), lax.rem(k, 2)
    has_row = k < N_TILE - 1
    has_col = b < N_BRANCH - 1

    loads = [pltpu.make_async_copy(inputs[n], loaded[n], l_sem.at[n]) for n in range(13)]
    for n in (12, 1, 2, 3, 5, 6, 7, 8, 9, 10, 11, 0, 4):
        loads[n].start()

    def tile_of(zz, yy, cc):
        return zz * 8 + yy * 2 + cc

    def wrap(value, count):
        return lax.rem(value + count, count)

    left, right = wrap(b - 1, N_BRANCH), wrap(b + 1, N_BRANCH)
    up1, up2 = wrap(k - 1, N_TILE), wrap(k - 2, N_TILE)
    down1, down2 = wrap(k + 1, N_TILE), wrap(k + 2, N_TILE)
    y_prev, y_next = wrap(y - 1, 4), wrap(y + 1, 4)

    partners = [
        (b, up1), (b, up2), (b, down1), (b, down2), (left, k), (right, k), (left, up1), (right, down1),
        (b, tile_of(z, y_prev, c)), (b, tile_of(z, y_next, c)), (b, tile_of(z, y, 1 - c)),
    ]
    barrier = pltpu.get_barrier_semaphore()
    for step in range(1, NZ):
        pl.semaphore_signal(
            barrier, inc=1, device_id=(b, tile_of(wrap(z + step, NZ), y, c)), device_id_type=MESH
        )
    for who in partners:
        pl.semaphore_signal(barrier, inc=1, device_id=who, device_id_type=MESH)

    for ref in (e3, e2, e1, c1, c2, c3, sg1, sg2, q20, q30a, q30b, q31, k1, k2a, k2b, nxt, win):
        ref[...] = jnp.zeros_like(ref)

    for load in loads:
        load.wait()
    row_f[...] = jnp.zeros_like(row_f)
    col_f[...] = jnp.zeros_like(col_f)
    at_row, at_col = 0, 0
    for g, p in ((g2, p2), (g3, p3), (g4, p4)):
        rows = g.shape[0]
        masked = jnp.where(p[...].astype(F32) > 0, g[...].astype(F32), 0.0)
        for cell in range(8):
            row_f[at_row + cell : at_row + cell + 1, :] = masked[0:1, CELL * cell : CELL * (cell + 1)]
        col_f[at_col : at_col + rows, :] = masked[:, 0:CELL]
        at_row, at_col = at_row + 8, at_col + rows
    for m, at_row, at_col in ((m20, 24, 8), (m30a, 28, 12), (m31, 32, 18), (m30b, 36, 16)):
        rows, units = m.shape[0], m.shape[1] // CELL
        value = m[...].astype(F32)
        for unit in range(units):
            row_f[at_row + unit : at_row + unit + 1, :] = value[0:1, CELL * unit : CELL * (unit + 1)]
        col_f[at_col : at_col + rows, :] = value[:, 0:CELL]
    row_out[...] = row_f[...].astype(BF)
    col_out[...] = col_f[...].astype(BF)


    pl.semaphore_wait(barrier, len(partners) + NZ - 1)
    first = [
        remote(raw, raw1, h_send.at[0], h_recv.at[0], b, up1),
        remote(raw, raw2, h_send.at[1], h_recv.at[1], b, up2),
        remote(row_out, row_in, h_send.at[2], h_recv.at[2], b, up1),
        remote(col_out, col_in, h_send.at[3], h_recv.at[3], left, k),
        remote(col_out, corner_in, h_send.at[4], h_recv.at[4], left, up1),
    ]
    for copy in first:
        copy.start()

    def put(buffer, row, value):
        rows = value.shape[0]
        for l in range(3):
            buffer[l, row : row + rows, :] = value[:, 128 * l : 128 * (l + 1)]

    def spread_units(buffer, value, units):
        rows = value.shape[0]
        for unit in range(units):
            for l in range(3):
                piece = value[:, CELL * unit + 128 * l : CELL * unit + 128 * (l + 1)]
                if rows == 1:
                    buffer[l, unit : unit + 1, :] = piece
                else:
                    buffer[l, pl.ds(unit, rows, stride=units), :] = piece

    def masked(g, p):
        return jnp.where(p[...].astype(F32) > 0, g[...].astype(F32), 0.0)

    spread_units(c0, masked(g1, p1), 8)
    for buffer, g, p in ((c1, g2, p2), (c2, g3, p3), (c3, g4, p4)):
        spread_units(buffer, masked(g, p), 8)
    for buffer, m, units in ((q20, m20, 4), (q30a, m30a, 4), (q31, m31, 4), (q30b, m30b, 2)):
        spread_units(buffer, m[...].astype(F32), units)

    group, j = k // 4, lax.rem(k, 4)
    first_tile = (7 * j) // 3
    delta = 13734 * j - 6144 * first_tile - 360 * group + BASE * 128
    lane = lax.broadcasted_iota(jnp.int32, (RAW_ROWS, 128), 1)
    for d, shard in enumerate((raw, raw1, raw2)):
        if d > 0:
            first[d - 1].wait_recv()
        start = delta + SHARD * d
        q, phase = start // 128, lax.rem(start, 128)
        rolled = pltpu.roll(shard[...].astype(F32), phase, 1)
        win[pl.ds(q, RAW_ROWS), :] += jnp.where(lane >= phase, rolled, 0.0)
        win[pl.ds(q + 1, RAW_ROWS), :] += jnp.where(lane >= phase, 0.0, rolled)
    for s in range(2):
        n = 7 * j + 2 * b + s
        row_tile = 9 * group + n // 3
        offset = jnp.where(row_tile >= 124, 2, 10)
        origin = BASE + 3 * (16 * (n // 3 - first_tile) + offset) + lax.rem(n, 3)
        tiles[s, b, y, c, z] = win[pl.ds(origin, 16, stride=3), :].astype(BF)

    copies = []
    own = tiles.at[:, b, y, c, z]
    for step in (8, 7, 9, 6, 10, 5, 11, 4, 12, 3, 13, 2, 14, 1, 15):
        copy = remote(
            own, own, z_send.at[step - 1], z_recv.at[step - 1], b, tile_of(wrap(z + step, NZ), y, c)
        )
        copy.start()
        copies.append(copy)

    for copy in first[2:]:
        copy.wait_recv()
    row_halo = row_in[...].astype(F32)
    col_halo = col_in[...].astype(F32)
    corner = corner_in[...].astype(F32)
    row_zero = jnp.where(has_row, row_halo, 0.0)
    col_zero = jnp.where(has_col, col_halo, 0.0)
    corner_zero = jnp.where(has_row & has_col, corner, 0.0)
    at = 0
    for buffer, rows, halo in ((c1, 4, 0), (c2, 2, 8), (c3, 1, 16)):
        put(buffer, 8 * rows, row_zero[halo : halo + 8])
        put(buffer, 8 * rows + 8, col_zero[at : at + rows])
        put(buffer, 8 * rows + 8 + rows, corner_zero[at : at + 1])
        at += rows
    for buffer, rows, units, halo, at in ((q20, 4, 4, 24, 8), (q30a, 4, 4, 28, 12), (q31, 2, 4, 32, 18), (q30b, 2, 2, 36, 16)):
        put(buffer, rows * units, row_halo[halo : halo + units])
        put(buffer, (rows + 1) * units, col_halo[at : at + rows])
        put(buffer, (rows + 1) * units + rows, corner[at : at + 1])

    def flags(buffer):
        whole = jnp.concatenate([buffer[l] for l in range(3)], axis=1)
        return jnp.where(whole > 0, 1.0, 0.0).astype(BF)

    def target20(shift):
        def target(col):
            part, lane = col // CELL, lax.rem(col, CELL)
            pixel, channel = lane // 96, lax.rem(lane, 96) - shift
            return jnp.where((channel >= 0) & (channel < 48), part * 192 + pixel * 48 + channel, -1)

        return target

    def target31(col):
        part, lane = col // CELL, lax.rem(col, CELL)
        return jnp.where(lane < 192, part * 192 + lane, -1)

    def target30b(col):
        part, lane = col // CELL, lax.rem(col, CELL) - 192
        return jnp.where((lane >= 0) & (lane < 96), part * 96 + lane, -1)

    def keep(buffer, value, parts, count, extra_from, extra_rows, extra_to):
        for l in range(3):
            for part in range(parts):
                lanes = slice(part * CELL + 128 * l, part * CELL + 128 * (l + 1))
                buffer[l, pl.ds(part, count, stride=parts), :] = value[0:count, lanes]
            buffer[l, extra_to : extra_to + extra_rows, :] = value[
                extra_from : extra_from + extra_rows, 128 * l : 128 * (l + 1)
            ]

    mask1 = dot(flags(q20), unit_matrix(CELL, 768, target20(0))) + dot(
        flags(q30a), unit_matrix(CELL, 768, target20(48))
    )
    keep(k1, mask1, 2, 20, 20, 5, 40)
    keep(k2a, dot(flags(q31), unit_matrix(CELL, 768, target31)), 2, 12, 12, 3, 24)
    keep(k2b, dot(flags(q30b), unit_matrix(CELL, 1536, target30b)), 4, 6, 6, 3, 24)

    def load_rows(row_tile, count):
        columns = [
            jnp.concatenate([tiles[tile_at(row_tile + t, jb)] for t in range(count)], axis=0) for jb in range(3)
        ]
        return jnp.concatenate(columns, axis=1)

    def rows_of(key, rows, j, at=0):
        n = CELL // j
        r0 = ROW0[key]
        row_tile, offset = (286, 0) if r0 == 0 else divmod(r0 - 10, 16)
        count = -(-(offset + rows) // 16)
        width = 256 if j == 192 else 128

        def target(col):
            part, lane = col // width, lax.rem(col, width) - at
            return jnp.where((lane >= 0) & (lane < j), part * j + lane, -1)

        split = dot(load_rows(row_tile, count), unit_matrix(CELL, n * width, target))
        parts = []
        for half in range(width // 128):
            for part in range(n):
                wide[half, pl.ds(part, 16 * count, stride=n), :] = split[
                    :, part * width + 128 * half : part * width + 128 * (half + 1)
                ]
            parts.append(wide[half, offset * n : (offset + rows) * n, :])
        return parts[0] if len(parts) == 1 else jnp.concatenate(parts, axis=1)

    def place(weights, j, low, high):
        rows = weights.shape[1]

        def target(col):
            which = col // j
            return jnp.where((which >= low) & (which < high), lax.rem(col, j), -1)

        return dot(weights, unit_matrix(rows, CELL, target))

    def taps(e, row0, pitch, weights, placed, seg, nxt_seg, nxt_width):
        count = len(placed)
        i = weights.shape[0] // 9

        def tap(value, a, bb):
            return value[(3 * a + bb) * i : (3 * a + bb + 1) * i]

        for a in range(3):
            for q in range(count):
                even = row0 + CELL * a + 2 * q * pitch
                e[even : even + i, seg : seg + CELL] = tap(placed[q], a, 1).astype(BF)
                odd = even + pitch
                value = tap(placed[q], a, 2)
                if q + 1 < count:
                    value = value + tap(placed[q + 1], a, 0)
                else:
                    e[odd : odd + i, nxt_seg : nxt_seg + nxt_width] = tap(weights, a, 0).astype(BF)
                e[odd : odd + i, seg : seg + CELL] = value.astype(BF)

    def fill_e3():
        for key, i, row0, pitch in (
            ((3, 2, 0), 192, 0, 192),
            ((3, 1, 1), 96, 1152, 96),
            ((3, 0, 2), 48, 1152 + 192, 48),
        ):
            r0 = ROW0[key]
            start = 124 + (r0 - 1986) // 16 if r0 >= 1986 else (r0 - 10) // 16
            for a in range(3):
                even = row0 + CELL * a
                odd = even + pitch
                for bb, at, seg in ((1, even, 0), (2, odd, 0), (0, odd, CELL)):
                    first = start + (3 * a + bb) * (i // 16)
                    for t in range(i // 16):
                        for jb in range(3):
                            e3[at + 16 * t : at + 16 * (t + 1), seg + 128 * jb : seg + 128 * (jb + 1)] = tiles[
                                tile_at(first + t, jb)
                            ]

    def fill_e2():
        w = rows_of((2, 1, 0), 432, 192)
        taps(e2, 0, 96, w, [place(w.astype(BF), 192, q, q + 1) for q in range(2)], 0, 768, 256)
        w = rows_of((3, 1, 0), 216, 96)
        taps(e2, 0, 96, w, [place(w.astype(BF), 96, q, q + 1) for q in range(2)], 384, 1024, 128)
        w = rows_of((2, 0, 1), 216, 192)
        placed = [place(w.astype(BF), 192, q, q + 1) for q in range(2)]
        taps(e2, 1152, 96, w, placed, 0, 768, 256)
        w = rows_of((3, 0, 1), 54, 48)
        w_next = rows_of((3, 0, 1), 54, 48, 64)
        placed = [place(w.astype(BF), 48, 4 + q, 5 + q) for q in range(2)]
        taps(e2, 1152 + 48, 96, w_next, placed, 384, 1024 + 128, 128)

    def fill_e1():
        w = rows_of((1, 0, 0), 108, 96)
        taps(e1, 0, 48, w, [place(w.astype(BF), 96, q, q + 1) for q in range(4)], 0, 768, 128)
        w = rows_of((2, 0, 0), 54, 48) + 0.0
        w = w + rows_of((3, 0, 0), 54, 48, 48)
        taps(e1, 0, 48, w, [place(w.astype(BF), 96, q, q + 1) for q in range(4)], 384, 896, 128)

    def fill_up():
        u3[:, 0:384] = place(rows_of((0, 3, 0), 48, 48).astype(BF), 48, 0, 8).astype(BF)
        u3[:, 384:768] = place(rows_of((1, 3, 0), 96, 96).astype(BF), 96, 0, 4).astype(BF)
        u3[:, 768:1152] = place(rows_of((2, 3, 0), 192, 192).astype(BF), 192, 0, 2).astype(BF)
        w02 = rows_of((0, 2, 0), 24, 48).astype(BF)
        w12 = rows_of((1, 2, 0), 48, 96).astype(BF)
        for q in range(2):
            u2[192 * q : 192 * (q + 1), 0:384] = place(w02, 48, 4 * q, 4 * q + 4).astype(BF)
            u2[192 * q : 192 * (q + 1), 384:768] = place(w12, 96, 2 * q, 2 * q + 2).astype(BF)
        w01 = rows_of((0, 1, 0), 12, 48).astype(BF)
        for q in range(4):
            u1[96 * q : 96 * (q + 1), :] = place(w01, 48, 2 * q, 2 * q + 2).astype(BF)

    for copy in copies:
        copy.wait_recv()

    class Half:
        def __init__(self, s, lo):
            self.s, self.lo = s, lo
            self.u, self.v = (b, y) if s == 0 else (y, b)
            self.pending, self.across = [], []
            self.used = 36 * (2 * s + lo // 8)

        def bundle(self, u, v, part):
            x_at, y_at = (u, v) if self.s == 0 else (v, u)
            ref = tiles.at[self.s, x_at, y_at, c]
            return ref.at[pl.ds(self.lo, 8)] if part is None else ref.at[pl.ds(self.lo + 4 * part, 4)]

        def send(self, u, v, part, to_u, to_v, other_core=False):
            x_to, y_to = (to_u, to_v) if self.s == 0 else (to_v, to_u)
            ref = self.bundle(u, v, part)
            copy = remote(
                ref, ref, s_send.at[self.used], s_recv.at[self.used], x_to,
                tile_of(z, y_to, 1 - c if other_core else c),
            )
            copy.start()
            self.used += 1
            self.pending.append(copy)
            if other_core:
                self.across.append(copy)
            return copy

        def first(self):
            u, v = self.u, self.v
            self.to_next = self.send(u, v, None, wrap(u + 1, 4), v)
            self.to_prev = self.send(u, v, None, wrap(u - 1, 4), v)
            self.second = [self.spread(u)]

        def spread(self, u_of):
            u, v = self.u, self.v
            to_next = self.send(u_of, v, None, u, wrap(v + 1, 4))
            to_prev = self.send(u_of, v, None, u, wrap(v - 1, 4))
            self.send(u_of, v, None, u, v, True)
            return u_of, to_next, to_prev

        def forward(self):
            u, v = self.u, self.v
            self.to_next.wait_recv()
            prev_u, next_u = wrap(u - 1, 4), wrap(u + 1, 4)
            self.far_next = self.send(prev_u, v, 0, next_u, v)
            self.second.append(self.spread(prev_u))
            self.to_prev.wait_recv()
            self.far_prev = self.send(next_u, v, 1, prev_u, v)
            self.second.append(self.spread(next_u))

        def far(self):
            self.far_next.wait_recv()
            self.far_prev.wait_recv()
            self.second.append(self.spread(wrap(self.u + 2, 4)))

        def finish(self, number):
            u, v = self.u, self.v
            u_of, to_next, to_prev = self.second[number]
            to_next.wait_recv()
            a = self.send(u_of, wrap(v - 1, 4), 0, u, wrap(v + 1, 4))
            self.send(u_of, wrap(v - 1, 4), None, u, v, True)
            to_prev.wait_recv()
            d = self.send(u_of, wrap(v + 1, 4), 1, u, wrap(v - 1, 4))
            self.send(u_of, wrap(v + 1, 4), None, u, v, True)
            return u_of, a, d

        def last(self, state):
            u_of, a, d = state
            a.wait_recv()
            d.wait_recv()
            self.send(u_of, wrap(self.v + 2, 4), None, self.u, self.v, True)

        def arrived(self):
            for copy in self.across:
                copy.wait_recv()

    near, far = [Half(0, 0), Half(1, 0)], [Half(0, 8), Half(1, 8)]
    for half in near + far:
        half.first()
    for half in near + far:
        half.forward()
    for half in near + far:
        half.far()

    def finish(part, numbers):
        return [(half, half.finish(number)) for number in numbers for half in part]

    near_states = finish(near, range(4))
    for half, state in near_states:
        half.last(state)
    far_states = finish(far, range(4))
    for half in near:
        half.arrived()
    fill_e2()
    for half, state in far_states:
        half.last(state)
    fill_e1()
    for half in far:
        half.arrived()
    fill_up()
    fill_e3()

    def lanes_of(buffer, count=3):
        return [buffer[l] for l in range(count)]

    def shifted(buffer, rows, count):
        total = buffer.shape[1]
        pieces = []
        for l in range(count):
            nxt[l, 0 : 8 * rows, :] = buffer[l, 1 : 8 * rows + 1, :]
            for p in range(rows):
                nxt[l, 8 * p + 7 : 8 * p + 8, :] = buffer[l, 8 * rows + p : 8 * rows + p + 1, :]
            nxt[l, 8 * rows : total, :] = jnp.zeros((total - 8 * rows, 128), F32)
            pieces.append(nxt[l, 0:total, :])
        return pieces

    def lhs(pieces):
        return jnp.concatenate([piece.astype(BF) for piece in pieces], axis=1)

    def rows_out(y, a, lo, hi, lane0):
        return y[lo:hi, lane0 + CELL * a : lane0 + CELL * (a + 1)]

    def upsampled(y, p, lane0):
        even = rows_out(y, 1, 8 * p, 8 * p + 8, lane0)
        odd = rows_out(y, 2, 8 * p, 8 * p + 8, lane0) + rows_out(y, 0, 8 * p + 8, 8 * p + 16, lane0)
        return even, odd

    def section(buffer, y, rows, kept):
        base = 8 * (rows + 1)
        for p in range(rows):
            even, odd = upsampled(y, p, 1152)
            put(buffer, 16 * p, even)
            put(buffer, 16 * p + 8, odd)
        put(buffer, 16 * rows, rows_out(y, 1, 8 * rows, 8 * rows + 8, 1152))
        extra = 8 * (2 * rows + 1)
        for p in range(rows + 1):
            put(buffer, extra + 2 * p, rows_out(y, 1, base + p, base + p + 1, 1152))
            if p < rows:
                odd = rows_out(y, 2, base + p, base + p + 1, 1152) + rows_out(y, 0, base + p + 1, base + p + 2, 1152)
                put(buffer, extra + 2 * p + 1, odd)
        for l in range(3):
            buffer[l] = jnp.where(kept(l) > 0.5, buffer[l], 0.0)

    def emit(ref, rows, value):
        put(out, 0, value)
        for cell in range(8):
            for l in range(3):
                lane0 = CELL * cell + 128 * l
                if rows == 1:
                    piece = out[l, cell : cell + 1, :]
                else:
                    piece = out[l, pl.ds(cell, rows, stride=8), :]
                ref[:, lane0 : lane0 + 128] = piece.astype(BF)

    def block_sums(buffer, rows, factor):
        groups = []
        for first in range(0, rows, factor):
            pieces = []
            for l in range(3):
                total = buffer[l, 8 * first : 8 * first + 8, :]
                for p in range(first + 1, first + factor):
                    total = total + buffer[l, 8 * p : 8 * p + 8, :]
                pieces.append(total)
            groups.append(jnp.concatenate(pieces, axis=1))
        return jnp.concatenate(groups, axis=0).astype(BF)

    def own(buffer, rows):
        return jnp.concatenate([buffer[l, 0 : 8 * rows, :] for l in range(3)], axis=1)

    up = jnp.concatenate([block_sums(c0, 8, 8), block_sums(c1, 4, 4), block_sums(c2, 2, 2)], axis=1)
    emit(o4, 1, own(c3, 1) + dot_nt(up, u3[...]))

    y3 = dot_nt(lhs(lanes_of(c3) + shifted(c3, 2, 3)), e3[...])
    up = jnp.concatenate([block_sums(c0, 8, 4), block_sums(c1, 4, 2)], axis=1)
    down = jnp.concatenate(upsampled(y3, 0, 0), axis=0)
    emit(o3, 2, own(c2, 2) + dot_nt(up, u2[...]) + down)

    section(sg2, y3, 1, lambda l: k2a[l] + k2b[l])
    y2 = dot_nt(lhs(lanes_of(c2) + lanes_of(sg2) + shifted(c2, 3, 2) + shifted(sg2, 3, 2)), e2[...])
    down = jnp.concatenate(upsampled(y2, 0, 0) + upsampled(y2, 1, 0), axis=0)
    emit(o2, 4, own(c1, 4) + dot_nt(block_sums(c0, 8, 2), u1[...]) + down)

    section(sg1, y2, 2, lambda l: k1[l])
    y1 = dot_nt(lhs(lanes_of(c1) + lanes_of(sg1) + shifted(c1, 5, 1) + shifted(sg1, 5, 1)), e1[...])
    rows = []
    for p in range(4):
        rows.extend(upsampled(y1, p, 0))
    emit(o1, 8, own(c0, 8) + jnp.concatenate(rows, axis=0))

    for half in near + far:
        for copy in half.pending:
            copy.wait_send()
    for copy in copies + first:
        copy.wait_send()


def finish_kernel(*refs):
    sems = refs[8]
    copies = [pltpu.make_async_copy(refs[n], refs[4 + n], sems.at[n]) for n in range(4)]
    for copy in copies:
        copy.start()
    for copy in copies:
        copy.wait()


ANY = pl.BlockSpec(memory_space=pl.ANY)
VMEM = pl.BlockSpec(memory_space=pltpu.VMEM)
TILES = (2, 4, 4, 2, NZ, 16, 128)


def per_device(*operands):
    maps = operands[:12]
    raw = jnp.pad(operands[12], (0, RAW_ROWS * 128 - SHARD)).reshape(RAW_ROWS, 128)

    def cells(rows):
        return pltpu.VMEM((3, rows, 128), F32)

    def buffer(*shape):
        return pltpu.VMEM(shape, BF)

    def sems(count):
        return pltpu.SemaphoreType.DMA((count,))

    results = [jax.ShapeDtypeStruct(g.shape, BF) for g in maps[:4]]
    done = pl.pallas_call(
        exchange_kernel,
        out_shape=results,
        in_specs=[ANY] * 13,
        out_specs=[VMEM] * 4,
        scratch_shapes=[buffer(*m.shape) for m in maps] + [
            buffer(RAW_ROWS, 128),
            buffer(*TILES), buffer(48, CELL), buffer(32, CELL), buffer(32, CELL),
            buffer(RAW_ROWS, 128), buffer(RAW_ROWS, 128), pltpu.VMEM((WINDOW, 128), F32),
            pltpu.VMEM((48, CELL), F32), pltpu.VMEM((32, CELL), F32), buffer(48, CELL), buffer(32, CELL),
            buffer(2304, 768), buffer(2304, 1280), buffer(1152, 1024),
            buffer(384, 1152), buffer(384, 768), buffer(384, 384),
            pltpu.VMEM((2, 1024, 128), F32),
            cells(64), cells(48), cells(32), cells(32), cells(48), cells(32),
            cells(32), cells(32), cells(16), cells(16), cells(48), cells(32), cells(32), cells(48), cells(64),
            sems(13), sems(5), sems(5), sems(NZ - 1), sems(NZ - 1), sems(144), sems(144),
        ],
        compiler_params=pltpu.CompilerParams(
            collective_id=0, has_side_effects=True, vmem_limit_bytes=60 * 2**20
        ),
        name="exchange",
    )(*maps, raw)
    return pl.pallas_call(
        finish_kernel,
        out_shape=results,
        in_specs=[ANY] * 4,
        out_specs=[ANY] * 4,
        scratch_shapes=[sems(4)],
        compiler_params=pltpu.CompilerParams(vmem_limit_bytes=60 * 2**20),
        name="finish",
    )(*done)


def solution(mesh):
    maps = P("tile", "branch")
    return jax.shard_map(
        per_device, mesh=mesh, in_specs=(maps,) * 12 + (P("tile"),), out_specs=(maps,) * 4, check_vma=False
    )
```

time: 75.2 us -> 64.8 us (0.86)
  local copies, waits for them, and re-layouts: 11.6 us -> 1.36 us
    unnamed x28 -> x0, local copies, waits for them, and re-layouts: 10.8 us -> none
where the time goes in v2:
time: 64.8 us; the launch traced here: 64.6 us
  Pallas kernels  62.6 us (97%)
  local copies, waits for them, and re-layouts  1.36 us (2%)
    pallas_call x1, Pallas kernels, per_device(): pl.pallas_call(exchange_kernel, out_shape=results, in_specs=[ANY] * 13, o...  58.5 us
    pallas_call x1, Pallas kernels, per_device(): pl.pallas_call(finish_kernel, out_shape=results, in_specs=[ANY] * 4, out_...  4.12 us
    reshape x1, local copies, waits for them, and re-layouts, per_device(): jnp.pad(operands[12], (0, RAW_ROWS * 128 - SHARD)).reshape(RAW_ROWS, 128)  1.36 us

profile of v2, /device:TPU:1, one launch (start us, length us, event | category | flops | bytes accessed | tf_op | source)
XLA Modules:
  0.0 64.6 jit_solution(6369289236556045638)
XLA Ops:
  0.6 1.4 %pad_bitcast_fusion.refs_12_ = bf16[112,128]{1,0:T(8,128)(2,1)} fusion(bf16[13734]{0:T(1024)(128)(2,1)} %param.25), kind=kLoop, calls=%fused_computation | loop fusion | bytes 56140 | tf_op jit(solution)/shard_map/reshape | solution.py:577
  2.0 58.5 %exchange.1 = (bf16[8,3072]{1,0:T(8,128)(2,1)}, bf16[4,3072]{1,0:T(4,128)(2,1)}, bf16[2,3072]{1,0:T(2,128)(2,1)}, bf16[1,3072]{1,0:T(2,128)(2,1)}) custom-call(bf16[8,3072]{1,0:T(8,128)(2,1)} %refs_0_.1, bf16[4,3072]{1,0:T(4,128)(2,1)} %refs_1_.1, bf16[2,3072]{1,0:T(2,128)(2,1)} %refs_2_.1, bf16[1,3072]{1,0:T(2,128)(2,1)} %refs_3_.1, ...), custom_call_target="tpu_custom_call" | custom-call | tf_op jit(solution)/shard_map/exchange/pallas_call | solution.py:589
  60.5 4.1 %finish.1 = (bf16[8,3072]{1,0:T(8,128)(2,1)}, bf16[4,3072]{1,0:T(4,128)(2,1)}, bf16[2,3072]{1,0:T(2,128)(2,1)}, bf16[1,3072]{1,0:T(2,128)(2,1)}) custom-call(bf16[8,3072]{1,0:T(8,128)(2,1)} %get-tuple-element.8.refs_0_, bf16[4,3072]{1,0:T(4,128)(2,1)} %get-tuple-element.9.refs_1_, bf16[2,3072]{1,0:T(2,128)(2,1)} %get-tuple-element.10.refs_2_, ...), custom_call_target="tpu_custom_call" | custom-call | tf_op jit(solution)/shard_map/finish/pallas_call | solution.py:611

commit v3 on v2

--- a/solution.py
+++ b/solution.py
@@ -327,25 +327,31 @@
                                 tile_at(first + t, jb)
                             ]
 
-    def fill_e2():
+    def fill_e2_21():
         w = rows_of((2, 1, 0), 432, 192)
-        taps(e2, 0, 96, w, [place(w.astype(BF), 192, q, q + 1) for q in range(2)], 0, 768, 256)
+        taps(e2, 0, 96, w, [place(w.astype(BF), 192, q, q + 1) for q in range(2)], 0, 384, 256)
+
+    def fill_e2_31():
         w = rows_of((3, 1, 0), 216, 96)
-        taps(e2, 0, 96, w, [place(w.astype(BF), 96, q, q + 1) for q in range(2)], 384, 1024, 128)
+        taps(e2, 0, 96, w, [place(w.astype(BF), 96, q, q + 1) for q in range(2)], 640, 1024, 128)
+
+    def fill_e2_mid():
         w = rows_of((2, 0, 1), 216, 192)
         placed = [place(w.astype(BF), 192, q, q + 1) for q in range(2)]
-        taps(e2, 1152, 96, w, placed, 0, 768, 256)
+        taps(e2, 1152, 96, w, placed, 0, 384, 256)
         w = rows_of((3, 0, 1), 54, 48)
         w_next = rows_of((3, 0, 1), 54, 48, 64)
         placed = [place(w.astype(BF), 48, 4 + q, 5 + q) for q in range(2)]
-        taps(e2, 1152 + 48, 96, w_next, placed, 384, 1024 + 128, 128)
-
-    def fill_e1():
+        taps(e2, 1152 + 48, 96, w_next, placed, 640, 1024 + 128, 128)
+
+    def fill_e1_10():
         w = rows_of((1, 0, 0), 108, 96)
-        taps(e1, 0, 48, w, [place(w.astype(BF), 96, q, q + 1) for q in range(4)], 0, 768, 128)
+        taps(e1, 0, 48, w, [place(w.astype(BF), 96, q, q + 1) for q in range(4)], 0, 384, 128)
+
+    def fill_e1_mid():
         w = rows_of((2, 0, 0), 54, 48) + 0.0
         w = w + rows_of((3, 0, 0), 54, 48, 48)
-        taps(e1, 0, 48, w, [place(w.astype(BF), 96, q, q + 1) for q in range(4)], 384, 896, 128)
+        taps(e1, 0, 48, w, [place(w.astype(BF), 96, q, q + 1) for q in range(4)], 512, 896, 128)
 
     def fill_up():
         u3[:, 0:384] = place(rows_of((0, 3, 0), 48, 48).astype(BF), 48, 0, 8).astype(BF)
@@ -359,110 +365,6 @@
         w01 = rows_of((0, 1, 0), 12, 48).astype(BF)
         for q in range(4):
             u1[96 * q : 96 * (q + 1), :] = place(w01, 48, 2 * q, 2 * q + 2).astype(BF)
-
-    for copy in copies:
-        copy.wait_recv()
-
-    class Half:
-        def __init__(self, s, lo):
-            self.s, self.lo = s, lo
-            self.u, self.v = (b, y) if s == 0 else (y, b)
-            self.pending, self.across = [], []
-            self.used = 36 * (2 * s + lo // 8)
-
-        def bundle(self, u, v, part):
-            x_at, y_at = (u, v) if self.s == 0 else (v, u)
-            ref = tiles.at[self.s, x_at, y_at, c]
-            return ref.at[pl.ds(self.lo, 8)] if part is None else ref.at[pl.ds(self.lo + 4 * part, 4)]
-
-        def send(self, u, v, part, to_u, to_v, other_core=False):
-            x_to, y_to = (to_u, to_v) if self.s == 0 else (to_v, to_u)
-            ref = self.bundle(u, v, part)
-            copy = remote(
-                ref, ref, s_send.at[self.used], s_recv.at[self.used], x_to,
-                tile_of(z, y_to, 1 - c if other_core else c),
-            )
-            copy.start()
-            self.used += 1
-            self.pending.append(copy)
-            if other_core:
-                self.across.append(copy)
-            return copy
-
-        def first(self):
-            u, v = self.u, self.v
-            self.to_next = self.send(u, v, None, wrap(u + 1, 4), v)
-            self.to_prev = self.send(u, v, None, wrap(u - 1, 4), v)
-            self.second = [self.spread(u)]
-
-        def spread(self, u_of):
-            u, v = self.u, self.v
-            to_next = self.send(u_of, v, None, u, wrap(v + 1, 4))
-            to_prev = self.send(u_of, v, None, u, wrap(v - 1, 4))
-            self.send(u_of, v, None, u, v, True)
-            return u_of, to_next, to_prev
-
-        def forward(self):
-            u, v = self.u, self.v
-            self.to_next.wait_recv()
-            prev_u, next_u = wrap(u - 1, 4), wrap(u + 1, 4)
-            self.far_next = self.send(prev_u, v, 0, next_u, v)
-            self.second.append(self.spread(prev_u))
-            self.to_prev.wait_recv()
-            self.far_prev = self.send(next_u, v, 1, prev_u, v)
-            self.second.append(self.spread(next_u))
-
-        def far(self):
-            self.far_next.wait_recv()
-            self.far_prev.wait_recv()
-            self.second.append(self.spread(wrap(self.u + 2, 4)))
-
-        def finish(self, number):
-            u, v = self.u, self.v
-            u_of, to_next, to_prev = self.second[number]
-            to_next.wait_recv()
-            a = self.send(u_of, wrap(v - 1, 4), 0, u, wrap(v + 1, 4))
-            self.send(u_of, wrap(v - 1, 4), None, u, v, True)
-            to_prev.wait_recv()
-            d = self.send(u_of, wrap(v + 1, 4), 1, u, wrap(v - 1, 4))
-            self.send(u_of, wrap(v + 1, 4), None, u, v, True)
-            return u_of, a, d
-
-        def last(self, state):
-            u_of, a, d = state
-            a.wait_recv()
-            d.wait_recv()
-            self.send(u_of, wrap(self.v + 2, 4), None, self.u, self.v, True)
-
-        def arrived(self):
-            for copy in self.across:
-                copy.wait_recv()
-
-    near, far = [Half(0, 0), Half(1, 0)], [Half(0, 8), Half(1, 8)]
-    for half in near + far:
-        half.first()
-    for half in near + far:
-        half.forward()
-    for half in near + far:
-        half.far()
-
-    def finish(part, numbers):
-        return [(half, half.finish(number)) for number in numbers for half in part]
-
-    near_states = finish(near, range(4))
-    for half, state in near_states:
-        half.last(state)
-    far_states = finish(far, range(4))
-    for half in near:
-        half.arrived()
-    fill_e2()
-    for half, state in far_states:
-        half.last(state)
-    fill_e1()
-    for half in far:
-        half.arrived()
-    fill_up()
-    fill_e3()
 
     def lanes_of(buffer, count=3):
         return [buffer[l] for l in range(count)]
@@ -531,6 +433,120 @@
     def own(buffer, rows):
         return jnp.concatenate([buffer[l, 0 : 8 * rows, :] for l in range(3)], axis=1)
 
+    for copy in copies:
+        copy.wait_recv()
+
+    class Half:
+        def __init__(self, s, lo):
+            self.s, self.lo = s, lo
+            self.u, self.v = (b, y) if s == 0 else (y, b)
+            self.pending, self.across = [], []
+            self.used = 24 * (2 * s + lo // 8)
+
+        def bundle(self, u, v, part):
+            x_at, y_at = (u, v) if self.s == 0 else (v, u)
+            ref = tiles.at[self.s, x_at, y_at, c]
+            return ref.at[pl.ds(self.lo, 8)] if part is None else ref.at[pl.ds(self.lo + 4 * part, 4)]
+
+        def send(self, u, v, part, to_u, to_v):
+            x_to, y_to = (to_u, to_v) if self.s == 0 else (to_v, to_u)
+            ref = self.bundle(u, v, part)
+            copy = remote(
+                ref, ref, s_send.at[self.used], s_recv.at[self.used], x_to,
+                tile_of(z, y_to, c),
+            )
+            copy.start()
+            self.used += 1
+            self.pending.append(copy)
+            return copy
+
+        def first(self):
+            u, v = self.u, self.v
+            self.to_next = self.send(u, v, None, wrap(u + 1, 4), v)
+            self.to_prev = self.send(u, v, None, wrap(u - 1, 4), v)
+            self.second = [self.spread(u)]
+
+        def spread(self, u_of):
+            u, v = self.u, self.v
+            to_next = self.send(u_of, v, None, u, wrap(v + 1, 4))
+            to_prev = self.send(u_of, v, None, u, wrap(v - 1, 4))
+            return u_of, to_next, to_prev
+
+        def forward(self):
+            u, v = self.u, self.v
+            self.to_next.wait_recv()
+            prev_u, next_u = wrap(u - 1, 4), wrap(u + 1, 4)
+            self.far_next = self.send(prev_u, v, 0, next_u, v)
+            self.second.append(self.spread(prev_u))
+            self.to_prev.wait_recv()
+            self.far_prev = self.send(next_u, v, 1, prev_u, v)
+            self.second.append(self.spread(next_u))
+
+        def far(self):
+            self.far_next.wait_recv()
+            self.far_prev.wait_recv()
+            self.second.append(self.spread(wrap(self.u + 2, 4)))
+
+        def finish(self, number):
+            u, v = self.u, self.v
+            u_of, to_next, to_prev = self.second[number]
+            to_next.wait_recv()
+            a = self.send(u_of, wrap(v - 1, 4), 0, u, wrap(v + 1, 4))
+            to_prev.wait_recv()
+            d = self.send(u_of, wrap(v + 1, 4), 1, u, wrap(v - 1, 4))
+            return u_of, a, d
+
+        def last(self, state):
+            u_of, a, d = state
+            a.wait_recv()
+            d.wait_recv()
+            zs = pl.ds(self.lo, 8)
+            ref = tiles.at[0, u_of, :, c, zs] if self.s == 0 else tiles.at[1, :, u_of, c, zs]
+            copy = remote(
+                ref, ref, s_send.at[self.used], s_recv.at[self.used], b, tile_of(z, y, 1 - c)
+            )
+            copy.start()
+            self.used += 1
+            self.pending.append(copy)
+            self.across.append(copy)
+
+        def arrived(self):
+            for copy in self.across:
+                copy.wait_recv()
+
+    near, far = [Half(0, 0), Half(1, 0)], [Half(0, 8), Half(1, 8)]
+    for half in near + far:
+        half.first()
+    for half in near + far:
+        half.forward()
+    for half in near + far:
+        half.far()
+
+    def finish(part, numbers):
+        return [(half, half.finish(number)) for number in numbers for half in part]
+
+    near_states = finish(near, range(4))
+    for half, state in near_states:
+        half.last(state)
+    far_states = finish(far, (0, 1))
+    for half in near:
+        half.arrived()
+    fill_e2_21()
+    far_states += finish(far, (2,))
+    fill_e2_31()
+    far_states += finish(far, (3,))
+    fill_e2_mid()
+    for half, state in far_states:
+        half.last(state)
+    fill_e1_10()
+    fill_e1_mid()
+    y2 = dot_nt(lhs(lanes_of(c2) + shifted(c2, 3, 2)), e2[:, 0:640])
+    y1 = dot_nt(lhs(lanes_of(c1) + shifted(c1, 5, 1)), e1[:, 0:512])
+    for half in far:
+        half.arrived()
+    fill_up()
+    fill_e3()
+
     up = jnp.concatenate([block_sums(c0, 8, 8), block_sums(c1, 4, 4), block_sums(c2, 2, 2)], axis=1)
     emit(o4, 1, own(c3, 1) + dot_nt(up, u3[...]))
 
@@ -540,12 +556,12 @@
     emit(o3, 2, own(c2, 2) + dot_nt(up, u2[...]) + down)
 
     section(sg2, y3, 1, lambda l: k2a[l] + k2b[l])
-    y2 = dot_nt(lhs(lanes_of(c2) + lanes_of(sg2) + shifted(c2, 3, 2) + shifted(sg2, 3, 2)), e2[...])
+    y2 = y2 + dot_nt(lhs(lanes_of(sg2) + shifted(sg2, 3, 2)), e2[:, 640:1280])
     down = jnp.concatenate(upsampled(y2, 0, 0) + upsampled(y2, 1, 0), axis=0)
     emit(o2, 4, own(c1, 4) + dot_nt(block_sums(c0, 8, 2), u1[...]) + down)
 
     section(sg1, y2, 2, lambda l: k1[l])
-    y1 = dot_nt(lhs(lanes_of(c1) + lanes_of(sg1) + shifted(c1, 5, 1) + shifted(sg1, 5, 1)), e1[...])
+    y1 = y1 + dot_nt(lhs(lanes_of(sg1) + shifted(sg1, 5, 1)), e1[:, 512:1024])
     rows = []
     for p in range(4):
         rows.extend(upsampled(y1, p, 0))
@@ -559,12 +575,8 @@
 
 
 def finish_kernel(*refs):
-    sems = refs[8]
-    copies = [pltpu.make_async_copy(refs[n], refs[4 + n], sems.at[n]) for n in range(4)]
-    for copy in copies:
-        copy.start()
-    for copy in copies:
-        copy.wait()
+    for n in range(4):
+        refs[4 + n][...] = refs[n][...]
 
 
 ANY = pl.BlockSpec(memory_space=pl.ANY)
@@ -601,7 +613,7 @@
             pltpu.VMEM((2, 1024, 128), F32),
             cells(64), cells(48), cells(32), cells(32), cells(48), cells(32),
             cells(32), cells(32), cells(16), cells(16), cells(48), cells(32), cells(32), cells(48), cells(64),
-            sems(13), sems(5), sems(5), sems(NZ - 1), sems(NZ - 1), sems(144), sems(144),
+            sems(13), sems(5), sems(5), sems(NZ - 1), sems(NZ - 1), sems(96), sems(96),
         ],
         compiler_params=pltpu.CompilerParams(
             collective_id=0, has_side_effects=True, vmem_limit_bytes=60 * 2**20
@@ -611,9 +623,8 @@
     return pl.pallas_call(
         finish_kernel,
         out_shape=results,
-        in_specs=[ANY] * 4,
-        out_specs=[ANY] * 4,
-        scratch_shapes=[sems(4)],
+        in_specs=[VMEM] * 4,
+        out_specs=[VMEM] * 4,
         compiler_params=pltpu.CompilerParams(vmem_limit_bytes=60 * 2**20),
         name="finish",
     )(*done)

time: 64.8 us -> 64.3 us (level)
    pallas_call x1, Pallas kernels: 4.12 us -> 1.46 us  [per_device(): pl.pallas_call(finish_kernel, out_shape=results, in_specs=[VMEM] * 4, out...]
    pallas_call x1, Pallas kernels: 58.5 us -> 60.6 us  [per_device(): pl.pallas_call(exchange_kernel, out_shape=results, in_specs=[ANY] * 13, o...]
where the time goes in v3:
time: 64.3 us; the launch traced here: 64 us
  Pallas kernels  62 us (96%)
  local copies, waits for them, and re-layouts  1.36 us (2%)
    pallas_call x1, Pallas kernels, per_device(): pl.pallas_call(exchange_kernel, out_shape=results, in_specs=[ANY] * 13, o...  60.6 us
    pallas_call x1, Pallas kernels, per_device(): pl.pallas_call(finish_kernel, out_shape=results, in_specs=[VMEM] * 4, out...  1.46 us
    reshape x1, local copies, waits for them, and re-layouts, per_device(): jnp.pad(operands[12], (0, RAW_ROWS * 128 - SHARD)).reshape(RAW_ROWS, 128)  1.36 us

profile of v3, /device:TPU:1, one launch (start us, length us, event | category | flops | bytes accessed | tf_op | source)
XLA Modules:
  0.0 64.0 jit_solution(6824521633510235177)
XLA Ops:
  0.6 1.4 %pad_bitcast_fusion.refs_12_ = bf16[112,128]{1,0:T(8,128)(2,1)} fusion(bf16[13734]{0:T(1024)(128)(2,1)} %param.25), kind=kLoop, calls=%fused_computation | loop fusion | bytes 56140 | tf_op jit(solution)/shard_map/reshape | solution.py:589
  2.0 60.6 %exchange.1 = (bf16[8,3072]{1,0:T(8,128)(2,1)}, bf16[4,3072]{1,0:T(4,128)(2,1)}, bf16[2,3072]{1,0:T(2,128)(2,1)}, bf16[1,3072]{1,0:T(2,128)(2,1)}) custom-call(bf16[8,3072]{1,0:T(8,128)(2,1)} %refs_0_.1, bf16[4,3072]{1,0:T(4,128)(2,1)} %refs_1_.1, bf16[2,3072]{1,0:T(2,128)(2,1)} %refs_2_.1, bf16[1,3072]{1,0:T(2,128)(2,1)} %refs_3_.1, ...), custom_call_target="tpu_custom_call" | custom-call | tf_op jit(solution)/shard_map/exchange/pallas_call | solution.py:601
  62.6 1.5 %finish.1 = (bf16[8,3072]{1,0:T(8,128)(2,1)}, bf16[4,3072]{1,0:T(4,128)(2,1)}, bf16[2,3072]{1,0:T(2,128)(2,1)}, bf16[1,3072]{1,0:T(2,128)(2,1)}) custom-call(bf16[8,3072]{1,0:T(8,128)(2,1)} %get-tuple-element.8.refs_0_, bf16[4,3072]{1,0:T(4,128)(2,1)} %get-tuple-element.9.refs_1_, bf16[2,3072]{1,0:T(2,128)(2,1)} %get-tuple-element.10.refs_2_, ...), custom_call_target="tpu_custom_call" | custom-call | tf_op jit(solution)/shard_map/finish/pallas_call | solution.py:623

commit v4 on v3

--- a/solution.py
+++ b/solution.py
@@ -11,6 +11,7 @@
 N_TILE = 128
 N_BRANCH = 4
 NZ = 16
+Z_PARTS = ((0, 5), (5, 11))
 SHARD = 13734
 CELL = 384
 RAW_ROWS = 112
@@ -37,6 +38,14 @@
 }
 
 
+SPLITS = {(48, 0): 0, (48, 48): 1024, (48, 64): 2048, (96, 0): 3072, (192, 0): 3584}
+PLACES = (
+    [(48, 4 + q, 5 + q) for q in range(2)] + [(48, 0, 8), (48, 0, 4), (48, 4, 8)]
+    + [(48, 2 * q, 2 * q + 2) for q in range(4)] + [(96, q, q + 1) for q in range(4)]
+    + [(96, 0, 4), (96, 0, 2), (96, 2, 4), (192, 0, 1), (192, 1, 2), (192, 0, 2)]
+)
+
+
 def remote(src, dst, send, recv, branch, tile):
     return pltpu.make_async_remote_copy(
         src_ref=src, dst_ref=dst, send_sem=send, recv_sem=recv, device_id=(branch, tile), device_id_type=MESH
@@ -47,7 +56,11 @@
     group, n = row_tile // 9, 3 * (row_tile % 9) + jb
     j, slot = n // 7, n % 7
     k = 4 * group + j
-    return slot % 2, slot // 2, (k // 2) % 4, k % 2, k // 8
+    return k // 8, (slot % 2, slot // 2, (k // 2) % 4, k % 2)
+
+
+def place_of(distance):
+    return 2 * distance - 1 if distance > 0 else -2 * distance
 
 
 def dot(a, b):
@@ -71,7 +84,7 @@
     loaded, refs = refs[:13], refs[13:]
     (
         tiles, row_in, col_in, corner_in, raw1, raw2, win, row_f, col_f, row_out, col_out,
-        e3, e2, e1, u3, u2, u1, wide,
+        e3, e2, e1, u3, u2, u1, wide, splits, copies_of,
         c0, c1, c2, c3, sg1, sg2, q20, q30a, q30b, q31, k1, k2a, k2b, nxt, out,
         l_sem, h_send, h_recv, z_send, z_recv, s_send, s_recv,
     ) = refs
@@ -96,12 +109,11 @@
     left, right = wrap(b - 1, N_BRANCH), wrap(b + 1, N_BRANCH)
     up1, up2 = wrap(k - 1, N_TILE), wrap(k - 2, N_TILE)
     down1, down2 = wrap(k + 1, N_TILE), wrap(k + 2, N_TILE)
-    y_prev, y_next = wrap(y - 1, 4), wrap(y + 1, 4)
 
     partners = [
         (b, up1), (b, up2), (b, down1), (b, down2), (left, k), (right, k), (left, up1), (right, down1),
-        (b, tile_of(z, y_prev, c)), (b, tile_of(z, y_next, c)), (b, tile_of(z, y, 1 - c)),
-    ]
+        (b, tile_of(z, y, 1 - c)), (wrap(b + 2, 4), k),
+    ] + [(b, tile_of(z, wrap(y + d, 4), c)) for d in (1, 2, 3)]
     barrier = pltpu.get_barrier_semaphore()
     for step in range(1, NZ):
         pl.semaphore_signal(
@@ -146,6 +158,23 @@
     for copy in first:
         copy.start()
 
+    for (j, at), lanes in SPLITS.items():
+        width = 256 if j == 192 else 128
+
+        def split_target(col):
+            part, lane = col // width, lax.rem(col, width) - at
+            return jnp.where((lane >= 0) & (lane < j), part * j + lane, -1)
+
+        splits[:, lanes : lanes + CELL // j * width] = unit_matrix(CELL, CELL // j * width, split_target)
+    for number, (j, low, high) in enumerate(PLACES):
+
+        def place_target(col):
+            which = col // j
+            return jnp.where((which >= low) & (which < high), lax.rem(col, j), -1)
+
+        rows = 256 if j == 192 else 128
+        copies_of[0:rows, CELL * number : CELL * (number + 1)] = unit_matrix(rows, CELL, place_target)
+
     def put(buffer, row, value):
         rows = value.shape[0]
         for l in range(3):
@@ -187,16 +216,16 @@
         row_tile = 9 * group + n // 3
         offset = jnp.where(row_tile >= 124, 2, 10)
         origin = BASE + 3 * (16 * (n // 3 - first_tile) + offset) + lax.rem(n, 3)
-        tiles[s, b, y, c, z] = win[pl.ds(origin, 16, stride=3), :].astype(BF)
-
-    copies = []
-    own = tiles.at[:, b, y, c, z]
-    for step in (8, 7, 9, 6, 10, 5, 11, 4, 12, 3, 13, 2, 14, 1, 15):
-        copy = remote(
-            own, own, z_send.at[step - 1], z_recv.at[step - 1], b, tile_of(wrap(z + step, NZ), y, c)
+        tiles[s, b, y, c, 0] = win[pl.ds(origin, 16, stride=3), :].astype(BF)
+
+    copies = {}
+    for step in (1, 15, 2, 14, 3, 13, 4, 12, 5, 11, 6, 10, 7, 9, 8):
+        at = place_of(-step if step <= 7 else NZ - step)
+        copies[at] = remote(
+            tiles.at[:, b, y, c, 0], tiles.at[:, b, y, c, at], z_send.at[at - 1], z_recv.at[at - 1],
+            b, tile_of(wrap(z + step, NZ), y, c),
         )
-        copy.start()
-        copies.append(copy)
+        copies[at].start()
 
     for copy in first[2:]:
         copy.wait_recv()
@@ -253,9 +282,16 @@
     keep(k2a, dot(flags(q31), unit_matrix(CELL, 768, target31)), 2, 12, 12, 3, 24)
     keep(k2b, dot(flags(q30b), unit_matrix(CELL, 1536, target30b)), 4, 6, 6, 3, 24)
 
+    distances = [lax.rem(zz - z + 23, NZ) - 7 for zz in range(NZ)]
+    places = [jnp.where(d > 0, 2 * d - 1, -2 * d) for d in distances]
+
+    def tile(row_tile, jb):
+        zz, (s, x_at, y_at, c_at) = tile_at(row_tile, jb)
+        return tiles[s, x_at, y_at, c_at, places[zz]]
+
     def load_rows(row_tile, count):
         columns = [
-            jnp.concatenate([tiles[tile_at(row_tile + t, jb)] for t in range(count)], axis=0) for jb in range(3)
+            jnp.concatenate([tile(row_tile + t, jb) for t in range(count)], axis=0) for jb in range(3)
         ]
         return jnp.concatenate(columns, axis=1)
 
@@ -266,11 +302,8 @@
         count = -(-(offset + rows) // 16)
         width = 256 if j == 192 else 128
 
-        def target(col):
-            part, lane = col // width, lax.rem(col, width) - at
-            return jnp.where((lane >= 0) & (lane < j), part * j + lane, -1)
-
-        split = dot(load_rows(row_tile, count), unit_matrix(CELL, n * width, target))
+        lanes = SPLITS[j, at]
+        split = dot(load_rows(row_tile, count), splits[:, lanes : lanes + n * width])
         parts = []
         for half in range(width // 128):
             for part in range(n):
@@ -281,13 +314,8 @@
         return parts[0] if len(parts) == 1 else jnp.concatenate(parts, axis=1)
 
     def place(weights, j, low, high):
-        rows = weights.shape[1]
-
-        def target(col):
-            which = col // j
-            return jnp.where((which >= low) & (which < high), lax.rem(col, j), -1)
-
-        return dot(weights, unit_matrix(rows, CELL, target))
+        lanes = CELL * PLACES.index((j, low, high))
+        return dot(weights, copies_of[0 : weights.shape[1], lanes : lanes + CELL])
 
     def taps(e, row0, pitch, weights, placed, seg, nxt_seg, nxt_width):
         count = len(placed)
@@ -323,9 +351,9 @@
                     first = start + (3 * a + bb) * (i // 16)
                     for t in range(i // 16):
                         for jb in range(3):
-                            e3[at + 16 * t : at + 16 * (t + 1), seg + 128 * jb : seg + 128 * (jb + 1)] = tiles[
-                                tile_at(first + t, jb)
-                            ]
+                            e3[at + 16 * t : at + 16 * (t + 1), seg + 128 * jb : seg + 128 * (jb + 1)] = tile(
+                                first + t, jb
+                            )
 
     def fill_e2_21():
         w = rows_of((2, 1, 0), 432, 192)
@@ -433,117 +461,71 @@
     def own(buffer, rows):
         return jnp.concatenate([buffer[l, 0 : 8 * rows, :] for l in range(3)], axis=1)
 
-    for copy in copies:
-        copy.wait_recv()
-
-    class Half:
-        def __init__(self, s, lo):
-            self.s, self.lo = s, lo
+    class Part:
+        def __init__(self, s, lo, size, sem):
+            self.s, self.lo, self.size, self.used = s, lo, size, sem
             self.u, self.v = (b, y) if s == 0 else (y, b)
-            self.pending, self.across = [], []
-            self.used = 24 * (2 * s + lo // 8)
-
-        def bundle(self, u, v, part):
-            x_at, y_at = (u, v) if self.s == 0 else (v, u)
-            ref = tiles.at[self.s, x_at, y_at, c]
-            return ref.at[pl.ds(self.lo, 8)] if part is None else ref.at[pl.ds(self.lo + 4 * part, 4)]
-
-        def send(self, u, v, part, to_u, to_v):
-            x_to, y_to = (to_u, to_v) if self.s == 0 else (to_v, to_u)
-            ref = self.bundle(u, v, part)
-            copy = remote(
-                ref, ref, s_send.at[self.used], s_recv.at[self.used], x_to,
-                tile_of(z, y_to, c),
-            )
+            self.pending, self.second = [], []
+
+        def send(self, ref, x_to, tile_to):
+            copy = remote(ref, ref, s_send.at[self.used], s_recv.at[self.used], x_to, tile_to)
             copy.start()
             self.used += 1
             self.pending.append(copy)
             return copy
 
-        def first(self):
-            u, v = self.u, self.v
-            self.to_next = self.send(u, v, None, wrap(u + 1, 4), v)
-            self.to_prev = self.send(u, v, None, wrap(u - 1, 4), v)
-            self.second = [self.spread(u)]
+        def send_bundle(self, u_of, to_u, to_v):
+            zs = pl.ds(self.lo, self.size)
+            if self.s == 0:
+                return self.send(tiles.at[0, u_of, y, c, zs], to_u, tile_of(z, to_v, c))
+            return self.send(tiles.at[1, b, u_of, c, zs], to_v, tile_of(z, to_u, c))
 
         def spread(self, u_of):
-            u, v = self.u, self.v
-            to_next = self.send(u_of, v, None, u, wrap(v + 1, 4))
-            to_prev = self.send(u_of, v, None, u, wrap(v - 1, 4))
-            return u_of, to_next, to_prev
-
-        def forward(self):
-            u, v = self.u, self.v
-            self.to_next.wait_recv()
-            prev_u, next_u = wrap(u - 1, 4), wrap(u + 1, 4)
-            self.far_next = self.send(prev_u, v, 0, next_u, v)
-            self.second.append(self.spread(prev_u))
-            self.to_prev.wait_recv()
-            self.far_prev = self.send(next_u, v, 1, prev_u, v)
-            self.second.append(self.spread(next_u))
-
-        def far(self):
-            self.far_next.wait_recv()
-            self.far_prev.wait_recv()
-            self.second.append(self.spread(wrap(self.u + 2, 4)))
-
-        def finish(self, number):
-            u, v = self.u, self.v
-            u_of, to_next, to_prev = self.second[number]
-            to_next.wait_recv()
-            a = self.send(u_of, wrap(v - 1, 4), 0, u, wrap(v + 1, 4))
-            to_prev.wait_recv()
-            d = self.send(u_of, wrap(v + 1, 4), 1, u, wrap(v - 1, 4))
-            return u_of, a, d
-
-        def last(self, state):
-            u_of, a, d = state
-            a.wait_recv()
-            d.wait_recv()
-            zs = pl.ds(self.lo, 8)
-            ref = tiles.at[0, u_of, :, c, zs] if self.s == 0 else tiles.at[1, :, u_of, c, zs]
-            copy = remote(
-                ref, ref, s_send.at[self.used], s_recv.at[self.used], b, tile_of(z, y, 1 - c)
-            )
-            copy.start()
-            self.used += 1
-            self.pending.append(copy)
-            self.across.append(copy)
+            self.second.append((u_of, [self.send_bundle(u_of, self.u, wrap(self.v + d, 4)) for d in (1, 3, 2)]))
+
+        def start(self):
+            self.first = [(d, self.send_bundle(self.u, wrap(self.u + d, 4), self.v)) for d in (1, 3, 2)]
+            self.spread(self.u)
+
+        def pass_on(self):
+            for d, copy in self.first:
+                copy.wait_recv()
+                self.spread(wrap(self.u - d, 4))
+
+        def cross(self):
+            zs = pl.ds(self.lo, self.size)
+            self.across = []
+            for u_of, copies_in in self.second:
+                for copy in copies_in:
+                    copy.wait_recv()
+                ref = tiles.at[0, u_of, :, c, zs] if self.s == 0 else tiles.at[1, :, u_of, c, zs]
+                self.across.append(self.send(ref, b, tile_of(z, y, 1 - c)))
 
         def arrived(self):
             for copy in self.across:
                 copy.wait_recv()
 
-    near, far = [Half(0, 0), Half(1, 0)], [Half(0, 8), Half(1, 8)]
-    for half in near + far:
-        half.first()
-    for half in near + far:
-        half.forward()
-    for half in near + far:
-        half.far()
-
-    def finish(part, numbers):
-        return [(half, half.finish(number)) for number in numbers for half in part]
-
-    near_states = finish(near, range(4))
-    for half, state in near_states:
-        half.last(state)
-    far_states = finish(far, (0, 1))
-    for half in near:
-        half.arrived()
+    parts = []
+    for lo, size in Z_PARTS:
+        for at in range(max(lo, 1), lo + size):
+            copies[at].wait_recv()
+        pair = [Part(s, lo, size, 19 * (len(parts) + s)) for s in range(2)]
+        for part in pair:
+            part.start()
+        for part in pair:
+            part.pass_on()
+        parts += pair
+    for part in parts:
+        part.cross()
+    for part in parts:
+        part.arrived()
     fill_e2_21()
-    far_states += finish(far, (2,))
     fill_e2_31()
-    far_states += finish(far, (3,))
     fill_e2_mid()
-    for half, state in far_states:
-        half.last(state)
     fill_e1_10()
     fill_e1_mid()
     y2 = dot_nt(lhs(lanes_of(c2) + shifted(c2, 3, 2)), e2[:, 0:640])
     y1 = dot_nt(lhs(lanes_of(c1) + shifted(c1, 5, 1)), e1[:, 0:512])
-    for half in far:
-        half.arrived()
     fill_up()
     fill_e3()
 
@@ -567,10 +549,10 @@
         rows.extend(upsampled(y1, p, 0))
     emit(o1, 8, own(c0, 8) + jnp.concatenate(rows, axis=0))
 
-    for half in near + far:
-        for copy in half.pending:
+    for part in parts:
+        for copy in part.pending:
             copy.wait_send()
-    for copy in copies + first:
+    for copy in list(copies.values()) + first:
         copy.wait_send()
 
 
@@ -610,10 +592,10 @@
             pltpu.VMEM((48, CELL), F32), pltpu.VMEM((32, CELL), F32), buffer(48, CELL), buffer(32, CELL),
             buffer(2304, 768), buffer(2304, 1280), buffer(1152, 1024),
             buffer(384, 1152), buffer(384, 768), buffer(384, 384),
-            pltpu.VMEM((2, 1024, 128), F32),
+            pltpu.VMEM((2, 1024, 128), F32), buffer(CELL, 4096), buffer(256, CELL * len(PLACES)),
             cells(64), cells(48), cells(32), cells(32), cells(48), cells(32),
             cells(32), cells(32), cells(16), cells(16), cells(48), cells(32), cells(32), cells(48), cells(64),
-            sems(13), sems(5), sems(5), sems(NZ - 1), sems(NZ - 1), sems(96), sems(96),
+            sems(13), sems(5), sems(5), sems(NZ - 1), sems(NZ - 1), sems(38 * len(Z_PARTS)), sems(38 * len(Z_PARTS)),
         ],
         compiler_params=pltpu.CompilerParams(
             collective_id=0, has_side_effects=True, vmem_limit_bytes=60 * 2**20

time: 64.3 us -> 61.3 us (0.953)
  Pallas kernels: 62 us -> 59.1 us
    pallas_call x1, Pallas kernels: 60.6 us -> 57.6 us  [per_device(): pl.pallas_call(exchange_kernel, out_shape=results, in_specs=[ANY] * 13, o...]
where the time goes in v4:
time: 61.3 us; the launch traced here: 61.1 us
  Pallas kernels  59.1 us (96%)
  local copies, waits for them, and re-layouts  1.36 us (2%)
  between operations  0.64 us (1%)
    pallas_call x1, Pallas kernels, per_device(): pl.pallas_call(exchange_kernel, out_shape=results, in_specs=[ANY] * 13, o...  57.6 us
    pallas_call x1, Pallas kernels, per_device(): pl.pallas_call(finish_kernel, out_shape=results, in_specs=[VMEM] * 4, out...  1.46 us
    reshape x1, local copies, waits for them, and re-layouts, per_device(): jnp.pad(operands[12], (0, RAW_ROWS * 128 - SHARD)).reshape(RAW_ROWS, 128)  1.36 us

profile of v4, /device:TPU:1, one launch (start us, length us, event | category | flops | bytes accessed | tf_op | source)
XLA Modules:
  0.0 61.1 jit_solution(17149628647275289531)
XLA Ops:
  0.6 1.4 %pad_bitcast_fusion.refs_12_ = bf16[112,128]{1,0:T(8,128)(2,1)} fusion(bf16[13734]{0:T(1024)(128)(2,1)} %param.25), kind=kLoop, calls=%fused_computation | loop fusion | bytes 56140 | tf_op jit(solution)/shard_map/reshape | solution.py:571
  2.0 57.6 %exchange.1 = (bf16[8,3072]{1,0:T(8,128)(2,1)}, bf16[4,3072]{1,0:T(4,128)(2,1)}, bf16[2,3072]{1,0:T(2,128)(2,1)}, bf16[1,3072]{1,0:T(2,128)(2,1)}) custom-call(bf16[8,3072]{1,0:T(8,128)(2,1)} %refs_0_.1, bf16[4,3072]{1,0:T(4,128)(2,1)} %refs_1_.1, bf16[2,3072]{1,0:T(2,128)(2,1)} %refs_2_.1, bf16[1,3072]{1,0:T(2,128)(2,1)} %refs_3_.1, ...), custom_call_target="tpu_custom_call" | custom-call | tf_op jit(solution)/shard_map/exchange/pallas_call | solution.py:583
  59.6 1.5 %finish.1 = (bf16[8,3072]{1,0:T(8,128)(2,1)}, bf16[4,3072]{1,0:T(4,128)(2,1)}, bf16[2,3072]{1,0:T(2,128)(2,1)}, bf16[1,3072]{1,0:T(2,128)(2,1)}) custom-call(bf16[8,3072]{1,0:T(8,128)(2,1)} %get-tuple-element.8.refs_0_, bf16[4,3072]{1,0:T(4,128)(2,1)} %get-tuple-element.9.refs_1_, bf16[2,3072]{1,0:T(2,128)(2,1)} %get-tuple-element.10.refs_2_, ...), custom_call_target="tpu_custom_call" | custom-call | tf_op jit(solution)/shard_map/finish/pallas_call | solution.py:605

commit v5 on v4

--- a/solution.py
+++ b/solution.py
@@ -17,6 +17,8 @@
 RAW_ROWS = 112
 BASE = 104
 WINDOW = 464
+
+C1, C2, C3, SUMS, K1, K2, STRIP = 0, 48, 80, 112, 200, 248, 280
 
 ROW0 = {
     (0, 1, 0): 0,
@@ -56,7 +58,7 @@
     group, n = row_tile // 9, 3 * (row_tile % 9) + jb
     j, slot = n // 7, n % 7
     k = 4 * group + j
-    return k // 8, (slot % 2, slot // 2, (k // 2) % 4, k % 2)
+    return k // 8, (slot % 2 if slot < 6 else k % 2, slot // 2, (k // 2) % 4, k % 2)
 
 
 def place_of(distance):
@@ -83,12 +85,12 @@
     inputs, outputs, refs = refs[:13], refs[13:17], refs[17:]
     loaded, refs = refs[:13], refs[13:]
     (
-        tiles, row_in, col_in, corner_in, raw1, raw2, win, row_f, col_f, row_out, col_out,
+        tiles, row_in, col_in, corner_in, raw, raw1, raw2, shard_f, win, row_f, col_f, row_out, col_out,
         e3, e2, e1, u3, u2, u1, wide, splits, copies_of,
-        c0, c1, c2, c3, sg1, sg2, q20, q30a, q30b, q31, k1, k2a, k2b, nxt, out,
-        l_sem, h_send, h_recv, z_send, z_recv, s_send, s_recv,
+        c0, c1, c2, c3, sg1, sg2, q20, q30a, q30b, q31, k1, k2a, k2b, nxt, out, strip, acc, acc_in,
+        l_sem, h_send, h_recv, z_send, z_recv, s_send, s_recv, x_send, x_recv,
     ) = refs
-    g1, g2, g3, g4, p1, p2, p3, p4, m20, m30a, m30b, m31, raw = loaded
+    g1, g2, g3, g4, p1, p2, p3, p4, m20, m30a, m30b, m31, shard_in = loaded
     o1, o2, o3, o4 = outputs
     b = lax.axis_index("branch")
     k = lax.axis_index("tile")
@@ -122,10 +124,29 @@
     for who in partners:
         pl.semaphore_signal(barrier, inc=1, device_id=who, device_id_type=MESH)
 
-    for ref in (e3, e2, e1, c1, c2, c3, sg1, sg2, q20, q30a, q30b, q31, k1, k2a, k2b, nxt, win):
-        ref[...] = jnp.zeros_like(ref)
-
-    for load in loads:
+    win[...] = jnp.zeros_like(win)
+    loads[12].wait()
+    whole = SHARD // 1024 * 1024
+    rest = SHARD // 128 * 128
+    row_at = [n // 128 for n in (whole, rest)]
+    shard_f[0 : row_at[0], :] = shard_in[0:whole].astype(F32).reshape(row_at[0], 128)
+    shard_f[row_at[0] : row_at[1], :] = shard_in[whole:rest].astype(F32).reshape(row_at[1] - row_at[0], 128)
+    shard_f[row_at[1] : RAW_ROWS, :] = jnp.zeros((RAW_ROWS - row_at[1], 128), F32)
+    shard_f[row_at[1] : row_at[1] + 1, 0 : SHARD - rest] = shard_in[rest:SHARD].astype(F32).reshape(1, SHARD - rest)
+    raw[...] = shard_f[...].astype(BF)
+
+    pl.semaphore_wait(barrier, len(partners) + NZ - 1)
+    first = [
+        remote(raw, raw1, h_send.at[0], h_recv.at[0], b, up1),
+        remote(raw, raw2, h_send.at[1], h_recv.at[1], b, up2),
+        remote(row_out, row_in, h_send.at[2], h_recv.at[2], b, up1),
+        remote(col_out, col_in, h_send.at[3], h_recv.at[3], left, k),
+        remote(col_out, corner_in, h_send.at[4], h_recv.at[4], left, up1),
+    ]
+    for copy in first[:2]:
+        copy.start()
+
+    for load in loads[:12]:
         load.wait()
     row_f[...] = jnp.zeros_like(row_f)
     col_f[...] = jnp.zeros_like(col_f)
@@ -146,58 +167,8 @@
     row_out[...] = row_f[...].astype(BF)
     col_out[...] = col_f[...].astype(BF)
 
-
-    pl.semaphore_wait(barrier, len(partners) + NZ - 1)
-    first = [
-        remote(raw, raw1, h_send.at[0], h_recv.at[0], b, up1),
-        remote(raw, raw2, h_send.at[1], h_recv.at[1], b, up2),
-        remote(row_out, row_in, h_send.at[2], h_recv.at[2], b, up1),
-        remote(col_out, col_in, h_send.at[3], h_recv.at[3], left, k),
-        remote(col_out, corner_in, h_send.at[4], h_recv.at[4], left, up1),
-    ]
-    for copy in first:
+    for copy in first[2:]:
         copy.start()
-
-    for (j, at), lanes in SPLITS.items():
-        width = 256 if j == 192 else 128
-
-        def split_target(col):
-            part, lane = col // width, lax.rem(col, width) - at
-            return jnp.where((lane >= 0) & (lane < j), part * j + lane, -1)
-
-        splits[:, lanes : lanes + CELL // j * width] = unit_matrix(CELL, CELL // j * width, split_target)
-    for number, (j, low, high) in enumerate(PLACES):
-
-        def place_target(col):
-            which = col // j
-            return jnp.where((which >= low) & (which < high), lax.rem(col, j), -1)
-
-        rows = 256 if j == 192 else 128
-        copies_of[0:rows, CELL * number : CELL * (number + 1)] = unit_matrix(rows, CELL, place_target)
-
-    def put(buffer, row, value):
-        rows = value.shape[0]
-        for l in range(3):
-            buffer[l, row : row + rows, :] = value[:, 128 * l : 128 * (l + 1)]
-
-    def spread_units(buffer, value, units):
-        rows = value.shape[0]
-        for unit in range(units):
-            for l in range(3):
-                piece = value[:, CELL * unit + 128 * l : CELL * unit + 128 * (l + 1)]
-                if rows == 1:
-                    buffer[l, unit : unit + 1, :] = piece
-                else:
-                    buffer[l, pl.ds(unit, rows, stride=units), :] = piece
-
-    def masked(g, p):
-        return jnp.where(p[...].astype(F32) > 0, g[...].astype(F32), 0.0)
-
-    spread_units(c0, masked(g1, p1), 8)
-    for buffer, g, p in ((c1, g2, p2), (c2, g3, p3), (c3, g4, p4)):
-        spread_units(buffer, masked(g, p), 8)
-    for buffer, m, units in ((q20, m20, 4), (q30a, m30a, 4), (q31, m31, 4), (q30b, m30b, 2)):
-        spread_units(buffer, m[...].astype(F32), units)
 
     group, j = k // 4, lax.rem(k, 4)
     first_tile = (7 * j) // 3
@@ -212,7 +183,7 @@
         win[pl.ds(q, RAW_ROWS), :] += jnp.where(lane >= phase, rolled, 0.0)
         win[pl.ds(q + 1, RAW_ROWS), :] += jnp.where(lane >= phase, 0.0, rolled)
     for s in range(2):
-        n = 7 * j + 2 * b + s
+        n = 7 * j + jnp.where(b == 3, 6, 2 * b + s)
         row_tile = 9 * group + n // 3
         offset = jnp.where(row_tile >= 124, 2, 10)
         origin = BASE + 3 * (16 * (n // 3 - first_tile) + offset) + lax.rem(n, 3)
@@ -227,24 +198,43 @@
         )
         copies[at].start()
 
-    for copy in first[2:]:
-        copy.wait_recv()
-    row_halo = row_in[...].astype(F32)
-    col_halo = col_in[...].astype(F32)
-    corner = corner_in[...].astype(F32)
-    row_zero = jnp.where(has_row, row_halo, 0.0)
-    col_zero = jnp.where(has_col, col_halo, 0.0)
-    corner_zero = jnp.where(has_row & has_col, corner, 0.0)
-    at = 0
-    for buffer, rows, halo in ((c1, 4, 0), (c2, 2, 8), (c3, 1, 16)):
-        put(buffer, 8 * rows, row_zero[halo : halo + 8])
-        put(buffer, 8 * rows + 8, col_zero[at : at + rows])
-        put(buffer, 8 * rows + 8 + rows, corner_zero[at : at + 1])
-        at += rows
-    for buffer, rows, units, halo, at in ((q20, 4, 4, 24, 8), (q30a, 4, 4, 28, 12), (q31, 2, 4, 32, 18), (q30b, 2, 2, 36, 16)):
-        put(buffer, rows * units, row_halo[halo : halo + units])
-        put(buffer, (rows + 1) * units, col_halo[at : at + rows])
-        put(buffer, (rows + 1) * units + rows, corner[at : at + 1])
+    for (j, at), lanes in SPLITS.items():
+        width = 256 if j == 192 else 128
+
+        def split_target(col):
+            part, lane = col // width, lax.rem(col, width) - at
+            return jnp.where((lane >= 0) & (lane < j), part * j + lane, -1)
+
+        splits[:, lanes : lanes + CELL // j * width] = unit_matrix(CELL, CELL // j * width, split_target)
+    for number, (j, low, high) in enumerate(PLACES):
+
+        def place_target(col):
+            which = col // j
+            return jnp.where((which >= low) & (which < high), lax.rem(col, j), -1)
+
+        rows = 256 if j == 192 else 128
+        copies_of[0:rows, CELL * number : CELL * (number + 1)] = unit_matrix(rows, CELL, place_target)
+
+    for ref in (e3, e2, e1, c1, c2, c3, sg1, sg2, q20, q30a, q30b, q31, k1, k2a, k2b, nxt, acc):
+        ref[...] = jnp.zeros_like(ref)
+
+    def put(buffer, row, value):
+        rows = value.shape[0]
+        for l in range(3):
+            buffer[l, row : row + rows, :] = value[:, 128 * l : 128 * (l + 1)]
+
+    def spread_units(buffer, value, units):
+        rows = value.shape[0]
+        for unit in range(units):
+            for l in range(3):
+                piece = value[:, CELL * unit + 128 * l : CELL * unit + 128 * (l + 1)]
+                if rows == 1:
+                    buffer[l, unit : unit + 1, :] = piece
+                else:
+                    buffer[l, pl.ds(unit, rows, stride=units), :] = piece
+
+    def masked(g, p):
+        return jnp.where(p[...].astype(F32) > 0, g[...].astype(F32), 0.0)
 
     def flags(buffer):
         whole = jnp.concatenate([buffer[l] for l in range(3)], axis=1)
@@ -275,12 +265,68 @@
                 extra_from : extra_from + extra_rows, 128 * l : 128 * (l + 1)
             ]
 
-    mask1 = dot(flags(q20), unit_matrix(CELL, 768, target20(0))) + dot(
-        flags(q30a), unit_matrix(CELL, 768, target20(48))
+    def block_sums(buffer, rows, factor):
+        groups = []
+        for first in range(0, rows, factor):
+            pieces = []
+            for l in range(3):
+                total = buffer[l, 8 * first : 8 * first + 8, :]
+                for p in range(first + 1, first + factor):
+                    total = total + buffer[l, 8 * p : 8 * p + 8, :]
+                pieces.append(total)
+            groups.append(jnp.concatenate(pieces, axis=1))
+        return jnp.concatenate(groups, axis=0).astype(BF)
+
+    def own_maps():
+        spread_units(c0, masked(g1, p1), 8)
+        for buffer, g, p in ((c1, g2, p2), (c2, g3, p3), (c3, g4, p4)):
+            spread_units(buffer, masked(g, p), 8)
+        for buffer, m, units in ((q20, m20, 4), (q30a, m30a, 4), (q31, m31, 4), (q30b, m30b, 2)):
+            spread_units(buffer, m[...].astype(F32), units)
+
+        for copy in first[2:]:
+            copy.wait_recv()
+        row_halo = row_in[...].astype(F32)
+        col_halo = col_in[...].astype(F32)
+        corner = corner_in[...].astype(F32)
+        row_zero = jnp.where(has_row, row_halo, 0.0)
+        col_zero = jnp.where(has_col, col_halo, 0.0)
+        corner_zero = jnp.where(has_row & has_col, corner, 0.0)
+        at = 0
+        for buffer, rows, halo in ((c1, 4, 0), (c2, 2, 8), (c3, 1, 16)):
+            put(buffer, 8 * rows, row_zero[halo : halo + 8])
+            put(buffer, 8 * rows + 8, col_zero[at : at + rows])
+            put(buffer, 8 * rows + 8 + rows, corner_zero[at : at + 1])
+            at += rows
+        for buffer, rows, units, halo, at in ((q20, 4, 4, 24, 8), (q30a, 4, 4, 28, 12), (q31, 2, 4, 32, 18), (q30b, 2, 2, 36, 16)):
+            put(buffer, rows * units, row_halo[halo : halo + units])
+            put(buffer, (rows + 1) * units, col_halo[at : at + rows])
+            put(buffer, (rows + 1) * units + rows, corner[at : at + 1])
+
+        mask1 = dot(flags(q20), unit_matrix(CELL, 768, target20(0))) + dot(
+            flags(q30a), unit_matrix(CELL, 768, target20(48))
+        )
+        keep(k1, mask1, 2, 20, 20, 5, 40)
+        keep(k2a, dot(flags(q31), unit_matrix(CELL, 768, target31)), 2, 12, 12, 3, 24)
+        keep(k2b, dot(flags(q30b), unit_matrix(CELL, 1536, target30b)), 4, 6, 6, 3, 24)
+        pooled = [block_sums(c0, 8, f) for f in (2, 4, 8)] + [block_sums(c1, 4, f) for f in (2, 4)] + [block_sums(c2, 2, 2)]
+        for l in range(3):
+            strip[0, l, C1 : C1 + 48, :] = c1[l]
+            strip[0, l, C2 : C2 + 32, :] = c2[l]
+            strip[0, l, C3 : C3 + 32, :] = c3[l]
+            strip[0, l, K1 : K1 + 48, :] = k1[l]
+            strip[0, l, K2 : K2 + 32, :] = k2a[l] + k2b[l]
+        row = SUMS
+        for value in pooled:
+            rows = value.shape[0]
+            for l in range(3):
+                strip[0, l, row : row + rows, :] = value[:, 128 * l : 128 * (l + 1)].astype(F32)
+            row += rows
+        strip_copy.start()
+
+    strip_copy = remote(
+        strip.at[0], strip.at[1], x_send.at[0], x_recv.at[0], b, tile_of(z, y, 1 - c)
     )
-    keep(k1, mask1, 2, 20, 20, 5, 40)
-    keep(k2a, dot(flags(q31), unit_matrix(CELL, 768, target31)), 2, 12, 12, 3, 24)
-    keep(k2b, dot(flags(q30b), unit_matrix(CELL, 1536, target30b)), 4, 6, 6, 3, 24)
 
     distances = [lax.rem(zz - z + 23, NZ) - 7 for zz in range(NZ)]
     places = [jnp.where(d > 0, 2 * d - 1, -2 * d) for d in distances]
@@ -336,12 +382,8 @@
                     e[odd : odd + i, nxt_seg : nxt_seg + nxt_width] = tap(weights, a, 0).astype(BF)
                 e[odd : odd + i, seg : seg + CELL] = value.astype(BF)
 
-    def fill_e3():
-        for key, i, row0, pitch in (
-            ((3, 2, 0), 192, 0, 192),
-            ((3, 1, 1), 96, 1152, 96),
-            ((3, 0, 2), 48, 1152 + 192, 48),
-        ):
+    def fill_e3(kernels):
+        for key, i, row0, pitch in kernels:
             r0 = ROW0[key]
             start = 124 + (r0 - 1986) // 16 if r0 >= 1986 else (r0 - 10) // 16
             for a in range(3):
@@ -394,16 +436,21 @@
         for q in range(4):
             u1[96 * q : 96 * (q + 1), :] = place(w01, 48, 2 * q, 2 * q + 2).astype(BF)
 
-    def lanes_of(buffer, count=3):
-        return [buffer[l] for l in range(count)]
-
-    def shifted(buffer, rows, count):
-        total = buffer.shape[1]
+    def reader(t, base):
+        return lambda l, lo, hi: strip[t, l, base + lo : base + hi, :]
+
+    def section_reader(buffer, t):
+        return lambda l, lo, hi: buffer[t, l, lo:hi, :]
+
+    def cells_of(read, total):
+        return [read(l, 0, total) for l in range(3)]
+
+    def shifted(read, rows, total, count):
         pieces = []
         for l in range(count):
-            nxt[l, 0 : 8 * rows, :] = buffer[l, 1 : 8 * rows + 1, :]
+            nxt[l, 0 : 8 * rows, :] = read(l, 1, 8 * rows + 1)
             for p in range(rows):
-                nxt[l, 8 * p + 7 : 8 * p + 8, :] = buffer[l, 8 * rows + p : 8 * rows + p + 1, :]
+                nxt[l, 8 * p + 7 : 8 * p + 8, :] = read(l, 8 * rows + p, 8 * rows + p + 1)
             nxt[l, 8 * rows : total, :] = jnp.zeros((total - 8 * rows, 128), F32)
             pieces.append(nxt[l, 0:total, :])
         return pieces
@@ -411,32 +458,118 @@
     def lhs(pieces):
         return jnp.concatenate([piece.astype(BF) for piece in pieces], axis=1)
 
-    def rows_out(y, a, lo, hi, lane0):
-        return y[lo:hi, lane0 + CELL * a : lane0 + CELL * (a + 1)]
-
-    def upsampled(y, p, lane0):
-        even = rows_out(y, 1, 8 * p, 8 * p + 8, lane0)
-        odd = rows_out(y, 2, 8 * p, 8 * p + 8, lane0) + rows_out(y, 0, 8 * p + 8, 8 * p + 16, lane0)
-        return even, odd
-
-    def section(buffer, y, rows, kept):
-        base = 8 * (rows + 1)
+    def both(make):
+        return jnp.concatenate([make(t) for t in range(2)], axis=0)
+
+    def level_three(t):
+        read = reader(t, C3)
+        return lhs(cells_of(read, 32) + shifted(read, 2, 32, 3))
+
+    def level_two(t):
+        read = reader(t, C2)
+        return lhs(cells_of(read, 32) + shifted(read, 3, 32, 2))
+
+    def level_one(t):
+        read = reader(t, C1)
+        return lhs(cells_of(read, 48) + shifted(read, 5, 48, 1))
+
+    def sums_of(t, *blocks):
+        pieces = []
+        for start, rows in blocks:
+            pieces += [strip[t, l, SUMS + start : SUMS + start + rows, :] for l in range(3)]
+        return lhs(pieces)
+
+    def rows_out(y, a, lo, hi):
+        return y[lo:hi, CELL * a : CELL * (a + 1)]
+
+    def upsampled(y, p, base):
+        lo = base + 8 * p
+        even = rows_out(y, 1, lo, lo + 8)
+        return even, rows_out(y, 2, lo, lo + 8) + rows_out(y, 0, lo + 8, lo + 16)
+
+    def section(buffer, t, y, rows, y_base, kept):
+        view = buffer.at[t]
         for p in range(rows):
-            even, odd = upsampled(y, p, 1152)
-            put(buffer, 16 * p, even)
-            put(buffer, 16 * p + 8, odd)
-        put(buffer, 16 * rows, rows_out(y, 1, 8 * rows, 8 * rows + 8, 1152))
-        extra = 8 * (2 * rows + 1)
+            even, odd = upsampled(y, p, y_base)
+            put(view, 16 * p, even)
+            put(view, 16 * p + 8, odd)
+        put(view, 16 * rows, rows_out(y, 1, y_base + 8 * rows, y_base + 8 * rows + 8))
+        extra, base = 8 * (2 * rows + 1), y_base + 8 * (rows + 1)
         for p in range(rows + 1):
-            put(buffer, extra + 2 * p, rows_out(y, 1, base + p, base + p + 1, 1152))
+            put(view, extra + 2 * p, rows_out(y, 1, base + p, base + p + 1))
             if p < rows:
-                odd = rows_out(y, 2, base + p, base + p + 1, 1152) + rows_out(y, 0, base + p + 1, base + p + 2, 1152)
-                put(buffer, extra + 2 * p + 1, odd)
+                odd = rows_out(y, 2, base + p, base + p + 1) + rows_out(y, 0, base + p + 1, base + p + 2)
+                put(view, extra + 2 * p + 1, odd)
         for l in range(3):
-            buffer[l] = jnp.where(kept(l) > 0.5, buffer[l], 0.0)
-
-    def emit(ref, rows, value):
-        put(out, 0, value)
+            buffer[t, l] = jnp.where(strip[t, l, kept : kept + buffer.shape[2], :] > 0.5, buffer[t, l], 0.0)
+
+    def direct():
+        fill_e2_21()
+        fill_e1_10()
+        fill_up()
+        fill_e3((((3, 2, 0), 192, 0, 192),))
+        y3 = dot_nt(both(level_three), e3[0:1152, :])
+        y2 = dot_nt(both(level_two), e2[0:1152, 0:640])
+        y1 = dot_nt(both(level_one), e1[:, 0:512])
+        x3 = dot_nt(both(lambda t: sums_of(t, (48, 8), (72, 8), (80, 8))), u3[...])
+        x2 = dot_nt(both(lambda t: sums_of(t, (32, 16), (56, 16))), u2[...])
+        x1 = dot_nt(both(lambda t: sums_of(t, (0, 32))), u1[...])
+        for t in (1, 0):
+            view = acc.at[t]
+            for p in range(4):
+                even, odd = upsampled(y1, p, 48 * t)
+                put(view, 16 * p, even)
+                put(view, 16 * p + 8, odd)
+            for p in range(2):
+                even, odd = upsampled(y2, p, 32 * t)
+                put(view, 64 + 16 * p, even + x1[32 * t + 16 * p : 32 * t + 16 * p + 8])
+                put(view, 72 + 16 * p, odd + x1[32 * t + 16 * p + 8 : 32 * t + 16 * p + 16])
+            even, odd = upsampled(y3, 0, 32 * t)
+            put(view, 96, even + x2[16 * t : 16 * t + 8])
+            put(view, 104, odd + x2[16 * t + 8 : 16 * t + 16])
+            put(view, 112, x3[8 * t : 8 * t + 8])
+
+    def chained():
+        fill_e2_31()
+        fill_e2_mid()
+        fill_e1_mid()
+        fill_e3((((3, 1, 1), 96, 1152, 96), ((3, 0, 2), 48, 1152 + 192, 48)))
+        y2_maps = dot_nt(both(level_two), e2[1152:2304, 0:640])
+        y3 = dot_nt(both(level_three), e3[1152:2304, :])
+        for t in range(2):
+            section(sg2, t, y3, 1, 32 * t, K2)
+
+        def grads_two(t):
+            read = section_reader(sg2, t)
+            return lhs(cells_of(read, 32) + shifted(read, 3, 32, 2))
+
+        grads = both(grads_two)
+        y2 = y2_maps + dot_nt(grads, e2[1152:2304, 640:1280])
+        for t in range(2):
+            section(sg1, t, y2, 2, 32 * t, K1)
+
+        def grads_one(t):
+            read = section_reader(sg1, t)
+            return lhs(cells_of(read, 48) + shifted(read, 5, 48, 1))
+
+        y1 = dot_nt(both(grads_one), e1[:, 512:1024])
+        y2 = dot_nt(grads, e2[0:1152, 640:1280])
+        for t in (1, 0):
+            view = acc.at[t]
+            for p in range(4):
+                even, odd = upsampled(y1, p, 48 * t)
+                put(view, 16 * p, even)
+                put(view, 16 * p + 8, odd)
+            for p in range(2):
+                even, odd = upsampled(y2, p, 32 * t)
+                put(view, 64 + 16 * p, even)
+                put(view, 72 + 16 * p, odd)
+
+    def emit(ref, rows, base, maps_of):
+        for l in range(3):
+            out[l, 0 : 8 * rows, :] = (
+                maps_of[l, 0 : 8 * rows, :] + acc[0, l, base : base + 8 * rows, :] + acc_in[l, base : base + 8 * rows, :]
+            )
         for cell in range(8):
             for l in range(3):
                 lane0 = CELL * cell + 128 * l
@@ -446,42 +579,36 @@
                     piece = out[l, pl.ds(cell, rows, stride=8), :]
                 ref[:, lane0 : lane0 + 128] = piece.astype(BF)
 
-    def block_sums(buffer, rows, factor):
-        groups = []
-        for first in range(0, rows, factor):
-            pieces = []
-            for l in range(3):
-                total = buffer[l, 8 * first : 8 * first + 8, :]
-                for p in range(first + 1, first + factor):
-                    total = total + buffer[l, 8 * p : 8 * p + 8, :]
-                pieces.append(total)
-            groups.append(jnp.concatenate(pieces, axis=1))
-        return jnp.concatenate(groups, axis=0).astype(BF)
-
-    def own(buffer, rows):
-        return jnp.concatenate([buffer[l, 0 : 8 * rows, :] for l in range(3)], axis=1)
-
     class Part:
         def __init__(self, s, lo, size, sem):
             self.s, self.lo, self.size, self.used = s, lo, size, sem
             self.u, self.v = (b, y) if s == 0 else (y, b)
             self.pending, self.second = [], []
 
-        def send(self, ref, x_to, tile_to):
+        def holds(self, x_of):
+            return (x_of != 3) | (c == self.s)
+
+        def send(self, ref, x_to, tile_to, x_of=None):
             copy = remote(ref, ref, s_send.at[self.used], s_recv.at[self.used], x_to, tile_to)
-            copy.start()
             self.used += 1
-            self.pending.append(copy)
+            self.pending.append((copy, x_of))
+            self.when(x_of, copy.start)
             return copy
+
+        def when(self, x_of, act):
+            if x_of is None:
+                act()
+            else:
+                pl.when(self.holds(x_of))(act)
 
         def send_bundle(self, u_of, to_u, to_v):
             zs = pl.ds(self.lo, self.size)
             if self.s == 0:
-                return self.send(tiles.at[0, u_of, y, c, zs], to_u, tile_of(z, to_v, c))
-            return self.send(tiles.at[1, b, u_of, c, zs], to_v, tile_of(z, to_u, c))
+                return self.send(tiles.at[0, u_of, y, c, zs], to_u, tile_of(z, to_v, c), u_of)
+            return self.send(tiles.at[1, b, u_of, c, zs], to_v, tile_of(z, to_u, c), b)
 
         def spread(self, u_of):
-            self.second.append((u_of, [self.send_bundle(u_of, self.u, wrap(self.v + d, 4)) for d in (1, 3, 2)]))
+            self.second.append((u_of, [(d, self.send_bundle(u_of, self.u, wrap(self.v + d, 4))) for d in (1, 3, 2)]))
 
         def start(self):
             self.first = [(d, self.send_bundle(self.u, wrap(self.u + d, 4), self.v)) for d in (1, 3, 2)]
@@ -489,21 +616,26 @@
 
         def pass_on(self):
             for d, copy in self.first:
-                copy.wait_recv()
-                self.spread(wrap(self.u - d, 4))
+                u_of = wrap(self.u - d, 4)
+                self.when(u_of if self.s == 0 else b, copy.wait_recv)
+                self.spread(u_of)
 
         def cross(self):
             zs = pl.ds(self.lo, self.size)
             self.across = []
             for u_of, copies_in in self.second:
-                for copy in copies_in:
-                    copy.wait_recv()
+                for d, copy in copies_in:
+                    self.when(u_of if self.s == 0 else wrap(b - d, 4), copy.wait_recv)
                 ref = tiles.at[0, u_of, :, c, zs] if self.s == 0 else tiles.at[1, :, u_of, c, zs]
                 self.across.append(self.send(ref, b, tile_of(z, y, 1 - c)))
 
         def arrived(self):
             for copy in self.across:
                 copy.wait_recv()
+
+        def sent(self):
+            for copy, x_of in self.pending:
+                self.when(x_of, copy.wait_send)
 
     parts = []
     for lo, size in Z_PARTS:
@@ -512,48 +644,30 @@
         pair = [Part(s, lo, size, 19 * (len(parts) + s)) for s in range(2)]
         for part in pair:
             part.start()
+        if lo == 0:
+            own_maps()
         for part in pair:
             part.pass_on()
         parts += pair
     for part in parts:
         part.cross()
+    strip_copy.wait_recv()
     for part in parts:
         part.arrived()
-    fill_e2_21()
-    fill_e2_31()
-    fill_e2_mid()
-    fill_e1_10()
-    fill_e1_mid()
-    y2 = dot_nt(lhs(lanes_of(c2) + shifted(c2, 3, 2)), e2[:, 0:640])
-    y1 = dot_nt(lhs(lanes_of(c1) + shifted(c1, 5, 1)), e1[:, 0:512])
-    fill_up()
-    fill_e3()
-
-    up = jnp.concatenate([block_sums(c0, 8, 8), block_sums(c1, 4, 4), block_sums(c2, 2, 2)], axis=1)
-    emit(o4, 1, own(c3, 1) + dot_nt(up, u3[...]))
-
-    y3 = dot_nt(lhs(lanes_of(c3) + shifted(c3, 2, 3)), e3[...])
-    up = jnp.concatenate([block_sums(c0, 8, 4), block_sums(c1, 4, 2)], axis=1)
-    down = jnp.concatenate(upsampled(y3, 0, 0), axis=0)
-    emit(o3, 2, own(c2, 2) + dot_nt(up, u2[...]) + down)
-
-    section(sg2, y3, 1, lambda l: k2a[l] + k2b[l])
-    y2 = y2 + dot_nt(lhs(lanes_of(sg2) + shifted(sg2, 3, 2)), e2[:, 640:1280])
-    down = jnp.concatenate(upsampled(y2, 0, 0) + upsampled(y2, 1, 0), axis=0)
-    emit(o2, 4, own(c1, 4) + dot_nt(block_sums(c0, 8, 2), u1[...]) + down)
-
-    section(sg1, y2, 2, lambda l: k1[l])
-    y1 = y1 + dot_nt(lhs(lanes_of(sg1) + shifted(sg1, 5, 1)), e1[:, 512:1024])
-    rows = []
-    for p in range(4):
-        rows.extend(upsampled(y1, p, 0))
-    emit(o1, 8, own(c0, 8) + jnp.concatenate(rows, axis=0))
-
+    pl.when(c == 0)(direct)
+    pl.when(c == 1)(chained)
+    acc_copy = remote(acc.at[1], acc_in, x_send.at[1], x_recv.at[1], b, tile_of(z, y, 1 - c))
+    acc_copy.start()
     for part in parts:
-        for copy in part.pending:
-            copy.wait_send()
-    for copy in list(copies.values()) + first:
+        part.sent()
+    for copy in list(copies.values()) + first + [strip_copy]:
         copy.wait_send()
+    acc_copy.wait_recv()
+    emit(o4, 1, 112, c3)
+    emit(o3, 2, 96, c2)
+    emit(o2, 4, 64, c1)
+    emit(o1, 8, 0, c0)
+    acc_copy.wait_send()
 
 
 def finish_kernel(*refs):
@@ -568,7 +682,6 @@
 
 def per_device(*operands):
     maps = operands[:12]
-    raw = jnp.pad(operands[12], (0, RAW_ROWS * 128 - SHARD)).reshape(RAW_ROWS, 128)
 
     def cells(rows):
         return pltpu.VMEM((3, rows, 128), F32)
@@ -586,22 +699,25 @@
         in_specs=[ANY] * 13,
         out_specs=[VMEM] * 4,
         scratch_shapes=[buffer(*m.shape) for m in maps] + [
-            buffer(RAW_ROWS, 128),
+            buffer(SHARD),
             buffer(*TILES), buffer(48, CELL), buffer(32, CELL), buffer(32, CELL),
-            buffer(RAW_ROWS, 128), buffer(RAW_ROWS, 128), pltpu.VMEM((WINDOW, 128), F32),
+            buffer(RAW_ROWS, 128), buffer(RAW_ROWS, 128), buffer(RAW_ROWS, 128),
+            pltpu.VMEM((RAW_ROWS, 128), F32), pltpu.VMEM((WINDOW, 128), F32),
             pltpu.VMEM((48, CELL), F32), pltpu.VMEM((32, CELL), F32), buffer(48, CELL), buffer(32, CELL),
             buffer(2304, 768), buffer(2304, 1280), buffer(1152, 1024),
             buffer(384, 1152), buffer(384, 768), buffer(384, 384),
             pltpu.VMEM((2, 1024, 128), F32), buffer(CELL, 4096), buffer(256, CELL * len(PLACES)),
-            cells(64), cells(48), cells(32), cells(32), cells(48), cells(32),
+            cells(64), cells(48), cells(32), cells(32),
+            pltpu.VMEM((2, 3, 48, 128), F32), pltpu.VMEM((2, 3, 32, 128), F32),
             cells(32), cells(32), cells(16), cells(16), cells(48), cells(32), cells(32), cells(48), cells(64),
-            sems(13), sems(5), sems(5), sems(NZ - 1), sems(NZ - 1), sems(38 * len(Z_PARTS)), sems(38 * len(Z_PARTS)),
+            pltpu.VMEM((2, 3, STRIP, 128), F32), pltpu.VMEM((2, 3, 120, 128), F32), cells(120),
+            sems(13), sems(5), sems(5), sems(NZ - 1), sems(NZ - 1), sems(38 * len(Z_PARTS)), sems(38 * len(Z_PARTS)), sems(2), sems(2),
         ],
         compiler_params=pltpu.CompilerParams(
             collective_id=0, has_side_effects=True, vmem_limit_bytes=60 * 2**20
         ),
         name="exchange",
-    )(*maps, raw)
+    )(*operands)
     return pl.pallas_call(
         finish_kernel,
         out_shape=results,

time: 61.3 us -> 55.7 us (0.909)
  Pallas kernels: 59.1 us -> 54.8 us
  local copies, waits for them, and re-layouts: 1.36 us -> 0 us
    pallas_call x1, Pallas kernels: 57.6 us -> 53.4 us  [per_device(): pl.pallas_call(exchange_kernel, out_shape=results, in_specs=[ANY] * 13, o...]
    reshape x1 -> x0, local copies, waits for them, and re-layouts: 1.36 us -> none  [per_device(): jnp.pad(operands[12], (0, RAW_ROWS * 128 - SHARD)).reshape(RAW_ROWS, 128)]
where the time goes in v5:
time: 55.7 us; the launch traced here: 55.5 us
  Pallas kernels  54.8 us (98%)
  between operations  0.64 us (1%)
    pallas_call x1, Pallas kernels, per_device(): pl.pallas_call(exchange_kernel, out_shape=results, in_specs=[ANY] * 13, o...  53.4 us
    pallas_call x1, Pallas kernels, per_device(): pl.pallas_call(finish_kernel, out_shape=results, in_specs=[VMEM] * 4, out...  1.46 us

profile of v5, /device:TPU:1, one launch (start us, length us, event | category | flops | bytes accessed | tf_op | source)
XLA Modules:
  0.0 55.5 jit_solution(13278230931126057620)
XLA Ops:
  0.6 53.4 %exchange.1 = (bf16[8,3072]{1,0:T(8,128)(2,1)}, bf16[4,3072]{1,0:T(4,128)(2,1)}, bf16[2,3072]{1,0:T(2,128)(2,1)}, bf16[1,3072]{1,0:T(2,128)(2,1)}) custom-call(bf16[8,3072]{1,0:T(8,128)(2,1)} %refs_0_.1, bf16[4,3072]{1,0:T(4,128)(2,1)} %refs_1_.1, bf16[2,3072]{1,0:T(2,128)(2,1)} %refs_2_.1, bf16[1,3072]{1,0:T(2,128)(2,1)} %refs_3_.1, ...), custom_call_target="tpu_custom_call" | custom-call | tf_op jit(solution)/shard_map/exchange/pallas_call | solution.py:696
  54.0 1.5 %finish.1 = (bf16[8,3072]{1,0:T(8,128)(2,1)}, bf16[4,3072]{1,0:T(4,128)(2,1)}, bf16[2,3072]{1,0:T(2,128)(2,1)}, bf16[1,3072]{1,0:T(2,128)(2,1)}) custom-call(bf16[8,3072]{1,0:T(8,128)(2,1)} %get-tuple-element.8.refs_0_, bf16[4,3072]{1,0:T(4,128)(2,1)} %get-tuple-element.9.refs_1_, bf16[2,3072]{1,0:T(2,128)(2,1)} %get-tuple-element.10.refs_2_, ...), custom_call_target="tpu_custom_call" | custom-call | tf_op jit(solution)/shard_map/finish/pallas_call | solution.py:721

commit v6 on v5

--- a/solution.py
+++ b/solution.py
@@ -11,12 +11,11 @@
 N_TILE = 128
 N_BRANCH = 4
 NZ = 16
-Z_PARTS = ((0, 5), (5, 11))
+Z_PARTS = ((0, 9), (9, 7))
 SHARD = 13734
 CELL = 384
 RAW_ROWS = 112
-BASE = 104
-WINDOW = 464
+FLAT_ROWS = 13744
 
 C1, C2, C3, SUMS, K1, K2, STRIP = 0, 48, 80, 112, 200, 248, 280
 
@@ -54,15 +53,8 @@
     )
 
 
-def tile_at(row_tile, jb):
-    group, n = row_tile // 9, 3 * (row_tile % 9) + jb
-    j, slot = n // 7, n % 7
-    k = 4 * group + j
-    return k // 8, (slot % 2 if slot < 6 else k % 2, slot // 2, (k // 2) % 4, k % 2)
-
-
-def place_of(distance):
-    return 2 * distance - 1 if distance > 0 else -2 * distance
+def slots_of(k):
+    return [(t % 2 if t < 6 else k % 2, t // 2, (k // 2) % 4, k % 2) for t in range(7)]
 
 
 def dot(a, b):
@@ -85,7 +77,7 @@
     inputs, outputs, refs = refs[:13], refs[13:17], refs[17:]
     loaded, refs = refs[:13], refs[13:]
     (
-        tiles, row_in, col_in, corner_in, raw, raw1, raw2, shard_f, win, row_f, col_f, row_out, col_out,
+        tiles, row_in, col_in, corner_in, shard_f, flat, row_f, col_f, row_out, col_out,
         e3, e2, e1, u3, u2, u1, wide, splits, copies_of,
         c0, c1, c2, c3, sg1, sg2, q20, q30a, q30b, q31, k1, k2a, k2b, nxt, out, strip, acc, acc_in,
         l_sem, h_send, h_recv, z_send, z_recv, s_send, s_recv, x_send, x_recv,
@@ -109,22 +101,18 @@
         return lax.rem(value + count, count)
 
     left, right = wrap(b - 1, N_BRANCH), wrap(b + 1, N_BRANCH)
-    up1, up2 = wrap(k - 1, N_TILE), wrap(k - 2, N_TILE)
-    down1, down2 = wrap(k + 1, N_TILE), wrap(k + 2, N_TILE)
+    up1, down1 = wrap(k - 1, N_TILE), wrap(k + 1, N_TILE)
 
     partners = [
-        (b, up1), (b, up2), (b, down1), (b, down2), (left, k), (right, k), (left, up1), (right, down1),
+        (b, up1), (b, down1), (left, k), (right, k), (left, up1), (right, down1),
         (b, tile_of(z, y, 1 - c)), (wrap(b + 2, 4), k),
     ] + [(b, tile_of(z, wrap(y + d, 4), c)) for d in (1, 2, 3)]
+    along_z = [1, -1, 2, -2, 3, -3, 4, -4]
+    partners += [(b, tile_of(wrap(z + d, NZ), y, c)) for d in along_z]
     barrier = pltpu.get_barrier_semaphore()
-    for step in range(1, NZ):
-        pl.semaphore_signal(
-            barrier, inc=1, device_id=(b, tile_of(wrap(z + step, NZ), y, c)), device_id_type=MESH
-        )
     for who in partners:
         pl.semaphore_signal(barrier, inc=1, device_id=who, device_id_type=MESH)
 
-    win[...] = jnp.zeros_like(win)
     loads[12].wait()
     whole = SHARD // 1024 * 1024
     rest = SHARD // 128 * 128
@@ -133,18 +121,19 @@
     shard_f[row_at[0] : row_at[1], :] = shard_in[whole:rest].astype(F32).reshape(row_at[1] - row_at[0], 128)
     shard_f[row_at[1] : RAW_ROWS, :] = jnp.zeros((RAW_ROWS - row_at[1], 128), F32)
     shard_f[row_at[1] : row_at[1] + 1, 0 : SHARD - rest] = shard_in[rest:SHARD].astype(F32).reshape(1, SHARD - rest)
-    raw[...] = shard_f[...].astype(BF)
-
-    pl.semaphore_wait(barrier, len(partners) + NZ - 1)
-    first = [
-        remote(raw, raw1, h_send.at[0], h_recv.at[0], b, up1),
-        remote(raw, raw2, h_send.at[1], h_recv.at[1], b, up2),
-        remote(row_out, row_in, h_send.at[2], h_recv.at[2], b, up1),
-        remote(col_out, col_in, h_send.at[3], h_recv.at[3], left, k),
-        remote(col_out, corner_in, h_send.at[4], h_recv.at[4], left, up1),
-    ]
-    for copy in first[:2]:
+    for s in range(2):
+        row = jnp.where(b == 3, 96, 32 * b + 16 * s)
+        tiles[s, b, y, c, 4] = shard_f[pl.ds(pl.multiple_of(row, 16), 16), :].astype(BF)
+
+    pl.semaphore_wait(barrier, len(partners))
+    near = []
+    for n, d in enumerate(along_z):
+        copy = remote(
+            tiles.at[:, b, y, c, 4], tiles.at[:, b, y, c, 4 - d], z_send.at[n], z_recv.at[n],
+            b, tile_of(wrap(z + d, NZ), y, c),
+        )
         copy.start()
+        near.append(copy)
 
     for load in loads[:12]:
         load.wait()
@@ -167,36 +156,13 @@
     row_out[...] = row_f[...].astype(BF)
     col_out[...] = col_f[...].astype(BF)
 
-    for copy in first[2:]:
+    first = [
+        remote(row_out, row_in, h_send.at[0], h_recv.at[0], b, up1),
+        remote(col_out, col_in, h_send.at[1], h_recv.at[1], left, k),
+        remote(col_out, corner_in, h_send.at[2], h_recv.at[2], left, up1),
+    ]
+    for copy in first:
         copy.start()
-
-    group, j = k // 4, lax.rem(k, 4)
-    first_tile = (7 * j) // 3
-    delta = 13734 * j - 6144 * first_tile - 360 * group + BASE * 128
-    lane = lax.broadcasted_iota(jnp.int32, (RAW_ROWS, 128), 1)
-    for d, shard in enumerate((raw, raw1, raw2)):
-        if d > 0:
-            first[d - 1].wait_recv()
-        start = delta + SHARD * d
-        q, phase = start // 128, lax.rem(start, 128)
-        rolled = pltpu.roll(shard[...].astype(F32), phase, 1)
-        win[pl.ds(q, RAW_ROWS), :] += jnp.where(lane >= phase, rolled, 0.0)
-        win[pl.ds(q + 1, RAW_ROWS), :] += jnp.where(lane >= phase, 0.0, rolled)
-    for s in range(2):
-        n = 7 * j + jnp.where(b == 3, 6, 2 * b + s)
-        row_tile = 9 * group + n // 3
-        offset = jnp.where(row_tile >= 124, 2, 10)
-        origin = BASE + 3 * (16 * (n // 3 - first_tile) + offset) + lax.rem(n, 3)
-        tiles[s, b, y, c, 0] = win[pl.ds(origin, 16, stride=3), :].astype(BF)
-
-    copies = {}
-    for step in (1, 15, 2, 14, 3, 13, 4, 12, 5, 11, 6, 10, 7, 9, 8):
-        at = place_of(-step if step <= 7 else NZ - step)
-        copies[at] = remote(
-            tiles.at[:, b, y, c, 0], tiles.at[:, b, y, c, at], z_send.at[at - 1], z_recv.at[at - 1],
-            b, tile_of(wrap(z + step, NZ), y, c),
-        )
-        copies[at].start()
 
     for (j, at), lanes in SPLITS.items():
         width = 256 if j == 192 else 128
@@ -284,7 +250,7 @@
         for buffer, m, units in ((q20, m20, 4), (q30a, m30a, 4), (q31, m31, 4), (q30b, m30b, 2)):
             spread_units(buffer, m[...].astype(F32), units)
 
-        for copy in first[2:]:
+        for copy in first:
             copy.wait_recv()
         row_halo = row_in[...].astype(F32)
         col_halo = col_in[...].astype(F32)
@@ -328,35 +294,40 @@
         strip.at[0], strip.at[1], x_send.at[0], x_recv.at[0], b, tile_of(z, y, 1 - c)
     )
 
-    distances = [lax.rem(zz - z + 23, NZ) - 7 for zz in range(NZ)]
-    places = [jnp.where(d > 0, 2 * d - 1, -2 * d) for d in distances]
-
-    def tile(row_tile, jb):
-        zz, (s, x_at, y_at, c_at) = tile_at(row_tile, jb)
-        return tiles[s, x_at, y_at, c_at, places[zz]]
-
-    def load_rows(row_tile, count):
-        columns = [
-            jnp.concatenate([tile(row_tile + t, jb) for t in range(count)], axis=0) for jb in range(3)
-        ]
-        return jnp.concatenate(columns, axis=1)
+    places = [lax.rem(zz - z + 4 + NZ, NZ) for zz in range(NZ)]
+    lane_no = lax.broadcasted_iota(jnp.int32, (RAW_ROWS, 128), 1)
+
+    def line_up(ranges):
+        for shard in range(N_TILE):
+            first_row, phase = divmod(SHARD * shard, 128)
+            if not any(first_row < 3 * hi and first_row + 109 > 3 * lo for lo, hi in ranges):
+                continue
+            blocks = [tiles[s, x_at, y_at, c_at, places[shard // 8]] for s, x_at, y_at, c_at in slots_of(shard)]
+            value = jnp.concatenate(blocks, axis=0).astype(F32)
+            if phase == 0:
+                flat[first_row : first_row + RAW_ROWS, :] = value
+                continue
+            value = pltpu.roll(value, phase, 1)
+            pltpu.store(flat.at[first_row : first_row + RAW_ROWS, :], value, mask=lane_no >= phase)
+            pltpu.store(flat.at[first_row + 1 : first_row + 1 + RAW_ROWS, :], value, mask=lane_no < phase)
+
+    def load_rows(row, count):
+        return [flat[pl.ds(3 * row + jb, count, stride=3), :].astype(BF) for jb in range(3)]
 
     def rows_of(key, rows, j, at=0):
         n = CELL // j
-        r0 = ROW0[key]
-        row_tile, offset = (286, 0) if r0 == 0 else divmod(r0 - 10, 16)
-        count = -(-(offset + rows) // 16)
         width = 256 if j == 192 else 128
 
         lanes = SPLITS[j, at]
-        split = dot(load_rows(row_tile, count), splits[:, lanes : lanes + n * width])
+        whole = jnp.concatenate(load_rows(ROW0[key], rows), axis=1)
+        split = dot(whole, splits[:, lanes : lanes + n * width])
         parts = []
         for half in range(width // 128):
             for part in range(n):
-                wide[half, pl.ds(part, 16 * count, stride=n), :] = split[
+                wide[half, pl.ds(part, rows, stride=n), :] = split[
                     :, part * width + 128 * half : part * width + 128 * (half + 1)
                 ]
-            parts.append(wide[half, offset * n : (offset + rows) * n, :])
+            parts.append(wide[half, 0 : rows * n, :])
         return parts[0] if len(parts) == 1 else jnp.concatenate(parts, axis=1)
 
     def place(weights, j, low, high):
@@ -384,18 +355,12 @@
 
     def fill_e3(kernels):
         for key, i, row0, pitch in kernels:
-            r0 = ROW0[key]
-            start = 124 + (r0 - 1986) // 16 if r0 >= 1986 else (r0 - 10) // 16
             for a in range(3):
                 even = row0 + CELL * a
                 odd = even + pitch
                 for bb, at, seg in ((1, even, 0), (2, odd, 0), (0, odd, CELL)):
-                    first = start + (3 * a + bb) * (i // 16)
-                    for t in range(i // 16):
-                        for jb in range(3):
-                            e3[at + 16 * t : at + 16 * (t + 1), seg + 128 * jb : seg + 128 * (jb + 1)] = tile(
-                                first + t, jb
-                            )
+                    for jb, piece in enumerate(load_rows(ROW0[key] + (3 * a + bb) * i, i)):
+                        e3[at : at + i, seg + 128 * jb : seg + 128 * (jb + 1)] = piece
 
     def fill_e2_21():
         w = rows_of((2, 1, 0), 432, 192)
@@ -504,6 +469,7 @@
             buffer[t, l] = jnp.where(strip[t, l, kept : kept + buffer.shape[2], :] > 0.5, buffer[t, l], 0.0)
 
     def direct():
+        line_up(((0, 336), (606, 1230), (2850, 4578)))
         fill_e2_21()
         fill_e1_10()
         fill_up()
@@ -530,6 +496,7 @@
             put(view, 112, x3[8 * t : 8 * t + 8])
 
     def chained():
+        line_up(((336, 606), (1230, 2850)))
         fill_e2_31()
         fill_e2_mid()
         fill_e1_mid()
@@ -637,18 +604,29 @@
             for copy, x_of in self.pending:
                 self.when(x_of, copy.wait_send)
 
-    parts = []
-    for lo, size in Z_PARTS:
-        for at in range(max(lo, 1), lo + size):
-            copies[at].wait_recv()
-        pair = [Part(s, lo, size, 19 * (len(parts) + s)) for s in range(2)]
-        for part in pair:
-            part.start()
-        if lo == 0:
-            own_maps()
-        for part in pair:
-            part.pass_on()
-        parts += pair
+    for copy in near:
+        copy.wait_recv()
+    far = [
+        remote(
+            tiles.at[:, b, y, c, pl.ds(lo, size)], tiles.at[:, b, y, c, pl.ds(to, size)], z_send.at[8 + n], z_recv.at[8 + n],
+            b, tile_of(wrap(z + d, NZ), y, c),
+        )
+        for n, (lo, size, to, d) in enumerate(((5, 4, 9, -4), (1, 3, 13, 4)))
+    ]
+    for copy in far:
+        copy.start()
+    parts = [Part(s, lo, size, 19 * (2 * n + s)) for n, (lo, size) in enumerate(Z_PARTS) for s in range(2)]
+    for part in parts[:2]:
+        part.start()
+    own_maps()
+    for part in parts[:2]:
+        part.pass_on()
+    for copy in far:
+        copy.wait_recv()
+    for part in parts[2:]:
+        part.start()
+    for part in parts[2:]:
+        part.pass_on()
     for part in parts:
         part.cross()
     strip_copy.wait_recv()
@@ -660,7 +638,7 @@
     acc_copy.start()
     for part in parts:
         part.sent()
-    for copy in list(copies.values()) + first + [strip_copy]:
+    for copy in near + far + first + [strip_copy]:
         copy.wait_send()
     acc_copy.wait_recv()
     emit(o4, 1, 112, c3)
@@ -701,8 +679,7 @@
         scratch_shapes=[buffer(*m.shape) for m in maps] + [
             buffer(SHARD),
             buffer(*TILES), buffer(48, CELL), buffer(32, CELL), buffer(32, CELL),
-            buffer(RAW_ROWS, 128), buffer(RAW_ROWS, 128), buffer(RAW_ROWS, 128),
-            pltpu.VMEM((RAW_ROWS, 128), F32), pltpu.VMEM((WINDOW, 128), F32),
+            pltpu.VMEM((RAW_ROWS, 128), F32), pltpu.VMEM((FLAT_ROWS, 128), F32),
             pltpu.VMEM((48, CELL), F32), pltpu.VMEM((32, CELL), F32), buffer(48, CELL), buffer(32, CELL),
             buffer(2304, 768), buffer(2304, 1280), buffer(1152, 1024),
             buffer(384, 1152), buffer(384, 768), buffer(384, 384),
@@ -711,7 +688,7 @@
             pltpu.VMEM((2, 3, 48, 128), F32), pltpu.VMEM((2, 3, 32, 128), F32),
             cells(32), cells(32), cells(16), cells(16), cells(48), cells(32), cells(32), cells(48), cells(64),
             pltpu.VMEM((2, 3, STRIP, 128), F32), pltpu.VMEM((2, 3, 120, 128), F32), cells(120),
-            sems(13), sems(5), sems(5), sems(NZ - 1), sems(NZ - 1), sems(38 * len(Z_PARTS)), sems(38 * len(Z_PARTS)), sems(2), sems(2),
+            sems(13), sems(3), sems(3), sems(10), sems(10), sems(38 * len(Z_PARTS)), sems(38 * len(Z_PARTS)), sems(2), sems(2),
         ],
         compiler_params=pltpu.CompilerParams(
             collective_id=0, has_side_effects=True, vmem_limit_bytes=60 * 2**20

time: 55.7 us -> 51 us (0.916)
  Pallas kernels: 54.8 us -> 50.1 us
    pallas_call x1, Pallas kernels: 53.4 us -> 48.7 us  [per_device(): pl.pallas_call(exchange_kernel, out_shape=results, in_specs=[ANY] * 13, o...]
where the time goes in v6:
time: 51 us; the launch traced here: 50.8 us
  Pallas kernels  50.1 us (98%)
  between operations  0.64 us (1%)
    pallas_call x1, Pallas kernels, per_device(): pl.pallas_call(exchange_kernel, out_shape=results, in_specs=[ANY] * 13, o...  48.7 us
    pallas_call x1, Pallas kernels, per_device(): pl.pallas_call(finish_kernel, out_shape=results, in_specs=[VMEM] * 4, out...  1.46 us

profile of v6, /device:TPU:1, one launch (start us, length us, event | category | flops | bytes accessed | tf_op | source)
XLA Modules:
  0.0 50.8 jit_solution(3308721177778558734)
XLA Ops:
  0.6 48.7 %exchange.1 = (bf16[8,3072]{1,0:T(8,128)(2,1)}, bf16[4,3072]{1,0:T(4,128)(2,1)}, bf16[2,3072]{1,0:T(2,128)(2,1)}, bf16[1,3072]{1,0:T(2,128)(2,1)}) custom-call(bf16[8,3072]{1,0:T(8,128)(2,1)} %refs_0_.1, bf16[4,3072]{1,0:T(4,128)(2,1)} %refs_1_.1, bf16[2,3072]{1,0:T(2,128)(2,1)} %refs_2_.1, bf16[1,3072]{1,0:T(2,128)(2,1)} %refs_3_.1, ...), custom_call_target="tpu_custom_call" | custom-call | tf_op jit(solution)/shard_map/exchange/pallas_call | solution.py:674
  49.3 1.5 %finish.1 = (bf16[8,3072]{1,0:T(8,128)(2,1)}, bf16[4,3072]{1,0:T(4,128)(2,1)}, bf16[2,3072]{1,0:T(2,128)(2,1)}, bf16[1,3072]{1,0:T(2,128)(2,1)}) custom-call(bf16[8,3072]{1,0:T(8,128)(2,1)} %get-tuple-element.8.refs_0_, bf16[4,3072]{1,0:T(4,128)(2,1)} %get-tuple-element.9.refs_1_, bf16[2,3072]{1,0:T(2,128)(2,1)} %get-tuple-element.10.refs_2_, ...), custom_call_target="tpu_custom_call" | custom-call | tf_op jit(solution)/shard_map/finish/pallas_call | solution.py:698

commit v7 on v6

--- a/solution.py
+++ b/solution.py
@@ -91,8 +91,7 @@
     has_col = b < N_BRANCH - 1
 
     loads = [pltpu.make_async_copy(inputs[n], loaded[n], l_sem.at[n]) for n in range(13)]
-    for n in (12, 1, 2, 3, 5, 6, 7, 8, 9, 10, 11, 0, 4):
-        loads[n].start()
+    loads[12].start()
 
     def tile_of(zz, yy, cc):
         return zz * 8 + yy * 2 + cc
@@ -112,6 +111,8 @@
     barrier = pltpu.get_barrier_semaphore()
     for who in partners:
         pl.semaphore_signal(barrier, inc=1, device_id=who, device_id_type=MESH)
+    for n in (1, 2, 3, 5, 6, 7, 8, 9, 10, 11, 0, 4):
+        loads[n].start()
 
     loads[12].wait()
     whole = SHARD // 1024 * 1024
@@ -164,23 +165,6 @@
     for copy in first:
         copy.start()
 
-    for (j, at), lanes in SPLITS.items():
-        width = 256 if j == 192 else 128
-
-        def split_target(col):
-            part, lane = col // width, lax.rem(col, width) - at
-            return jnp.where((lane >= 0) & (lane < j), part * j + lane, -1)
-
-        splits[:, lanes : lanes + CELL // j * width] = unit_matrix(CELL, CELL // j * width, split_target)
-    for number, (j, low, high) in enumerate(PLACES):
-
-        def place_target(col):
-            which = col // j
-            return jnp.where((which >= low) & (which < high), lax.rem(col, j), -1)
-
-        rows = 256 if j == 192 else 128
-        copies_of[0:rows, CELL * number : CELL * (number + 1)] = unit_matrix(rows, CELL, place_target)
-
     for ref in (e3, e2, e1, c1, c2, c3, sg1, sg2, q20, q30a, q30b, q31, k1, k2a, k2b, nxt, acc):
         ref[...] = jnp.zeros_like(ref)
 
@@ -444,6 +428,15 @@
             pieces += [strip[t, l, SUMS + start : SUMS + start + rows, :] for l in range(3)]
         return lhs(pieces)
 
+    def taps_of(own, own_weights, after, after_weights):
+        whole = dot_nt(own, own_weights)
+        last = dot_nt(after, jnp.concatenate([after_weights[CELL * a + 256 : CELL * (a + 1)] for a in range(3)], axis=0))
+        pieces = []
+        for a in range(3):
+            pieces.append(whole[:, CELL * a : CELL * a + 256])
+            pieces.append(whole[:, CELL * a + 256 : CELL * (a + 1)] + last[:, 128 * a : 128 * (a + 1)])
+        return jnp.concatenate(pieces, axis=1)
+
     def rows_out(y, a, lo, hi):
         return y[lo:hi, CELL * a : CELL * (a + 1)]
 
@@ -475,8 +468,9 @@
         fill_up()
         fill_e3((((3, 2, 0), 192, 0, 192),))
         y3 = dot_nt(both(level_three), e3[0:1152, :])
-        y2 = dot_nt(both(level_two), e2[0:1152, 0:640])
-        y1 = dot_nt(both(level_one), e1[:, 0:512])
+        maps_two, maps_one = both(level_two), both(level_one)
+        y2 = taps_of(maps_two[:, 0:384], e2[0:1152, 0:384], maps_two[:, 384:640], e2[0:1152, 384:640])
+        y1 = taps_of(maps_one[:, 0:384], e1[:, 0:384], maps_one[:, 384:512], e1[:, 384:512])
         x3 = dot_nt(both(lambda t: sums_of(t, (48, 8), (72, 8), (80, 8))), u3[...])
         x2 = dot_nt(both(lambda t: sums_of(t, (32, 16), (56, 16))), u2[...])
         x1 = dot_nt(both(lambda t: sums_of(t, (0, 32))), u1[...])
@@ -501,7 +495,8 @@
         fill_e2_mid()
         fill_e1_mid()
         fill_e3((((3, 1, 1), 96, 1152, 96), ((3, 0, 2), 48, 1152 + 192, 48)))
-        y2_maps = dot_nt(both(level_two), e2[1152:2304, 0:640])
+        maps_two = both(level_two)
+        y2_maps = taps_of(maps_two[:, 0:384], e2[1152:2304, 0:384], maps_two[:, 384:640], e2[1152:2304, 384:640])
         y3 = dot_nt(both(level_three), e3[1152:2304, :])
         for t in range(2):
             section(sg2, t, y3, 1, 32 * t, K2)
@@ -511,7 +506,9 @@
             return lhs(cells_of(read, 32) + shifted(read, 3, 32, 2))
 
         grads = both(grads_two)
-        y2 = y2_maps + dot_nt(grads, e2[1152:2304, 640:1280])
+        y2 = y2_maps + taps_of(
+            grads[:, 128:384], e2[1152:2304, 768:1024], grads[:, 512:640], e2[1152:2304, 1152:1280]
+        )
         for t in range(2):
             section(sg1, t, y2, 2, 32 * t, K1)
 
@@ -519,8 +516,9 @@
             read = section_reader(sg1, t)
             return lhs(cells_of(read, 48) + shifted(read, 5, 48, 1))
 
-        y1 = dot_nt(both(grads_one), e1[:, 512:1024])
-        y2 = dot_nt(grads, e2[0:1152, 640:1280])
+        ones = both(grads_one)
+        y1 = taps_of(ones[:, 0:384], e1[:, 512:896], ones[:, 384:512], e1[:, 896:1024])
+        y2 = taps_of(grads[:, 0:256], e2[0:1152, 640:896], grads[:, 384:512], e2[0:1152, 1024:1152])
         for t in (1, 0):
             view = acc.at[t]
             for p in range(4):
@@ -619,6 +617,23 @@
     for part in parts[:2]:
         part.start()
     own_maps()
+    for (j, at), lanes in SPLITS.items():
+        width = 256 if j == 192 else 128
+
+        def split_target(col):
+            part, lane = col // width, lax.rem(col, width) - at
+            return jnp.where((lane >= 0) & (lane < j), part * j + lane, -1)
+
+        splits[:, lanes : lanes + CELL // j * width] = unit_matrix(CELL, CELL // j * width, split_target)
+    for number, (j, low, high) in enumerate(PLACES):
+
+        def place_target(col):
+            which = col // j
+            return jnp.where((which >= low) & (which < high), lax.rem(col, j), -1)
+
+        rows = 256 if j == 192 else 128
+        copies_of[0:rows, CELL * number : CELL * (number + 1)] = unit_matrix(rows, CELL, place_target)
+
     for part in parts[:2]:
         part.pass_on()
     for copy in far:
@@ -653,7 +668,7 @@
         refs[4 + n][...] = refs[n][...]
 
 
-ANY = pl.BlockSpec(memory_space=pl.ANY)
+HBM = pl.BlockSpec(memory_space=pltpu.HBM)
 VMEM = pl.BlockSpec(memory_space=pltpu.VMEM)
 TILES = (2, 4, 4, 2, NZ, 16, 128)
 
@@ -674,7 +689,7 @@
     done = pl.pallas_call(
         exchange_kernel,
         out_shape=results,
-        in_specs=[ANY] * 13,
+        in_specs=[HBM] * 13,
         out_specs=[VMEM] * 4,
         scratch_shapes=[buffer(*m.shape) for m in maps] + [
             buffer(SHARD),
@@ -691,7 +706,7 @@
             sems(13), sems(3), sems(3), sems(10), sems(10), sems(38 * len(Z_PARTS)), sems(38 * len(Z_PARTS)), sems(2), sems(2),
         ],
         compiler_params=pltpu.CompilerParams(
-            collective_id=0, has_side_effects=True, vmem_limit_bytes=60 * 2**20
+            collective_id=0, has_side_effects=True, vmem_limit_bytes=46 * 2**20
         ),
         name="exchange",
     )(*operands)
@@ -700,7 +715,7 @@
         out_shape=results,
         in_specs=[VMEM] * 4,
         out_specs=[VMEM] * 4,
-        compiler_params=pltpu.CompilerParams(vmem_limit_bytes=60 * 2**20),
+        compiler_params=pltpu.CompilerParams(vmem_limit_bytes=4 * 2**20),
         name="finish",
     )(*done)
 

time: 51 us -> 58.6 us (1.15)
  local copies, waits for them, and re-layouts: 0 us -> 9.42 us
  Pallas kernels: 50.1 us -> 47.8 us
    unnamed x0 -> x26, local copies, waits for them, and re-layouts: none -> 9.42 us
    pallas_call x1, Pallas kernels: 48.7 us -> 47.1 us  [per_device(): pl.pallas_call(exchange_kernel, out_shape=results, in_specs=[HBM] * 13, o...]
    pallas_call x1, Pallas kernels: 1.46 us -> 0.64 us  [per_device(): pl.pallas_call(finish_kernel, out_shape=results, in_specs=[VMEM] * 4, out...]
where the time goes in v7:
time: 58.6 us; the launch traced here: 57.9 us
  Pallas kernels  47.8 us (82%)
  local copies, waits for them, and re-layouts  9.42 us (16%)
  between operations  0.67 us (1%)
    pallas_call x1, Pallas kernels, per_device(): pl.pallas_call(exchange_kernel, out_shape=results, in_specs=[HBM] * 13, o...  47.1 us
    unnamed x26, local copies, waits for them, and re-layouts  9.42 us

profile of v7, /device:TPU:1, one launch (start us, length us, event | category | flops | bytes accessed | tf_op | source)
XLA Modules:
  0.0 57.9 jit_solution(10538431438846449177)
XLA Ops:
  0.6 0.0 copy-start
  0.6 0.8 %copy-done = bf16[8,3072]{1,0:T(8,128)(2,1)S(1)} copy-done((bf16[8,3072]{1,0:T(8,128)(2,1)S(1)}, bf16[8,3072]{1,0:T(8,128)(2,1)}, u32[]{:S(2)}) %copy-start) | copy-done | bytes 49176
  1.4 0.0 copy-start.1
  1.4 0.8 %copy-done.1 = bf16[8,3072]{1,0:T(8,128)(2,1)S(1)} copy-done((bf16[8,3072]{1,0:T(8,128)(2,1)S(1)}, bf16[8,3072]{1,0:T(8,128)(2,1)}, u32[]{:S(2)}) %copy-start.1) | copy-done | bytes 49176
  2.2 0.0 copy-start.2
  2.2 0.7 %copy-done.2 = bf16[13734]{0:T(1024)(128)(2,1)S(1)} copy-done((bf16[13734]{0:T(1024)(128)(2,1)S(1)}, bf16[13734]{0:T(1024)(128)(2,1)}, u32[]{:S(2)}) %copy-start.2) | copy-done | bytes 27492
  3.0 0.0 copy-start.3
  3.0 0.7 %copy-done.3 = bf16[4,3072]{1,0:T(4,128)(2,1)S(1)} copy-done((bf16[4,3072]{1,0:T(4,128)(2,1)S(1)}, bf16[4,3072]{1,0:T(4,128)(2,1)}, u32[]{:S(2)}) %copy-start.3) | copy-done | bytes 24600
  3.7 0.0 copy-start.4
  3.7 0.7 %copy-done.4 = bf16[4,3072]{1,0:T(4,128)(2,1)S(1)} copy-done((bf16[4,3072]{1,0:T(4,128)(2,1)S(1)}, bf16[4,3072]{1,0:T(4,128)(2,1)}, u32[]{:S(2)}) %copy-start.4) | copy-done | bytes 24600
  4.5 0.0 copy-start.5
  4.5 0.7 %copy-done.5 = bf16[2,3072]{1,0:T(2,128)(2,1)S(1)} copy-done((bf16[2,3072]{1,0:T(2,128)(2,1)S(1)}, bf16[2,3072]{1,0:T(2,128)(2,1)}, u32[]{:S(2)}) %copy-start.5) | copy-done | bytes 12312
  5.2 0.0 copy-start.6
  5.2 0.7 %copy-done.6 = bf16[1,3072]{1,0:T(2,128)(2,1)S(1)} copy-done((bf16[1,3072]{1,0:T(2,128)(2,1)S(1)}, bf16[1,3072]{1,0:T(2,128)(2,1)}, u32[]{:S(2)}) %copy-start.6) | copy-done | bytes 6168
  5.9 0.0 copy-start.7
  5.9 0.7 %copy-done.7 = bf16[2,3072]{1,0:T(2,128)(2,1)S(1)} copy-done((bf16[2,3072]{1,0:T(2,128)(2,1)S(1)}, bf16[2,3072]{1,0:T(2,128)(2,1)}, u32[]{:S(2)}) %copy-start.7) | copy-done | bytes 12312
  6.6 0.0 copy-start.8
  6.6 0.7 %copy-done.8 = bf16[1,3072]{1,0:T(2,128)(2,1)S(1)} copy-done((bf16[1,3072]{1,0:T(2,128)(2,1)S(1)}, bf16[1,3072]{1,0:T(2,128)(2,1)}, u32[]{:S(2)}) %copy-start.8) | copy-done | bytes 6168
  7.3 0.0 copy-start.9
  7.3 0.7 %copy-done.9 = bf16[4,1536]{1,0:T(4,128)(2,1)S(1)} copy-done((bf16[4,1536]{1,0:T(4,128)(2,1)S(1)}, bf16[4,1536]{1,0:T(4,128)(2,1)}, u32[]{:S(2)}) %copy-start.9) | copy-done | bytes 12312
  8.0 0.0 copy-start.10
  8.0 0.7 %copy-done.10 = bf16[4,1536]{1,0:T(4,128)(2,1)S(1)} copy-done((bf16[4,1536]{1,0:T(4,128)(2,1)S(1)}, bf16[4,1536]{1,0:T(4,128)(2,1)}, u32[]{:S(2)}) %copy-start.10) | copy-done | bytes 12312
  8.7 0.0 copy-start.11
  8.7 0.7 %copy-done.11 = bf16[2,1536]{1,0:T(2,128)(2,1)S(1)} copy-done((bf16[2,1536]{1,0:T(2,128)(2,1)S(1)}, bf16[2,1536]{1,0:T(2,128)(2,1)}, u32[]{:S(2)}) %copy-start.11) | copy-done | bytes 6168
  9.4 0.0 copy-start.12
  9.4 0.7 %copy-done.12 = bf16[2,768]{1,0:T(2,128)(2,1)S(1)} copy-done((bf16[2,768]{1,0:T(2,128)(2,1)S(1)}, bf16[2,768]{1,0:T(2,128)(2,1)}, u32[]{:S(2)}) %copy-start.12) | copy-done | bytes 3096
  10.1 47.1 %exchange.1 = (bf16[8,3072]{1,0:T(8,128)(2,1)S(1)}, bf16[4,3072]{1,0:T(4,128)(2,1)S(1)}, bf16[2,3072]{1,0:T(2,128)(2,1)S(1)}, bf16[1,3072]{1,0:T(2,128)(2,1)S(1)}) custom-call(bf16[8,3072]{1,0:T(8,128)(2,1)S(1)} %copy-done, bf16[4,3072]{1,0:T(4,128)(2,1)S(1)} %copy-done.3, bf16[2,3072]{1,0:T(2,128)(2,1)S(1)} %copy-done.5, bf16[1,3072]{1,0:T(2,128)(2,1)S(1)} %copy-done.6, ...), custom_call_target="tpu_custom_call" | custom-call | tf_op jit(solution)/shard_map/exchange/pallas_call | solution.py:689
  57.2 0.6 %finish.1 = (bf16[8,3072]{1,0:T(8,128)(2,1)}, bf16[4,3072]{1,0:T(4,128)(2,1)}, bf16[2,3072]{1,0:T(2,128)(2,1)}, bf16[1,3072]{1,0:T(2,128)(2,1)}) custom-call(bf16[8,3072]{1,0:T(8,128)(2,1)S(1)} %get-tuple-element.8.refs_0_, bf16[4,3072]{1,0:T(4,128)(2,1)S(1)} %get-tuple-element.9.refs_1_, bf16[2,3072]{1,0:T(2,128)(2,1)S(1)} %get-tuple-element.10.refs_2_, ...), custom_call_target="tpu_custom_call" | custom-call | tf_op jit(solution)/shard_map/finish/pallas_call | solution.py:713
Async XLA Ops:
  0.6 0.8 %copy-start = (bf16[8,3072]{1,0:T(8,128)(2,1)S(1)}, bf16[8,3072]{1,0:T(8,128)(2,1)}, u32[]{:S(2)}) copy-start(bf16[8,3072]{1,0:T(8,128)(2,1)} %refs_0_.1) | copy-start | bytes 147460
  1.4 0.8 %copy-start.1 = (bf16[8,3072]{1,0:T(8,128)(2,1)S(1)}, bf16[8,3072]{1,0:T(8,128)(2,1)}, u32[]{:S(2)}) copy-start(bf16[8,3072]{1,0:T(8,128)(2,1)} %refs_4_.1) | copy-start | bytes 147460
  2.2 0.7 %copy-start.2 = (bf16[13734]{0:T(1024)(128)(2,1)S(1)}, bf16[13734]{0:T(1024)(128)(2,1)}, u32[]{:S(2)}) copy-start(bf16[13734]{0:T(1024)(128)(2,1)} %refs_12_.1) | copy-start | bytes 82408
  3.0 0.7 %copy-start.3 = (bf16[4,3072]{1,0:T(4,128)(2,1)S(1)}, bf16[4,3072]{1,0:T(4,128)(2,1)}, u32[]{:S(2)}) copy-start(bf16[4,3072]{1,0:T(4,128)(2,1)} %refs_1_.1) | copy-start | bytes 73732
  3.7 0.7 %copy-start.4 = (bf16[4,3072]{1,0:T(4,128)(2,1)S(1)}, bf16[4,3072]{1,0:T(4,128)(2,1)}, u32[]{:S(2)}) copy-start(bf16[4,3072]{1,0:T(4,128)(2,1)} %refs_5_.1) | copy-start | bytes 73732
  4.5 0.7 %copy-start.5 = (bf16[2,3072]{1,0:T(2,128)(2,1)S(1)}, bf16[2,3072]{1,0:T(2,128)(2,1)}, u32[]{:S(2)}) copy-start(bf16[2,3072]{1,0:T(2,128)(2,1)} %refs_2_.1) | copy-start | bytes 36868
  5.2 0.7 %copy-start.6 = (bf16[1,3072]{1,0:T(2,128)(2,1)S(1)}, bf16[1,3072]{1,0:T(2,128)(2,1)}, u32[]{:S(2)}) copy-start(bf16[1,3072]{1,0:T(2,128)(2,1)} %refs_3_.1) | copy-start | bytes 18436
  5.9 0.7 %copy-start.7 = (bf16[2,3072]{1,0:T(2,128)(2,1)S(1)}, bf16[2,3072]{1,0:T(2,128)(2,1)}, u32[]{:S(2)}) copy-start(bf16[2,3072]{1,0:T(2,128)(2,1)} %refs_6_.1) | copy-start | bytes 36868
  6.6 0.7 %copy-start.8 = (bf16[1,3072]{1,0:T(2,128)(2,1)S(1)}, bf16[1,3072]{1,0:T(2,128)(2,1)}, u32[]{:S(2)}) copy-start(bf16[1,3072]{1,0:T(2,128)(2,1)} %refs_7_.1) | copy-start | bytes 18436
  7.3 0.7 %copy-start.9 = (bf16[4,1536]{1,0:T(4,128)(2,1)S(1)}, bf16[4,1536]{1,0:T(4,128)(2,1)}, u32[]{:S(2)}) copy-start(bf16[4,1536]{1,0:T(4,128)(2,1)} %refs_8_.1) | copy-start | bytes 36868
  8.0 0.7 %copy-start.10 = (bf16[4,1536]{1,0:T(4,128)(2,1)S(1)}, bf16[4,1536]{1,0:T(4,128)(2,1)}, u32[]{:S(2)}) copy-start(bf16[4,1536]{1,0:T(4,128)(2,1)} %refs_9_.1) | copy-start | bytes 36868
  8.7 0.7 %copy-start.11 = (bf16[2,1536]{1,0:T(2,128)(2,1)S(1)}, bf16[2,1536]{1,0:T(2,128)(2,1)}, u32[]{:S(2)}) copy-start(bf16[2,1536]{1,0:T(2,128)(2,1)} %refs_11_.1) | copy-start | bytes 18436
  9.4 0.7 %copy-start.12 = (bf16[2,768]{1,0:T(2,128)(2,1)S(1)}, bf16[2,768]{1,0:T(2,128)(2,1)}, u32[]{:S(2)}) copy-start(bf16[2,768]{1,0:T(2,128)(2,1)} %refs_10_.1) | copy-start | bytes 9220

commit v8 on v7

--- a/solution.py
+++ b/solution.py
@@ -668,7 +668,7 @@
         refs[4 + n][...] = refs[n][...]
 
 
-HBM = pl.BlockSpec(memory_space=pltpu.HBM)
+ANY = pl.BlockSpec(memory_space=pl.ANY)
 VMEM = pl.BlockSpec(memory_space=pltpu.VMEM)
 TILES = (2, 4, 4, 2, NZ, 16, 128)
 
@@ -688,8 +688,8 @@
     results = [jax.ShapeDtypeStruct(g.shape, BF) for g in maps[:4]]
     done = pl.pallas_call(
         exchange_kernel,
-        out_shape=results,
-        in_specs=[HBM] * 13,
+        out_shape=[pltpu.VMEM(g.shape, BF) for g in maps[:4]],
+        in_specs=[ANY] * 13,
         out_specs=[VMEM] * 4,
         scratch_shapes=[buffer(*m.shape) for m in maps] + [
             buffer(SHARD),
@@ -706,7 +706,7 @@
             sems(13), sems(3), sems(3), sems(10), sems(10), sems(38 * len(Z_PARTS)), sems(38 * len(Z_PARTS)), sems(2), sems(2),
         ],
         compiler_params=pltpu.CompilerParams(
-            collective_id=0, has_side_effects=True, vmem_limit_bytes=46 * 2**20
+            collective_id=0, has_side_effects=True, vmem_limit_bytes=60 * 2**20
         ),
         name="exchange",
     )(*operands)

time: 58.6 us -> 48.6 us (0.83)
  local copies, waits for them, and re-layouts: 9.42 us -> 0 us
    unnamed x26 -> x0, local copies, waits for them, and re-layouts: 9.42 us -> none
where the time goes in v8:
time: 48.6 us; the launch traced here: 48.4 us
  Pallas kernels  47.8 us (98%)
  between operations  0.64 us (1%)
    pallas_call x1, Pallas kernels, per_device(): pl.pallas_call(exchange_kernel, out_shape=[pltpu.VMEM(g.shape, BF) for g...  47.1 us

profile of v8, /device:TPU:1, one launch (start us, length us, event | category | flops | bytes accessed | tf_op | source)
XLA Modules:
  0.0 48.4 jit_solution(5758019467735931870)
XLA Ops:
  0.6 47.1 %exchange.1 = (bf16[8,3072]{1,0:T(8,128)(2,1)S(1)}, bf16[4,3072]{1,0:T(4,128)(2,1)S(1)}, bf16[2,3072]{1,0:T(2,128)(2,1)S(1)}, bf16[1,3072]{1,0:T(2,128)(2,1)S(1)}) custom-call(bf16[8,3072]{1,0:T(8,128)(2,1)} %refs_0_.1, bf16[4,3072]{1,0:T(4,128)(2,1)} %refs_1_.1, bf16[2,3072]{1,0:T(2,128)(2,1)} %refs_2_.1, bf16[1,3072]{1,0:T(2,128)(2,1)} %refs_3_.1, ...), custom_call_target="tpu_custom_call" | custom-call | tf_op jit(solution)/shard_map/exchange/pallas_call | solution.py:689
  47.8 0.6 %finish.1 = (bf16[8,3072]{1,0:T(8,128)(2,1)}, bf16[4,3072]{1,0:T(4,128)(2,1)}, bf16[2,3072]{1,0:T(2,128)(2,1)}, bf16[1,3072]{1,0:T(2,128)(2,1)}) custom-call(bf16[8,3072]{1,0:T(8,128)(2,1)S(1)} %get-tuple-element.8.refs_0_, bf16[4,3072]{1,0:T(4,128)(2,1)S(1)} %get-tuple-element.9.refs_1_, bf16[2,3072]{1,0:T(2,128)(2,1)S(1)} %get-tuple-element.10.refs_2_, ...), custom_call_target="tpu_custom_call" | custom-call | tf_op jit(solution)/shard_map/finish/pallas_call | solution.py:713

commit v9 on v8

--- a/solution.py
+++ b/solution.py
@@ -106,7 +106,7 @@
         (b, up1), (b, down1), (left, k), (right, k), (left, up1), (right, down1),
         (b, tile_of(z, y, 1 - c)), (wrap(b + 2, 4), k),
     ] + [(b, tile_of(z, wrap(y + d, 4), c)) for d in (1, 2, 3)]
-    along_z = [1, -1, 2, -2, 3, -3, 4, -4]
+    along_z = [4, -4, 3, -3, 2, -2, 1, -1]
     partners += [(b, tile_of(wrap(z + d, NZ), y, c)) for d in along_z]
     barrier = pltpu.get_barrier_semaphore()
     for who in partners:
@@ -573,11 +573,10 @@
             return self.send(tiles.at[1, b, u_of, c, zs], to_v, tile_of(z, to_u, c), b)
 
         def spread(self, u_of):
-            self.second.append((u_of, [(d, self.send_bundle(u_of, self.u, wrap(self.v + d, 4))) for d in (1, 3, 2)]))
+            self.second.append((u_of, [(d, self.send_bundle(u_of, self.u, wrap(self.v + d, 4))) for d in (2, 1, 3)]))
 
         def start(self):
-            self.first = [(d, self.send_bundle(self.u, wrap(self.u + d, 4), self.v)) for d in (1, 3, 2)]
-            self.spread(self.u)
+            self.first = [(d, self.send_bundle(self.u, wrap(self.u + d, 4), self.v)) for d in (2, 1, 3)]
 
         def pass_on(self):
             for d, copy in self.first:
@@ -616,6 +615,8 @@
     parts = [Part(s, lo, size, 19 * (2 * n + s)) for n, (lo, size) in enumerate(Z_PARTS) for s in range(2)]
     for part in parts[:2]:
         part.start()
+    for part in parts[:2]:
+        part.spread(part.u)
     own_maps()
     for (j, at), lanes in SPLITS.items():
         width = 256 if j == 192 else 128
@@ -640,6 +641,8 @@
         copy.wait_recv()
     for part in parts[2:]:
         part.start()
+    for part in parts[2:]:
+        part.spread(part.u)
     for part in parts[2:]:
         part.pass_on()
     for part in parts:

time: 48.6 us -> 48.4 us (level)
  no operation moved by 1% of the time
where the time goes in v9:
time: 48.4 us; the launch traced here: 48.2 us
  Pallas kernels  47.6 us (98%)
  between operations  0.64 us (1%)
    pallas_call x1, Pallas kernels, per_device(): pl.pallas_call(exchange_kernel, out_shape=[pltpu.VMEM(g.shape, BF) for g...  47 us

profile of v9, /device:TPU:1, one launch (start us, length us, event | category | flops | bytes accessed | tf_op | source)
XLA Modules:
  0.0 48.2 jit_solution(12634179833840509813)
XLA Ops:
  0.6 47.0 %exchange.1 = (bf16[8,3072]{1,0:T(8,128)(2,1)S(1)}, bf16[4,3072]{1,0:T(4,128)(2,1)S(1)}, bf16[2,3072]{1,0:T(2,128)(2,1)S(1)}, bf16[1,3072]{1,0:T(2,128)(2,1)S(1)}) custom-call(bf16[8,3072]{1,0:T(8,128)(2,1)} %refs_0_.1, bf16[4,3072]{1,0:T(4,128)(2,1)} %refs_1_.1, bf16[2,3072]{1,0:T(2,128)(2,1)} %refs_2_.1, bf16[1,3072]{1,0:T(2,128)(2,1)} %refs_3_.1, ...), custom_call_target="tpu_custom_call" | custom-call | tf_op jit(solution)/shard_map/exchange/pallas_call | solution.py:692
  47.6 0.6 %finish.1 = (bf16[8,3072]{1,0:T(8,128)(2,1)}, bf16[4,3072]{1,0:T(4,128)(2,1)}, bf16[2,3072]{1,0:T(2,128)(2,1)}, bf16[1,3072]{1,0:T(2,128)(2,1)}) custom-call(bf16[8,3072]{1,0:T(8,128)(2,1)S(1)} %get-tuple-element.8.refs_0_, bf16[4,3072]{1,0:T(4,128)(2,1)S(1)} %get-tuple-element.9.refs_1_, bf16[2,3072]{1,0:T(2,128)(2,1)S(1)} %get-tuple-element.10.refs_2_, ...), custom_call_target="tpu_custom_call" | custom-call | tf_op jit(solution)/shard_map/finish/pallas_call | solution.py:716
